TPU v7x, 512 devices: a whole 4x8x8 slice. The times are simulated.
512 devices in a mesh: seg: 32 (over z_lo, y), op: 16 (over x, z_hi, core).
Axes of the slice: x: 4, y: 8, z: 8 (z_hi: 2, z_lo: 4; z = z_hi * 4 + z_lo), core: 2. Of those that a mesh axis runs over, the one named last changes fastest.
Arguments:
- left_part: bfloat16 [32, 4, 256, 256], P('seg'), may hold values from -1 to 2
- right_part: bfloat16 [32, 4, 256, 256], P('seg'), may hold values from -1 to 2
- inverse_values: float32 [32, 4, 256], P('seg'), may hold values from 0.6 to 1.6
- left_env: bfloat16 [32, 48, 4, 256, 256], P('seg', 'op'), may hold values from -2 to 12
- right_env: bfloat16 [32, 48, 4, 256, 256], P('seg', 'op'), may hold values from -1 to 2
- source: int32 [48, 4], P('op'), may hold values from 0 to 3
- term_active: int32 [48], P('op'), may hold values from 0 to 1, as said below
- sketch: float32 [32, 256, 128], P('seg'), may hold values from -6 to 6
- kept: int32 [32, 4], P('seg'), may hold values from 32 to 128, as said below
Outputs:
- kept_state: bfloat16 [32, 4, 256, 256], P('seg')
- new_boundary: bfloat16 [32, 4, 128, 256], P('seg')
Inputs may be any that keep to these rules, and one draw needn't show every extreme that they name: `kept`: in every junction one sector keeps exactly 128. `term_active`: on each index of op the filled slots come first and at least one is filled; on some index all 3 are, and on another exactly one is.
All inputs are finite; a program needn't handle non-finite values.
Results may differ from a plain program's by a relative error of at most 0.0093.
Values may be sent and summed in bfloat16 or wider, within the bound.
No kernel may reach another device: no remote copies, remote signals or barrier semaphores. Data moves between devices by JAX's collectives and lax.ppermute only.
A program may use at most 64 MiB of HBM per device.

v0:
```python
import jax
import jax.numpy as jnp
from jax import lax
from jax.sharding import PartitionSpec as P


def from_behind(array, axis, by):
    size = lax.axis_size(axis)
    return lax.ppermute(array, axis, [(i, (i + by) % size) for i in range(size)])


def apply_terms(vector, left_env, right_env, source, active):
    total = jnp.zeros(vector.shape, jnp.float32)

    def keep_total(current):
        return current

    for slot_number in range(left_env.shape[0]):

        def add_term(current, slot_number=slot_number):
            chosen = jnp.take(vector, source[slot_number], axis=0)
            inner = jnp.einsum(
                "bij,bjk->bik", left_env[slot_number], chosen, preferred_element_type=jnp.float32
            ).astype(jnp.bfloat16)
            return current + jnp.einsum(
                "bij,bjk->bik", inner, right_env[slot_number], preferred_element_type=jnp.float32
            )

        total = lax.cond(active[slot_number] > 0, add_term, keep_total, total)
    return total


def solve_one(lower, correlation):
    return jax.scipy.linalg.cho_solve((lower, True), correlation)


def truncate(ground, sketch, kept):
    size = ground.shape[1]
    cols = sketch.shape[1]
    mask = (jnp.arange(cols, dtype=jnp.int32)[None, :] < kept[:, None]).astype(jnp.float32)
    basis = sketch[None] * mask[:, None, :]
    image = jnp.einsum("bij,bjk->bik", ground, basis, precision=lax.Precision.HIGHEST)
    gram = jnp.einsum("bik,bil->bkl", image, image, precision=lax.Precision.HIGHEST) / (size * size)
    gram = gram + jnp.eye(cols, dtype=jnp.float32)[None] * (1.0 - mask)[:, None, :]
    lower = jnp.linalg.cholesky(gram)
    correlation = jnp.einsum("bik,bij->bkj", image, ground, precision=lax.Precision.HIGHEST)
    right = jax.vmap(solve_one)(lower, correlation) / size
    state = jnp.einsum("bik,bkj->bij", image, right, precision=lax.Precision.HIGHEST) / size
    return (state.astype(jnp.bfloat16), right.astype(jnp.bfloat16))


def lowest_ritz(first_vec, second_vec, ray_first, ray_second, coupling):
    lowest = 0.5 * (ray_first + ray_second) - jnp.sqrt(
        0.25 * (ray_second - ray_first) ** 2 + coupling**2
    )
    weight = ray_second - lowest
    length = jnp.sqrt(weight**2 + coupling**2)
    return (weight * first_vec - coupling * second_vec) / length


def shards(
    left_part, right_part, inverse_values, left_env, right_env, source, term_active, sketch, kept
):
    neighbour = from_behind(right_part, "seg", -1)
    scaled = (left_part[0].astype(jnp.float32) * inverse_values[0][:, None, :]).astype(jnp.bfloat16)
    center = jnp.einsum("bij,bjk->bik", scaled, neighbour[0], preferred_element_type=jnp.float32)
    first_vec = center / jnp.sqrt(jnp.mean(center * center) + 1e-06)
    lenv = left_env[0]
    renv = right_env[0]

    def product(vector):
        return apply_terms(vector, lenv, renv, source, term_active)

    def summed(vector):
        return lax.psum(product(vector), "op")

    first_img = summed(first_vec.astype(jnp.bfloat16))
    ray_first = jnp.mean(first_vec * first_img)
    resid = first_img - ray_first * first_vec
    coupling = jnp.sqrt(jnp.mean(resid * resid) + 1e-06)
    second_vec = resid / coupling
    second_img = summed(second_vec.astype(jnp.bfloat16))
    ray_second = jnp.mean(second_vec * second_img)
    ground = lowest_ritz(first_vec, second_vec, ray_first, ray_second, coupling)
    kept_state, right_factor = truncate(ground, sketch[0], kept[0])
    handed = from_behind(right_factor, "seg", 1)
    return (kept_state[None], handed[None])


def solution(mesh):
    placed = (
        P("seg", None, None, None),
        P("seg", None, None, None),
        P("seg", None, None),
        P("seg", "op", None, None, None),
        P("seg", "op", None, None, None),
        P("op", None),
        P("op"),
        P("seg", None, None),
        P("seg", None),
    )
    return jax.shard_map(
        shards,
        mesh=mesh,
        in_specs=placed,
        out_specs=(P("seg", None, None, None), P("seg", None, None, None)),
        check_vma=False,
    )
```

profile of v0, /device:TPU:1, one launch (start us, length us, event | category | flops | bytes accessed | tf_op | source)
XLA Modules:
  0.0 543.2 jit_solution(2403797456041813647)
XLA Ops:
  7.2 0.0 all-reduce.3.cloned.1.call-start
  7.2 11.4 %collective-permute-start = (bf16[1,4,256,256]{3,2,1,0:T(8,128)(2,1)}, bf16[1,4,256,256]{3,2,1,0:T(8,128)(2,1)S(1)}, u32[]{:S(2)}, u32[]{:S(2)}) collective-permute-start(bf16[1,4,256,256]{3,2,1,0:T(8,128)(2,1)} %param.24), channel_id=1, source_target_pairs={{0,496},{16,0},{32,16},{48,32},{64,48},{80,64},{96,80},{112,96},{1... | collective-permute-start | bytes 1572872 | tf_op jit(solution)/shard_map/ppermute | solution.py:9
  18.6 1.4 fusion.109
  21.9 7.6 %collective-permute-done = bf16[1,4,256,256]{3,2,1,0:T(8,128)(2,1)S(1)} collective-permute-done((bf16[1,4,256,256]{3,2,1,0:T(8,128)(2,1)}, bf16[1,4,256,256]{3,2,1,0:T(8,128)(2,1)S(1)}, u32[]{:S(2)}, u32[]{:S(2)}) %collective-permute-start) | collective-permute-done | bytes 524320 | tf_op jit(solution)/shard_map/ppermute | solution.py:9
  29.5 0.0 copy-start.5
  29.5 2.1 multiply_reduce_fusion.3
  32.3 0.1 fusion.108
  32.3 0.0 copy-done.5
  32.4 2.4 conditional.6
  32.4 0.6 gather_fusion
  33.0 1.7 fusion
  34.8 0.0 copy-start.1
  34.8 1.0 copy-done.1
  35.8 0.0 all-reduce.3.cloned.1.call-update
  35.8 0.0 all-reduce.5.cloned.1.call-start
  35.8 190.7 %all-reduce.3.cloned.1.call-done = f32[4,256,256]{2,1,0:T(8,128)} async-done(((f32[4,256,256]{2,1,0:T(8,128)}), f32[4,256,256]{2,1,0:T(8,128)}) %all-reduce.3.cloned.1.call-update) | async-done | bytes 1048592 | tf_op jit(solution)/shard_map/psum | solution.py:75
  226.5 0.0 copy-start
  226.5 2.2 multiply_reduce_fusion.2
  229.4 0.0 copy-done
  229.4 0.9 multiply_reduce_fusion.1
  231.0 1.0 fusion.107
  231.9 4.3 conditional.9
  232.0 2.4 gather_fusion.3
  234.4 1.9 fusion.43
  236.3 0.0 copy-start.3
  236.3 0.2 conditional.11
  236.5 0.0 copy-start.2
  236.5 1.0 copy-done.2
  237.5 0.0 all-reduce.5.cloned.1.call-update
  237.6 0.1 copy.17
  237.7 0.0 copy-done.3
  237.7 0.1 fusion.105
  237.8 0.1 broadcast_subtract_fusion
  237.9 0.0 copy-start.4
  237.9 191.1 %all-reduce.5.cloned.1.call-done = f32[4,256,256]{2,1,0:T(8,128)} async-done(((f32[4,256,256]{2,1,0:T(8,128)}), f32[4,256,256]{2,1,0:T(8,128)}) %all-reduce.5.cloned.1.call-update) | async-done | bytes 1048592 | tf_op jit(solution)/shard_map/psum | solution.py:75
  429.0 2.1 multiply_reduce_fusion
  431.9 0.0 copy-done.4
  431.9 1.4 fusion.93
  433.2 1.0 multiply_add_fusion
  434.2 0.1 copy.18
  434.4 0.1 fusion.100
  434.5 46.9 %custom-call.11 = f32[4,128,128]{2,1,0:T(8,128)S(1)} custom-call(f32[4,128,128]{2,1,0:T(8,128)S(1)} %fusion.100), custom_call_target="Cholesky" | custom-call | tf_op jit(solution)/shard_map/jit(cholesky)/cholesky | solution.py:45
  481.5 0.1 compare_reduce_fusion
  481.6 0.1 select_bitcast_fusion
  481.7 39.3 %custom-call.12 = f32[4,1,128,128]{2,3,1,0:T(8,128)S(1)} custom-call(f32[4,1,128,128]{3,2,1,0:T(8,128)S(1)} %select_bitcast_fusion), custom_call_target="InvertDiagBlocksLowerTriangular" | custom-call | tf_op jit(solution)/shard_map/vmap(jit(_cho_solve))/triangular_solve | solution.py:34
  521.0 1.3 fusion.106
  522.3 0.6 fusion.97
  522.9 0.6 fusion.110
  523.5 3.1 collective-permute-start.1
  526.6 1.8 fusion.87
  528.4 7.3 %collective-permute-done.1 = bf16[4,128,256]{2,1,0:T(8,128)(2,1)S(1)} collective-permute-done((bf16[4,128,256]{2,1,0:T(8,128)(2,1)S(1)}, bf16[4,128,256]{2,1,0:T(8,128)(2,1)S(1)}, u32[]{:S(2)}, u32[]{:S(2)}) %collective-permute-start.1) | collective-permute-done | bytes 262176 | tf_op jit(solution)/shard_map/ppermute | solution.py:9
  535.7 0.7 copy.36
  (12 shorter events, 0.1 us)
Async XLA Ops:
  7.2 219.4 %all-reduce.3.cloned.1.call-start = ((), (), s32[]{:S(2)}) async-start(), calls=%async_computation | async-start | bytes 2097152 | tf_op jit(solution)/shard_map/psum | solution.py:75
  7.2 22.2 %collective-permute-start = (bf16[1,4,256,256]{3,2,1,0:T(8,128)(2,1)}, bf16[1,4,256,256]{3,2,1,0:T(8,128)(2,1)S(1)}, u32[]{:S(2)}, u32[]{:S(2)}) collective-permute-start(bf16[1,4,256,256]{3,2,1,0:T(8,128)(2,1)} %param.24), channel_id=1, source_target_pairs={{0,496},{16,0},{32,16},{48,32},{64,48},{80,64},{96,80},{112,96},{1... | collective-permute-start | bytes 1572872 | tf_op jit(solution)/shard_map/ppermute | solution.py:9
  29.5 2.9 copy-start.5
  34.8 1.0 copy-start.1
  35.8 393.2 %all-reduce.5.cloned.1.call-start = ((), (), s32[]{:S(2)}) async-start(), calls=%async_computation.1 | async-start | bytes 2097152 | tf_op jit(solution)/shard_map/psum | solution.py:75
  226.5 2.9 copy-start
  236.3 1.4 copy-start.3
  236.5 1.0 copy-start.2
  237.9 194.0 %copy-start.4 = (f32[1,256,128]{2,1,0:T(8,128)S(1)}, f32[1,256,128]{2,1,0:T(8,128)}, u32[]{:S(2)}) copy-start(f32[1,256,128]{2,1,0:T(8,128)} %param.30) | copy-start | bytes 393220
  523.5 12.2 %collective-permute-start.1 = (bf16[4,128,256]{2,1,0:T(8,128)(2,1)S(1)}, bf16[4,128,256]{2,1,0:T(8,128)(2,1)S(1)}, u32[]{:S(2)}, u32[]{:S(2)}) collective-permute-start(bf16[4,128,256]{2,1,0:T(8,128)(2,1)S(1)} %get-tuple-element.128), channel_id=1, source_target_pairs={{0,16},{16,32},{32,48},{48,64},{64,80},{80,96},{96,112},{112,128},... | collective-permute-start | bytes 786440 | tf_op jit(solution)/shard_map/ppermute | solution.py:9
Sparse Core Ops, SparseCore 0:
  35.9 190.5 all-reduce.2
  237.7 191.2 all-reduce.4
where the time goes:
time: 543 us
  waiting for transfers between devices  397 us (73%)
  other arithmetic  93.1 us (17%)
  between operations  19 us (3%)
  starting transfers between devices  14.5 us (3%)
  matrix products  12.4 us (2%)
  local copies, waits for them, and re-layouts  7.31 us (1%)
    psum x2, waiting for transfers between devices, summed(): return lax.psum(product(vector), 'op')  382 us
    another operation x4, other arithmetic, truncate(): lower = jnp.linalg.cholesky(gram)  47.1 us
    another operation x3, other arithmetic, solve_one(): return jax.scipy.linalg.cho_solve((lower, True), correlation)  39.4 us
    ppermute x2, waiting for transfers between devices, from_behind(): lax.ppermute(array, axis, [(i, (i + by) % size) for i in range(size)])  14.9 us
    ppermute x2, starting transfers between devices, from_behind(): lax.ppermute(array, axis, [(i, (i + by) % size) for i in range(size)])  14.4 us
  transfers between devices with their start and end apart: 4, of which 4 were waited for; matrix products, arithmetic and copies ran while one was open for 1% of the time, Pallas kernels for 0%

commit v1 on v0

--- a/solution.py
+++ b/solution.py
@@ -7,6 +7,10 @@
 def from_behind(array, axis, by):
     size = lax.axis_size(axis)
     return lax.ppermute(array, axis, [(i, (i + by) % size) for i in range(size)])
+
+
+def plane_groups():
+    return [[x * 4 + z * 2 + c for x in range(4) for c in range(2)] for z in range(2)]
 
 
 def apply_terms(vector, left_env, right_env, source, active):
@@ -58,6 +62,17 @@
     return (weight * first_vec - coupling * second_vec) / length
 
 
+def sum_over_op(part):
+    chunks = part.astype(jnp.bfloat16).reshape(8, 128, 256)
+    chunks = lax.all_to_all(chunks, "op", 0, 0, axis_index_groups=plane_groups(), tiled=True)
+    own = jnp.sum(chunks.astype(jnp.float32), axis=0).astype(jnp.bfloat16)
+    other = lax.ppermute(own, "op", [(i, i ^ 2) for i in range(16)])
+    both = (own.astype(jnp.float32) + other.astype(jnp.float32)).astype(jnp.bfloat16)
+    spread = jnp.broadcast_to(both[None], (8, 128, 256))
+    whole = lax.all_to_all(spread, "op", 0, 0, axis_index_groups=plane_groups(), tiled=True)
+    return whole.reshape(4, 256, 256).astype(jnp.float32)
+
+
 def shards(
     left_part, right_part, inverse_values, left_env, right_env, source, term_active, sketch, kept
 ):
@@ -71,17 +86,16 @@
     def product(vector):
         return apply_terms(vector, lenv, renv, source, term_active)
 
-    def summed(vector):
-        return lax.psum(product(vector), "op")
-
-    first_img = summed(first_vec.astype(jnp.bfloat16))
-    ray_first = jnp.mean(first_vec * first_img)
-    resid = first_img - ray_first * first_vec
+    first_part = product(first_vec.astype(jnp.bfloat16))
+    ray_part = jnp.mean(first_vec * first_part)
+    resid = sum_over_op(first_part - ray_part * first_vec)
     coupling = jnp.sqrt(jnp.mean(resid * resid) + 1e-06)
     second_vec = resid / coupling
-    second_img = summed(second_vec.astype(jnp.bfloat16))
-    ray_second = jnp.mean(second_vec * second_img)
-    ground = lowest_ritz(first_vec, second_vec, ray_first, ray_second, coupling)
+    second_part = product(second_vec.astype(jnp.bfloat16))
+    rays = jnp.stack([ray_part, jnp.mean(second_vec * second_part)])
+    rays = jnp.broadcast_to(jnp.pad(rays, (0, 126))[None], (16, 128))
+    rays = jnp.sum(lax.all_to_all(rays, "op", 0, 0, tiled=True), axis=0)
+    ground = lowest_ritz(first_vec, second_vec, rays[0], rays[1], coupling)
     kept_state, right_factor = truncate(ground, sketch[0], kept[0])
     handed = from_behind(right_factor, "seg", 1)
     return (kept_state[None], handed[None])

time: 543 us -> 224 us (0.41)
  waiting for transfers between devices: 397 us -> 47.4 us
  starting transfers between devices: 14.5 us -> 47.5 us
  between operations: 19 us -> 8.8 us
    psum x2 -> x0, waiting for transfers between devices: 382 us -> none  [summed(): return lax.psum(product(vector), 'op')]
    all_to_all x0 -> x3, waiting for transfers between devices: none -> 28 us  [the longest x1 9.49 us: sum_over_op(): lax.all_to_all(chunks, 'op', 0, 0, axis_index_groups=plane_groups(), tile...]
    all_to_all x0 -> x3, starting transfers between devices: none -> 25.4 us  [the longest x1 12.6 us: shards(): rays = jnp.sum(lax.all_to_all(rays, 'op', 0, 0, tiled=True), axis=0)]
    ppermute x0 -> x1, starting transfers between devices: none -> 8.82 us  [sum_over_op(): other = lax.ppermute(own, 'op', [(i, i ^ 2) for i in range(16)])]
  transfers between devices with their start and end apart: 4 -> 6, of which waited for: 4 -> 6; matrix products, arithmetic and copies ran while one was open for 1% -> 2% of each run, Pallas kernels for 0% -> 0%
where the time goes in v1:
time: 224 us; the launch traced here: 223 us
  other arithmetic  91.9 us (41%)
  starting transfers between devices  47.5 us (21%)
  waiting for transfers between devices  47.4 us (21%)
  matrix products  16.2 us (7%)
  local copies, waits for them, and re-layouts  11.1 us (5%)
  between operations  8.8 us (4%)
    another operation x4, other arithmetic, truncate(): lower = jnp.linalg.cholesky(gram)  47.1 us
    another operation x3, other arithmetic, solve_one(): return jax.scipy.linalg.cho_solve((lower, True), correlation)  39.4 us
    ppermute x2, waiting for transfers between devices, from_behind(): lax.ppermute(array, axis, [(i, (i + by) % size) for i in range(size)])  17.8 us
    ppermute x2, starting transfers between devices, from_behind(): lax.ppermute(array, axis, [(i, (i + by) % size) for i in range(size)])  13.3 us
    all_to_all x1, starting transfers between devices, shards(): rays = jnp.sum(lax.all_to_all(rays, 'op', 0, 0, tiled=True), axis=0)  12.6 us
    all_to_all x1, waiting for transfers between devices, sum_over_op(): lax.all_to_all(chunks, 'op', 0, 0, axis_index_groups=plane_groups(), tile...  9.49 us
    all_to_all x1, waiting for transfers between devices, sum_over_op(): lax.all_to_all(spread, 'op', 0, 0, axis_index_groups=plane_groups(), tile...  9.33 us
    all_to_all x1, waiting for transfers between devices, shards(): rays = jnp.sum(lax.all_to_all(rays, 'op', 0, 0, tiled=True), axis=0)  9.2 us
  transfers between devices with their start and end apart: 6, of which 6 were waited for; matrix products, arithmetic and copies ran while one was open for 2% of the time, Pallas kernels for 0%

profile of v1, /device:TPU:1, one launch (start us, length us, event | category | flops | bytes accessed | tf_op | source)
XLA Modules:
  0.0 223.0 jit_solution(6302018011442155837)
XLA Ops:
  0.6 11.4 %collective-permute-start = (bf16[1,4,256,256]{3,2,1,0:T(8,128)(2,1)}, bf16[1,4,256,256]{3,2,1,0:T(8,128)(2,1)S(1)}, u32[]{:S(2)}, u32[]{:S(2)}) collective-permute-start(bf16[1,4,256,256]{3,2,1,0:T(8,128)(2,1)} %param.24), channel_id=1, source_target_pairs={{0,496},{16,0},{32,16},{48,32},{64,48},{80,64},{96,80},{112,96},{1... | collective-permute-start | bytes 1572872 | tf_op jit(solution)/shard_map/ppermute | solution.py:9
  12.0 1.4 fusion.113
  15.3 7.5 %collective-permute-done = bf16[1,4,256,256]{3,2,1,0:T(8,128)(2,1)S(1)} collective-permute-done((bf16[1,4,256,256]{3,2,1,0:T(8,128)(2,1)}, bf16[1,4,256,256]{3,2,1,0:T(8,128)(2,1)S(1)}, u32[]{:S(2)}, u32[]{:S(2)}) %collective-permute-start) | collective-permute-done | bytes 524320 | tf_op jit(solution)/shard_map/ppermute | solution.py:9
  22.9 0.0 copy-start.2
  22.9 2.1 multiply_reduce_fusion.1
  25.7 0.1 fusion.111
  25.8 0.0 copy-done.2
  25.8 2.5 %conditional.6 = (f32[4,256,256]{2,1,0:T(8,128)S(1)}) conditional(s32[]{:T(128)} %bitcast.23, () %tuple.45, (s32[3,4]{1,0:T(4,128)S(1)}, bf16[4,256,256]{2,1,0:T(8,128)(2,1)S(1)}, bf16[3,4,256,256]{3,2,1,0:T(8,128)(2,1)}, bf16[3,4,256,256]{3,2,1,0:T(8,128)(2,1)}) %tuple.92), branch_computations={%region_1.0_spmd, %region_2.4_spmd} | conditional | flops 268960800 | bytes 3674192 | solution.py:33
  25.8 0.6 gather_fusion
  26.4 1.9 fusion
  28.3 2.6 %conditional.7 = (f32[4,256,256]{2,1,0:T(8,128)S(1)}) conditional(s32[]{:T(128)} %bitcast.22, f32[4,256,256]{2,1,0:T(8,128)S(1)} %get-tuple-element.136, (s32[3,4]{1,0:T(4,128)S(1)}, bf16[4,256,256]{2,1,0:T(8,128)(2,1)S(1)}, bf16[3,4,256,256]{3,2,1,0:T(8,128)(2,1)}, bf16[3,4,256,256]{3,2,1,0:T(8,128)(2,1)}, f32[4,256,256]{2,1,0:T(8,128)S(1)}) %tuple.93), branch_computations={%region_3.5_spmd, %region_4.6_spmd} | conditional | flops 269222944 | bytes 4722768 | solution.py:33
  28.3 0.6 gather_fusion.1
  28.9 2.0 convolution_add_fusion
  30.9 0.9 multiply_reduce_fusion
  32.4 1.0 subtract_convert_fusion
  33.4 0.0 copy-start.1
  33.4 7.7 %all-to-all-start = ((bf16[8,128,256]{2,1,0:T(8,128)(2,1)}), bf16[8,128,256]{2,1,0:T(8,128)(2,1)S(1)}, u32[]{:S(2)}, u32[]{:S(2)}) async-start(bf16[8,128,256]{2,1,0:T(8,128)(2,1)} %bitcast.27), calls=%async_computation | async-start | bytes 1048576 | tf_op jit(solution)/shard_map/all_to_all | solution.py:67
  41.1 9.5 %all-to-all-done = bf16[8,128,256]{2,1,0:T(8,128)(2,1)S(1)} async-done(((bf16[8,128,256]{2,1,0:T(8,128)(2,1)}), bf16[8,128,256]{2,1,0:T(8,128)(2,1)S(1)}, u32[]{:S(2)}, u32[]{:S(2)}) %all-to-all-start) | async-done | bytes 524320 | tf_op jit(solution)/shard_map/all_to_all | solution.py:67
  50.6 0.1 reduce_sum.59
  50.6 8.8 %collective-permute-start.1 = (bf16[128,256]{1,0:T(8,128)(2,1)S(1)}, bf16[128,256]{1,0:T(8,128)(2,1)S(1)}, u32[]{:S(2)}, u32[]{:S(2)}) collective-permute-start(bf16[128,256]{1,0:T(8,128)(2,1)S(1)} %reduce_sum.59), channel_id=1, source_target_pairs={{0,2},{1,3},{2,0},{3,1},{4,6},{5,7},{6,4},{7,5},{8,10},{9,11},{10,... | collective-permute-start | bytes 196616 | tf_op jit(solution)/shard_map/ppermute | solution.py:69
  59.5 1.6 collective-permute-done.1
  61.1 0.8 broadcast_in_dim.19
  62.0 5.1 %all-to-all-start.1 = ((bf16[8,128,256]{2,1,0:T(8,128)(2,1)}), bf16[8,128,256]{2,1,0:T(8,128)(2,1)S(1)}, u32[]{:S(2)}, u32[]{:S(2)}) async-start(bf16[8,128,256]{2,1,0:T(8,128)(2,1)} %broadcast_in_dim.19), calls=%async_computation.1 | async-start | bytes 1048576 | tf_op jit(solution)/shard_map/all_to_all | solution.py:72
  67.1 0.0 copy-done.1
  67.1 0.1 fusion.109
  67.2 0.1 broadcast_subtract_fusion
  67.3 9.3 %all-to-all-done.1 = bf16[8,128,256]{2,1,0:T(8,128)(2,1)S(1)} async-done(((bf16[8,128,256]{2,1,0:T(8,128)(2,1)}), bf16[8,128,256]{2,1,0:T(8,128)(2,1)S(1)}, u32[]{:S(2)}, u32[]{:S(2)}) %all-to-all-start.1) | async-done | bytes 524320 | tf_op jit(solution)/shard_map/all_to_all | solution.py:72
  76.6 0.9 fusion.88
  78.2 0.1 convert_divide_fusion
  78.3 0.8 bitcast_convert_fusion
  79.1 4.4 %conditional.9 = (f32[4,256,256]{2,1,0:T(8,128)S(1)}) conditional(s32[]{:T(128)} %bitcast.23, () %tuple.49, (s32[3,4]{1,0:T(4,128)S(1)}, bf16[4,256,256]{2,1,0:T(8,128)(2,1)}, bf16[3,4,256,256]{3,2,1,0:T(8,128)(2,1)}, bf16[3,4,256,256]{3,2,1,0:T(8,128)(2,1)}) %tuple.95), branch_computations={%region_10.12_spmd, %region_11.13_spmd} | conditional | flops 268960800 | bytes 3674192 | solution.py:33
  79.1 2.4 %gather_fusion.3 = bf16[4,256,256]{2,1,0:T(8,128)(2,1)} fusion(bf16[4,256,256]{2,1,0:T(8,128)(2,1)} %get-tuple-element.93, s32[1024]{0:T(1024)S(1)} %pad_clamp_fusion.3), kind=kCustom, calls=%fused_computation.3.clone | custom fusion | bytes 1048592 | tf_op jit(solution)/shard_map/cond/branch_1_fun/jit(_take)/gather | solution.py:25
  81.5 2.0 fusion.43
  83.6 4.6 %conditional.10 = (f32[4,256,256]{2,1,0:T(8,128)S(1)}) conditional(s32[]{:T(128)} %bitcast.22, f32[4,256,256]{2,1,0:T(8,128)S(1)} %get-tuple-element.139, (s32[3,4]{1,0:T(4,128)S(1)}, bf16[4,256,256]{2,1,0:T(8,128)(2,1)}, bf16[3,4,256,256]{3,2,1,0:T(8,128)(2,1)}, bf16[3,4,256,256]{3,2,1,0:T(8,128)(2,1)}, f32[4,256,256]{2,1,0:T(8,128)S(1)}) %tuple.96), branch_computations={%region_12.14_spmd, %region_13.15_spmd} | conditional | flops 269222944 | bytes 4722768 | solution.py:33
  83.6 2.4 %gather_fusion.4 = bf16[4,256,256]{2,1,0:T(8,128)(2,1)} fusion(bf16[4,256,256]{2,1,0:T(8,128)(2,1)} %get-tuple-element.98, s32[1024]{0:T(1024)S(1)} %pad_clamp_fusion.4), kind=kCustom, calls=%fused_computation.4.clone | custom fusion | bytes 1048592 | tf_op jit(solution)/shard_map/cond/branch_1_fun/jit(_take)/gather | solution.py:25
  86.0 2.1 convolution_add_fusion.2
  88.2 0.9 fusion.90
  89.7 0.1 fusion.110
  89.8 0.6 broadcast_in_dim.22
  90.4 12.6 %all-to-all-start.2 = ((f32[16,1,128]{2,1,0:T(1,128)}), f32[16,1,128]{2,1,0:T(1,128)S(1)}, u32[]{:S(2)}, u32[]{:S(2)}) async-start(f32[16,1,128]{2,1,0:T(1,128)} %broadcast_in_dim.22), calls=%async_computation.2 | async-start | bytes 16384 | tf_op jit(solution)/shard_map/all_to_all | solution.py:97
  103.1 0.1 copy.34
  103.2 9.2 %all-to-all-done.2 = f32[16,1,128]{2,1,0:T(1,128)S(1)} async-done(((f32[16,1,128]{2,1,0:T(1,128)}), f32[16,1,128]{2,1,0:T(1,128)S(1)}, u32[]{:S(2)}, u32[]{:S(2)}) %all-to-all-start.2) | async-done | bytes 8224 | tf_op jit(solution)/shard_map/all_to_all | solution.py:97
  112.4 0.6 fusion.112
  116.3 0.0 copy-start
  116.3 0.2 fusion.92
  116.5 0.7 copy-done
  117.2 1.1 fusion.97
  118.3 1.1 fusion.115
  119.3 1.0 multiply_add_fusion
  120.4 0.1 copy.35
  120.5 0.1 fusion.104
  120.6 46.9 %custom-call.11 = f32[4,128,128]{2,1,0:T(8,128)S(1)} custom-call(f32[4,128,128]{2,1,0:T(8,128)S(1)} %fusion.104), custom_call_target="Cholesky" | custom-call | tf_op jit(solution)/shard_map/jit(cholesky)/cholesky | solution.py:49
  167.6 0.1 compare_reduce_fusion
  167.7 0.1 select_bitcast_fusion
  167.8 39.3 %custom-call.12 = f32[4,1,128,128]{2,3,1,0:T(8,128)S(1)} custom-call(f32[4,1,128,128]{3,2,1,0:T(8,128)S(1)} %select_bitcast_fusion), custom_call_target="InvertDiagBlocksLowerTriangular" | custom-call | tf_op jit(solution)/shard_map/vmap(jit(_cho_solve))/triangular_solve | solution.py:38
  207.1 0.6 fusion.101
  207.8 0.6 fusion.114
  208.4 1.9 collective-permute-start.2
  210.3 1.8 fusion.87
  212.1 10.2 %collective-permute-done.2 = bf16[4,128,256]{2,1,0:T(8,128)(2,1)S(1)} collective-permute-done((bf16[4,128,256]{2,1,0:T(8,128)(2,1)S(1)}, bf16[4,128,256]{2,1,0:T(8,128)(2,1)S(1)}, u32[]{:S(2)}, u32[]{:S(2)}) %collective-permute-start.2) | collective-permute-done | bytes 262176 | tf_op jit(solution)/shard_map/ppermute | solution.py:9
  222.3 0.7 copy.67
  (17 shorter events, 0.2 us)
Async XLA Ops:
  0.6 22.2 %collective-permute-start = (bf16[1,4,256,256]{3,2,1,0:T(8,128)(2,1)}, bf16[1,4,256,256]{3,2,1,0:T(8,128)(2,1)S(1)}, u32[]{:S(2)}, u32[]{:S(2)}) collective-permute-start(bf16[1,4,256,256]{3,2,1,0:T(8,128)(2,1)} %param.24), channel_id=1, source_target_pairs={{0,496},{16,0},{32,16},{48,32},{64,48},{80,64},{96,80},{112,96},{1... | collective-permute-start | bytes 1572872 | tf_op jit(solution)/shard_map/ppermute | solution.py:9
  22.9 2.9 %copy-start.2 = (s32[3,4]{1,0:T(4,128)S(1)}, s32[3,4]{1,0:T(4,128)}, u32[]{:S(2)}) copy-start(s32[3,4]{1,0:T(4,128)} %param.28) | copy-start | bytes 148
  33.4 33.7 %copy-start.1 = (s32[1,4]{1,0:T(1,128)S(1)}, s32[1,4]{1,0:T(1,128)}, u32[]{:S(2)}) copy-start(s32[1,4]{1,0:T(1,128)} %param.31) | copy-start | bytes 52
  33.4 17.2 %all-to-all-start = ((bf16[8,128,256]{2,1,0:T(8,128)(2,1)}), bf16[8,128,256]{2,1,0:T(8,128)(2,1)S(1)}, u32[]{:S(2)}, u32[]{:S(2)}) async-start(bf16[8,128,256]{2,1,0:T(8,128)(2,1)} %bitcast.27), calls=%async_computation | async-start | bytes 1048576 | tf_op jit(solution)/shard_map/all_to_all | solution.py:67
  50.6 10.5 %collective-permute-start.1 = (bf16[128,256]{1,0:T(8,128)(2,1)S(1)}, bf16[128,256]{1,0:T(8,128)(2,1)S(1)}, u32[]{:S(2)}, u32[]{:S(2)}) collective-permute-start(bf16[128,256]{1,0:T(8,128)(2,1)S(1)} %reduce_sum.59), channel_id=1, source_target_pairs={{0,2},{1,3},{2,0},{3,1},{4,6},{5,7},{6,4},{7,5},{8,10},{9,11},{10,... | collective-permute-start | bytes 196616 | tf_op jit(solution)/shard_map/ppermute | solution.py:69
  62.0 14.6 %all-to-all-start.1 = ((bf16[8,128,256]{2,1,0:T(8,128)(2,1)}), bf16[8,128,256]{2,1,0:T(8,128)(2,1)S(1)}, u32[]{:S(2)}, u32[]{:S(2)}) async-start(bf16[8,128,256]{2,1,0:T(8,128)(2,1)} %broadcast_in_dim.19), calls=%async_computation.1 | async-start | bytes 1048576 | tf_op jit(solution)/shard_map/all_to_all | solution.py:72
  90.4 22.0 %all-to-all-start.2 = ((f32[16,1,128]{2,1,0:T(1,128)}), f32[16,1,128]{2,1,0:T(1,128)S(1)}, u32[]{:S(2)}, u32[]{:S(2)}) async-start(f32[16,1,128]{2,1,0:T(1,128)} %broadcast_in_dim.22), calls=%async_computation.2 | async-start | bytes 16384 | tf_op jit(solution)/shard_map/all_to_all | solution.py:97
  116.3 0.9 copy-start
  208.4 14.0 %collective-permute-start.2 = (bf16[4,128,256]{2,1,0:T(8,128)(2,1)S(1)}, bf16[4,128,256]{2,1,0:T(8,128)(2,1)S(1)}, u32[]{:S(2)}, u32[]{:S(2)}) collective-permute-start(bf16[4,128,256]{2,1,0:T(8,128)(2,1)S(1)} %get-tuple-element.130), channel_id=1, source_target_pairs={{0,16},{16,32},{32,48},{48,64},{64,80},{80,96},{96,112},{112,128},... | collective-permute-start | bytes 786440 | tf_op jit(solution)/shard_map/ppermute | solution.py:9

commit v2 on v1

v2 whole, which is shorter than its diff:
```python
import jax
import jax.numpy as jnp
from jax import lax
from jax.experimental import pallas as pl
from jax.experimental.pallas import tpu as pltpu
from jax.sharding import PartitionSpec as P

bf16, f32 = jnp.bfloat16, jnp.float32


def env_copies(lenv_hbm, renv_hbm, lenv, renv, sems):
    copies = []
    for slot in range(lenv_hbm.shape[0]):
        copies.append(pltpu.make_async_copy(lenv_hbm.at[slot], lenv.at[slot], sems.at[slot, 0]))
        copies.append(
            pltpu.make_async_copy(
                renv_hbm.at[slot], renv.at[:, pl.ds(slot * 256, 256), :], sems.at[slot, 1]
            )
        )
    return copies


def own_terms(source, active, vector, lenv, renv, inner, copies, image):
    slots, sectors = lenv.shape[0], lenv.shape[1]
    for slot in range(slots):
        copies[2 * slot].wait()
        flag = active[slot].astype(f32)
        for b in range(sectors):
            product = jnp.dot(
                lenv[slot, b], vector[source[slot, b]], preferred_element_type=f32
            )
            inner[b, :, slot * 256 : (slot + 1) * 256] = (product * flag).astype(bf16)
    for slot in range(slots):
        copies[2 * slot + 1].wait()
    for b in range(sectors):
        image[b] = jnp.dot(inner[b], renv[b], preferred_element_type=f32)


def first_kernel(
    source, active, left_part, inverse, neighbour, lenv_hbm, renv_hbm,
    first, part, ray, lenv, renv, inner, vector, image, sems,
):
    copies = env_copies(lenv_hbm, renv_hbm, lenv, renv, sems)
    for copy in copies:
        copy.start()
    sectors = left_part.shape[0]
    count = sectors * 256 * 256
    squares = jnp.zeros((1, 256), f32)
    for b in range(sectors):
        scaled = (left_part[b].astype(f32) * inverse[b : b + 1, :]).astype(bf16)
        center = jnp.dot(scaled, neighbour[b], preferred_element_type=f32)
        first[b] = center
        squares += jnp.sum(center * center, axis=0, keepdims=True)
    scale = lax.rsqrt(jnp.sum(squares, axis=1, keepdims=True) / count + 1e-06)
    for b in range(sectors):
        scaled_center = first[b] * scale
        first[b] = scaled_center
        vector[b] = scaled_center.astype(bf16)
    own_terms(source, active, vector, lenv, renv, inner, copies, image)
    dots = jnp.zeros((1, 256), f32)
    for b in range(sectors):
        dots += jnp.sum(first[b] * image[b], axis=0, keepdims=True)
    own_ray = jnp.sum(dots, axis=1, keepdims=True) / count
    for b in range(sectors):
        part[b] = (image[b] - own_ray * first[b]).astype(bf16)
    ray[...] = jnp.broadcast_to(own_ray, ray.shape)


def second_kernel(
    source, active, resid, first_ray, lenv_hbm, renv_hbm,
    rays, coupling, lenv, renv, inner, vector, image, sems,
):
    copies = env_copies(lenv_hbm, renv_hbm, lenv, renv, sems)
    for copy in copies:
        copy.start()
    sectors = resid.shape[0]
    count = sectors * 256 * 256
    squares = jnp.zeros((1, 256), f32)
    for b in range(sectors):
        piece = resid[b].astype(f32)
        squares += jnp.sum(piece * piece, axis=0, keepdims=True)
    mean_square = jnp.sum(squares, axis=1, keepdims=True) / count + 1e-06
    scale = lax.rsqrt(mean_square)
    for b in range(sectors):
        vector[b] = (resid[b].astype(f32) * scale).astype(bf16)
    own_terms(source, active, vector, lenv, renv, inner, copies, image)
    dots = jnp.zeros((1, 256), f32)
    for b in range(sectors):
        dots += jnp.sum(resid[b].astype(f32) * image[b], axis=0, keepdims=True)
    own_ray = jnp.sum(dots, axis=1, keepdims=True) * scale / count
    lane = lax.broadcasted_iota(jnp.int32, rays.shape, 1)
    rays[...] = jnp.where(lane == 0, first_ray[0:1, :], jnp.broadcast_to(own_ray, rays.shape))
    coupling[...] = jnp.broadcast_to(jnp.sqrt(mean_square), coupling.shape)


SMEM = pl.BlockSpec(memory_space=pltpu.SMEM)
VMEM = pl.BlockSpec(memory_space=pltpu.VMEM)
ANY = pl.BlockSpec(memory_space=pl.ANY)


def env_scratch(slots, sectors):
    return [
        pltpu.VMEM((slots, sectors, 256, 256), bf16),
        pltpu.VMEM((sectors, slots * 256, 256), bf16),
        pltpu.VMEM((sectors, 256, slots * 256), bf16),
        pltpu.VMEM((sectors, 256, 256), bf16),
        pltpu.VMEM((sectors, 256, 256), f32),
        pltpu.SemaphoreType.DMA((slots, 2)),
    ]


def first_step(source, active, left_part, inverse, neighbour, lenv, renv):
    slots, sectors = lenv.shape[:2]
    return pl.pallas_call(
        first_kernel,
        out_shape=(
            jax.ShapeDtypeStruct((sectors, 256, 256), f32),
            jax.ShapeDtypeStruct((sectors, 256, 256), bf16),
            jax.ShapeDtypeStruct((8, 128), f32),
        ),
        in_specs=[SMEM, SMEM, VMEM, VMEM, VMEM, ANY, ANY],
        out_specs=(VMEM, VMEM, VMEM),
        scratch_shapes=env_scratch(slots, sectors),
        compiler_params=pltpu.CompilerParams(vmem_limit_bytes=24 * 2**20),
        cost_estimate=pl.CostEstimate(flops=940_000_000, bytes_accessed=6_000_000, transcendentals=0),
    )(source, active, left_part, inverse, neighbour, lenv, renv)


def second_step(source, active, resid, first_ray, lenv, renv):
    slots, sectors = lenv.shape[:2]
    return pl.pallas_call(
        second_kernel,
        out_shape=(
            jax.ShapeDtypeStruct((16, 128), f32),
            jax.ShapeDtypeStruct((8, 128), f32),
        ),
        in_specs=[SMEM, SMEM, VMEM, VMEM, ANY, ANY],
        out_specs=(VMEM, VMEM),
        scratch_shapes=env_scratch(slots, sectors),
        compiler_params=pltpu.CompilerParams(vmem_limit_bytes=24 * 2**20),
        cost_estimate=pl.CostEstimate(flops=800_000_000, bytes_accessed=4_000_000, transcendentals=0),
    )(source, active, resid, first_ray, lenv, renv)


HIGHEST = lax.Precision.HIGHEST
NN = (((1,), (0,)), ((), ()))
NT = (((1,), (1,)), ((), ()))
TN = (((0,), (0,)), ((), ()))


def exact_dot(left, right, dims=NN):
    return lax.dot_general(left, right, dims, precision=HIGHEST, preferred_element_type=f32)


def split(array):
    high = array.astype(bf16)
    return high, (array - high.astype(f32)).astype(bf16)


def fine_dot(left, right, dims=NN):
    def dot(a, b):
        return lax.dot_general(a, b, dims, preferred_element_type=f32)
    return dot(left[0], right[0]) + (dot(left[0], right[1]) + dot(left[1], right[0]))


def invert_blocks(packed):
    size = packed.shape[0]
    row = lax.broadcasted_iota(jnp.int32, packed.shape, 0)
    lane = lax.broadcasted_iota(jnp.int32, packed.shape, 1)
    place = lane % size
    start = lane - place

    def column(array, k):
        return jnp.take_along_axis(array, start + k, axis=1)

    here = column(packed, 0)
    for k in range(size):
        ahead = column(packed, k + 1) if k + 1 < size else None
        inverse = 1.0 / here[k : k + 1, :]
        pivot_row = jnp.where(place[k : k + 1, :] == k, 1.0, packed[k : k + 1, :]) * inverse
        packed = jnp.where(place == k, 0.0, packed) - here * pivot_row
        packed = jnp.where(row == k, pivot_row, packed)
        if ahead is not None:
            factor = here[k + 1 : k + 2, :] * inverse
            here = jnp.where(row == k, factor, ahead - here * factor)
    return packed


def invert(gram):
    sectors, cols, size = len(gram), gram[0].shape[0], 32
    row = lax.broadcasted_iota(jnp.int32, (cols, cols), 0)
    lane = lax.broadcasted_iota(jnp.int32, (cols, cols), 1)
    same = (row // size) == (lane // size)
    unit = jnp.where(row % size == lane % size, 1.0, 0.0).astype(f32)
    block_lane = lax.broadcasted_iota(jnp.int32, (size, cols), 1) // size
    for p in range(cols // size):
        rows = slice(p * size, (p + 1) * size)
        packed = jnp.zeros((size, cols), f32)
        for s in range(sectors):
            turned = pltpu.roll(gram[s][rows], ((s - p) * size) % cols, 1) if s != p else gram[s][rows]
            packed = jnp.where(block_lane == s, turned, packed)
        inverse = invert_blocks(packed)
        inverse = jnp.where(same, jnp.concatenate([inverse] * sectors, axis=0), 0.0)
        stacked = jnp.concatenate([g[rows] for g in gram], axis=0)
        stacked = jnp.where(lane // size == p, unit, stacked)
        panel = exact_dot(inverse, stacked)
        for s in range(sectors):
            own = panel[s * size : (s + 1) * size]
            tiled = jnp.concatenate([own] * (cols // size), axis=0)
            factor = jnp.where((lane // size == p) & (row // size != p), gram[s], 0.0)
            rest = jnp.where(lane // size == p, 0.0, gram[s])
            rest = jnp.where(row // size == p, tiled, rest)
            gram[s] = rest - exact_dot(factor, tiled)
    return gram


def truncate_kernel(kept, rays, coupling, first, resid, sketch, right, right_low, image):
    sectors, size = first.shape[:2]
    cols = sketch.shape[0]
    sums = jnp.sum(rays[...], axis=0, keepdims=True)
    ray_first, ray_second = sums[:, 0:1], sums[:, 1:2]
    between = coupling[0:1, 0:1]
    half = 0.5 * (ray_second - ray_first)
    weight = half + jnp.sqrt(half * half + between * between)
    length = lax.rsqrt(weight * weight + between * between)
    of_first, of_resid = weight * length, length
    tests = split(sketch[...])
    row = lax.broadcasted_iota(jnp.int32, (cols, cols), 0)
    lane = lax.broadcasted_iota(jnp.int32, (cols, cols), 1)
    gram, correlation = [], []
    for b in range(sectors):
        ground = split(of_first * first[b] - of_resid * resid[b].astype(f32))
        wide = lax.broadcasted_iota(jnp.int32, (cols, size), 0) < kept[0, b]
        own = jnp.where(wide, fine_dot(tests, ground, NT), 0.0)
        image[b] = own
        own = split(own)
        empty = jnp.where((row == lane) & (row >= kept[0, b]), 1.0, 0.0)
        gram.append(fine_dot(own, own, NT) * (1.0 / (size * size)) + empty)
        correlation.append(fine_dot(own, ground))
    gram = invert(gram)
    for b in range(sectors):
        own = exact_dot(gram[b], correlation[b]) * (1.0 / size)
        right[b] = own
        right_low[b] = own.astype(bf16)


def truncate_step(kept, rays, coupling, first, resid, sketch):
    sectors, size = first.shape[:2]
    cols = sketch.shape[0]
    return pl.pallas_call(
        truncate_kernel,
        out_shape=(
            jax.ShapeDtypeStruct((sectors, cols, size), f32),
            jax.ShapeDtypeStruct((sectors, cols, size), bf16),
            jax.ShapeDtypeStruct((sectors, cols, size), f32),
        ),
        in_specs=[SMEM] + [VMEM] * 5,
        out_specs=(VMEM, VMEM, VMEM),
        compiler_params=pltpu.CompilerParams(vmem_limit_bytes=24 * 2**20),
        cost_estimate=pl.CostEstimate(flops=900_000_000, bytes_accessed=4_000_000, transcendentals=0),
    )(kept, rays, coupling, first, resid, sketch)


def from_behind(array, axis, by):
    size = lax.axis_size(axis)
    return lax.ppermute(array, axis, [(i, (i + by) % size) for i in range(size)])


def plane_groups():
    return [[x * 4 + z * 2 + c for x in range(4) for c in range(2)] for z in range(2)]


def sum_over_op(part):
    chunks = part.reshape(8, 128, 256)
    chunks = lax.all_to_all(chunks, "op", 0, 0, axis_index_groups=plane_groups(), tiled=True)
    own = jnp.sum(chunks.astype(f32), axis=0).astype(bf16)
    other = lax.ppermute(own, "op", [(i, i ^ 2) for i in range(16)])
    both = (own.astype(f32) + other.astype(f32)).astype(bf16)
    spread = jnp.broadcast_to(both[None], (8, 128, 256))
    whole = lax.all_to_all(spread, "op", 0, 0, axis_index_groups=plane_groups(), tiled=True)
    return whole.reshape(4, 256, 256)


def shards(
    left_part, right_part, inverse_values, left_env, right_env, source, term_active, sketch, kept
):
    neighbour = from_behind(right_part, "seg", -1)
    lenv, renv = left_env[0], right_env[0]
    tests = sketch[0].T
    first, part, ray = first_step(
        source, term_active, left_part[0], inverse_values[0], neighbour[0], lenv, renv
    )
    resid = sum_over_op(part)
    rays, coupling = second_step(source, term_active, resid, ray, lenv, renv)
    rays = lax.all_to_all(rays, "op", 0, 0, tiled=True)
    right, right_low, image = truncate_step(kept, rays, coupling, first, resid, tests)
    handed = from_behind(right_low, "seg", 1)
    kept_state = jnp.einsum("bki,bkj->bij", image, right, precision=HIGHEST) / 256
    return (kept_state.astype(bf16)[None], handed[None])


def solution(mesh):
    placed = (
        P("seg", None, None, None),
        P("seg", None, None, None),
        P("seg", None, None),
        P("seg", "op", None, None, None),
        P("seg", "op", None, None, None),
        P("op", None),
        P("op"),
        P("seg", None, None),
        P("seg", None),
    )
    return jax.shard_map(
        shards,
        mesh=mesh,
        in_specs=placed,
        out_specs=(P("seg", None, None, None), P("seg", None, None, None)),
        check_vma=False,
    )
```

time: 224 us -> 122 us (0.54)
  other arithmetic: 91.9 us -> 1.13 us
  blocking collectives: 0 us -> 29 us
  starting transfers between devices: 47.5 us -> 30.1 us
  Pallas kernels: 0 us -> 16.8 us
  waiting for transfers between devices: 47.4 us -> 31.9 us
  matrix products: 16.2 us -> 1.83 us
  between operations: 8.8 us -> 0.77 us
    another operation x8 -> x0, other arithmetic: 86.6 us -> none  [the longest x4 47.1 us: truncate(): lower = jnp.linalg.cholesky(gram)]
    all_to_all x0 -> x2, blocking collectives: none -> 29 us  [the longest x1 15.4 us: sum_over_op(): lax.all_to_all(chunks, 'op', 0, 0, axis_index_groups=plane_groups(), tile...]
    all_to_all x3 -> x1, waiting for transfers between devices: 28 us -> 9.21 us  [shards(): rays = lax.all_to_all(rays, 'op', 0, 0, tiled=True)]
    pallas_call x0 -> x3, Pallas kernels: none -> 16.8 us  [the longest x1 10.5 us: truncate_step(): pl.pallas_call(truncate_kernel, out_shape=(jax.ShapeDtypeStruct((sectors,...]
    all_to_all x3 -> x1, starting transfers between devices: 25.4 us -> 8.86 us  [shards(): rays = lax.all_to_all(rays, 'op', 0, 0, tiled=True)]
    dot_general x9 -> x1, matrix products: 15 us -> 1.83 us  [shards(): jnp.einsum('bki,bkj->bij', image, right, precision=HIGHEST) / 256]
    unnamed x7 -> x34, local copies, waits for them, and re-layouts: 1.42 us -> 9.95 us
    gather x4 -> x0, local copies, waits for them, and re-layouts: 5.98 us -> none  [add_term(): chosen = jnp.take(vector, source[slot_number], axis=0)]
  transfers between devices with their start and end apart: 6 -> 4, of which waited for: 6 -> 4; matrix products, arithmetic and copies ran while one was open for 2% -> 2% of each run, Pallas kernels for 0% -> 0%
where the time goes in v2:
time: 122 us
  waiting for transfers between devices  31.9 us (26%)
  starting transfers between devices  30.1 us (25%)
  blocking collectives  29 us (24%)
  Pallas kernels  16.8 us (14%)
  local copies, waits for them, and re-layouts  9.99 us (8%)
  matrix products  1.83 us (2%)
    ppermute x2, waiting for transfers between devices, from_behind(): lax.ppermute(array, axis, [(i, (i + by) % size) for i in range(size)])  21.1 us
    all_to_all x1, blocking collectives, sum_over_op(): lax.all_to_all(chunks, 'op', 0, 0, axis_index_groups=plane_groups(), tile...  15.4 us
    all_to_all x1, blocking collectives, sum_over_op(): lax.all_to_all(spread, 'op', 0, 0, axis_index_groups=plane_groups(), tile...  13.7 us
    ppermute x2, starting transfers between devices, from_behind(): lax.ppermute(array, axis, [(i, (i + by) % size) for i in range(size)])  13.3 us
    pallas_call x1, Pallas kernels, truncate_step(): pl.pallas_call(truncate_kernel, out_shape=(jax.ShapeDtypeStruct((sectors,...  10.5 us
    unnamed x34, local copies, waits for them, and re-layouts  9.95 us
    all_to_all x1, waiting for transfers between devices, shards(): rays = lax.all_to_all(rays, 'op', 0, 0, tiled=True)  9.21 us
    all_to_all x1, starting transfers between devices, shards(): rays = lax.all_to_all(rays, 'op', 0, 0, tiled=True)  8.86 us
  transfers between devices with their start and end apart: 4, of which 4 were waited for; matrix products, arithmetic and copies ran while one was open for 2% of the time, Pallas kernels for 0%

profile of v2, /device:TPU:1, one launch (start us, length us, event | category | flops | bytes accessed | tf_op | source)
XLA Modules:
  0.0 121.6 jit_solution(12975487527259078044)
XLA Ops:
  0.6 11.4 %collective-permute-start = (bf16[1,4,256,256]{3,2,1,0:T(8,128)(2,1)}, bf16[1,4,256,256]{3,2,1,0:T(8,128)(2,1)S(1)}, u32[]{:S(2)}, u32[]{:S(2)}) collective-permute-start(bf16[1,4,256,256]{3,2,1,0:T(8,128)(2,1)} %param.10), channel_id=1, source_target_pairs={{0,496},{16,0},{32,16},{48,32},{64,48},{80,64},{96,80},{112,96},{1... | collective-permute-start | bytes 1572872 | tf_op jit(solution)/shard_map/ppermute | solution.py:266
  12.0 10.9 %collective-permute-done = bf16[1,4,256,256]{3,2,1,0:T(8,128)(2,1)S(1)} collective-permute-done((bf16[1,4,256,256]{3,2,1,0:T(8,128)(2,1)}, bf16[1,4,256,256]{3,2,1,0:T(8,128)(2,1)S(1)}, u32[]{:S(2)}, u32[]{:S(2)}) %collective-permute-start) | collective-permute-done | bytes 524320 | tf_op jit(solution)/shard_map/ppermute | solution.py:266
  22.9 0.0 copy-start
  22.9 1.4 %copy-done = bf16[1,3,4,256,256]{4,3,2,1,0:T(8,128)(2,1)S(1)} copy-done((bf16[1,3,4,256,256]{4,3,2,1,0:T(8,128)(2,1)S(1)}, bf16[1,3,4,256,256]{4,3,2,1,0:T(8,128)(2,1)}, u32[]{:S(2)}) %copy-start) | copy-done | bytes 1572888
  24.3 0.0 copy-start.2
  24.3 1.4 %copy-done.2 = bf16[1,3,4,256,256]{4,3,2,1,0:T(8,128)(2,1)S(1)} copy-done((bf16[1,3,4,256,256]{4,3,2,1,0:T(8,128)(2,1)S(1)}, bf16[1,3,4,256,256]{4,3,2,1,0:T(8,128)(2,1)}, u32[]{:S(2)}) %copy-start.2) | copy-done | bytes 1572888
  25.7 0.0 copy-start.6
  25.7 1.0 copy-done.6
  26.7 0.0 copy-start.7
  26.7 0.7 copy-done.7
  27.4 0.0 copy-start.9
  27.4 0.7 copy-done.9
  28.1 0.0 copy-start.10
  28.1 0.7 copy-done.10
  28.8 3.1 %shard_map.104 = (f32[4,256,256]{2,1,0:T(8,128)S(1)}, bf16[4,256,256]{2,1,0:T(8,128)(2,1)S(1)}, f32[8,128]{1,0:T(8,128)S(1)}) custom-call(s32[3,4]{1,0:T(4,128)S(1)} %copy-done.7, s32[3]{0:T(128)S(1)} %copy-done.10, bf16[4,256,256]{2,1,0:T(8,128)(2,1)S(1)} %bitcast.25, f32[4,256]{1,0:T(4,128)S(1)} %bitcast.30, bf16[4,256,256]{2,1,0:T(8,128)(2,1)S(1)} %bitcast.26, ...), custom_call_target="tpu_custom_call" | custom-call | flops 940000000 | bytes 6000000 | tf_op jit(solution)/shard_map/pallas_call | solution.py:114
  31.9 0.0 copy-start.12
  31.9 1.0 copy-done.12
  32.9 0.0 copy-start.1
  32.9 0.0 copy-start.3
  32.9 0.0 copy-start.8
  32.9 0.0 copy-start.11
  32.9 15.4 %all_to_all.21 = bf16[8,128,256]{2,1,0:T(8,128)(2,1)} all-to-all(bf16[8,128,256]{2,1,0:T(8,128)(2,1)S(1)} %bitcast.27), channel_id=1, replica_groups={{0,1,4,5,8,9,12,13},{2,3,6,7,10,11,14,15},{16,17,20,21,24,25,28,29},{18..., dimensions={0} | all-to-all | bytes 1048576 | tf_op jit(solution)/shard_map/all_to_all | solution.py:275
  48.2 1.1 reduce_sum.12
  49.3 7.9 %collective-permute-start.1 = (bf16[128,256]{1,0:T(8,128)(2,1)S(1)}, bf16[128,256]{1,0:T(8,128)(2,1)S(1)}, u32[]{:S(2)}, u32[]{:S(2)}) collective-permute-start(bf16[128,256]{1,0:T(8,128)(2,1)S(1)} %reduce_sum.12), channel_id=1, source_target_pairs={{0,2},{1,3},{2,0},{3,1},{4,6},{5,7},{6,4},{7,5},{8,10},{9,11},{10,... | collective-permute-start | bytes 196616 | tf_op jit(solution)/shard_map/ppermute | solution.py:277
  57.3 1.6 %collective-permute-done.1 = bf16[128,256]{1,0:T(8,128)(2,1)S(1)} collective-permute-done((bf16[128,256]{1,0:T(8,128)(2,1)S(1)}, bf16[128,256]{1,0:T(8,128)(2,1)S(1)}, u32[]{:S(2)}, u32[]{:S(2)}) %collective-permute-start.1) | collective-permute-done | bytes 65568 | tf_op jit(solution)/shard_map/ppermute | solution.py:277
  59.0 13.7 %all_to_all.22 = bf16[8,128,256]{2,1,0:T(8,128)(2,1)S(1)} all-to-all(bf16[8,128,256]{2,1,0:T(8,128)(2,1)S(1)} %broadcast_in_dim.12), channel_id=1, replica_groups={{0,1,4,5,8,9,12,13},{2,3,6,7,10,11,14,15},{16,17,20,21,24,25,28,29},{18..., dimensions={0} | all-to-all | bytes 1048576 | tf_op jit(solution)/shard_map/all_to_all | solution.py:280
  72.7 0.0 copy-start.4
  72.7 0.0 copy-done.1
  72.7 0.0 copy-done.3
  72.7 0.0 copy-done.8
  72.7 0.0 copy-done.11
  72.7 0.0 copy-start.15
  72.7 0.0 copy-start.14
  72.7 3.2 %shard_map.105 = (f32[16,128]{1,0:T(8,128)}, f32[8,128]{1,0:T(8,128)S(1)}) custom-call(s32[3,4]{1,0:T(4,128)S(1)} %copy-done.8, s32[3]{0:T(128)S(1)} %copy-done.11, bf16[4,256,256]{2,1,0:T(8,128)(2,1)S(1)} %bitcast.23, f32[8,128]{1,0:T(8,128)S(1)} %get-tuple-element.11.first_ray, bf16[3,4,256,256]{3,2,1,0:T(8,128)(2,1)S(1)} %bitcast.20, ...), custom_call_target="tpu_custom_call" | custom-call | flops 800000000 | bytes 4000000 | tf_op jit(solution)/shard_map/pallas_call | solution.py:131
  76.0 0.0 copy-done.4
  76.0 8.9 %all-to-all-start.2 = ((f32[16,1,128]{2,1,0:T(1,128)}), f32[16,1,128]{2,1,0:T(1,128)S(1)}, u32[]{:S(2)}, u32[]{:S(2)}) async-start(f32[16,1,128]{2,1,0:T(1,128)} %bitcast.8), calls=%async_computation.2 | async-start | bytes 16384 | tf_op jit(solution)/shard_map/all_to_all | solution.py:295
  84.8 0.0 copy-done.15
  84.8 0.1 copy.14
  84.9 9.2 %all-to-all-done.2 = f32[16,1,128]{2,1,0:T(1,128)S(1)} async-done(((f32[16,1,128]{2,1,0:T(1,128)}), f32[16,1,128]{2,1,0:T(1,128)S(1)}, u32[]{:S(2)}, u32[]{:S(2)}) %all-to-all-start.2) | async-done | bytes 8224 | tf_op jit(solution)/shard_map/all_to_all | solution.py:295
  94.2 0.0 copy-done.14
  94.2 0.0 copy-start.5
  94.2 1.0 copy-done.5
  95.2 0.0 copy-start.13
  95.2 1.2 %copy-done.13 = f32[4,256,256]{2,1,0:T(8,128)S(1)} copy-done((f32[4,256,256]{2,1,0:T(8,128)S(1)}, f32[4,256,256]{2,1,0:T(8,128)}, u32[]{:S(2)}) %copy-start.13) | copy-done | bytes 1048600
  96.4 10.5 %shard_map.106 = (f32[4,128,256]{2,1,0:T(8,128)S(1)}, bf16[4,128,256]{2,1,0:T(8,128)(2,1)S(1)}, f32[4,128,256]{2,1,0:T(8,128)S(1)}) custom-call(s32[1,4]{1,0:T(1,128)S(1)} %copy-done.14, f32[16,128]{1,0:T(8,128)S(1)} %bitcast.29, f32[8,128]{1,0:T(8,128)S(1)} %get-tuple-element.13.coupling, f32[4,256,256]{2,1,0:T(8,128)S(1)} %copy-done.13, ...), custom_call_target="tpu_custom_call" | custom-call | flops 900000000 | bytes 4000000 | tf_op jit(solution)/shard_map/pallas_call | solution.py:250
  106.9 1.9 %collective-permute-start.2 = (bf16[4,128,256]{2,1,0:T(8,128)(2,1)S(1)}, bf16[4,128,256]{2,1,0:T(8,128)(2,1)S(1)}, u32[]{:S(2)}, u32[]{:S(2)}) collective-permute-start(bf16[4,128,256]{2,1,0:T(8,128)(2,1)S(1)} %get-tuple-element.17), channel_id=1, source_target_pairs={{0,16},{16,32},{32,48},{48,64},{64,80},{80,96},{96,112},{112,128},... | collective-permute-start | bytes 786440 | tf_op jit(solution)/shard_map/ppermute | solution.py:266
  108.8 1.8 %fusion.1 = bf16[1,4,256,256]{3,2,1,0:T(8,128)(2,1)} fusion(f32[4,128,256]{2,1,0:T(8,128)S(1)} %get-tuple-element.15, f32[4,128,256]{2,1,0:T(8,128)S(1)} %get-tuple-element.16), kind=kOutput, calls=%fused_computation.2 | convolution fusion | flops 403177472 | bytes 1572864 | tf_op jit(solution)/shard_map/bki,bkj->bij/dot_general | solution.py:298
  110.7 10.2 %collective-permute-done.2 = bf16[4,128,256]{2,1,0:T(8,128)(2,1)S(1)} collective-permute-done((bf16[4,128,256]{2,1,0:T(8,128)(2,1)S(1)}, bf16[4,128,256]{2,1,0:T(8,128)(2,1)S(1)}, u32[]{:S(2)}, u32[]{:S(2)}) %collective-permute-start.2) | collective-permute-done | bytes 262176 | tf_op jit(solution)/shard_map/ppermute | solution.py:266
  120.9 0.7 copy.18
  (2 shorter events, 0.1 us)
Async XLA Ops:
  0.6 22.2 %collective-permute-start = (bf16[1,4,256,256]{3,2,1,0:T(8,128)(2,1)}, bf16[1,4,256,256]{3,2,1,0:T(8,128)(2,1)S(1)}, u32[]{:S(2)}, u32[]{:S(2)}) collective-permute-start(bf16[1,4,256,256]{3,2,1,0:T(8,128)(2,1)} %param.10), channel_id=1, source_target_pairs={{0,496},{16,0},{32,16},{48,32},{64,48},{80,64},{96,80},{112,96},{1... | collective-permute-start | bytes 1572872 | tf_op jit(solution)/shard_map/ppermute | solution.py:266
  22.9 1.4 %copy-start = (bf16[1,3,4,256,256]{4,3,2,1,0:T(8,128)(2,1)S(1)}, bf16[1,3,4,256,256]{4,3,2,1,0:T(8,128)(2,1)}, u32[]{:S(2)}) copy-start(bf16[1,3,4,256,256]{4,3,2,1,0:T(8,128)(2,1)} %param.12) | copy-start | bytes 4718596
  24.3 1.4 %copy-start.2 = (bf16[1,3,4,256,256]{4,3,2,1,0:T(8,128)(2,1)S(1)}, bf16[1,3,4,256,256]{4,3,2,1,0:T(8,128)(2,1)}, u32[]{:S(2)}) copy-start(bf16[1,3,4,256,256]{4,3,2,1,0:T(8,128)(2,1)} %param.13) | copy-start | bytes 4718596
  25.7 1.0 copy-start.6
  26.7 0.7 copy-start.7
  27.4 0.7 copy-start.9
  28.1 0.7 copy-start.10
  31.9 1.0 copy-start.12
  32.9 39.8 %copy-start.1 = (bf16[1,3,4,256,256]{4,3,2,1,0:T(8,128)(2,1)S(1)}, bf16[1,3,4,256,256]{4,3,2,1,0:T(8,128)(2,1)}, u32[]{:S(2)}) copy-start(bf16[1,3,4,256,256]{4,3,2,1,0:T(8,128)(2,1)} %param.12) | copy-start | bytes 4718596
  32.9 39.8 %copy-start.3 = (bf16[1,3,4,256,256]{4,3,2,1,0:T(8,128)(2,1)S(1)}, bf16[1,3,4,256,256]{4,3,2,1,0:T(8,128)(2,1)}, u32[]{:S(2)}) copy-start(bf16[1,3,4,256,256]{4,3,2,1,0:T(8,128)(2,1)} %param.13) | copy-start | bytes 4718596
  32.9 39.8 %copy-start.8 = (s32[3,4]{1,0:T(4,128)S(1)}, s32[3,4]{1,0:T(4,128)}, u32[]{:S(2)}) copy-start(s32[3,4]{1,0:T(4,128)} %source.3) | copy-start | bytes 148
  32.9 39.8 %copy-start.11 = (s32[3]{0:T(128)S(1)}, s32[3]{0:T(128)}, u32[]{:S(2)}) copy-start(s32[3]{0:T(128)} %active.3) | copy-start | bytes 40
  49.3 9.6 %collective-permute-start.1 = (bf16[128,256]{1,0:T(8,128)(2,1)S(1)}, bf16[128,256]{1,0:T(8,128)(2,1)S(1)}, u32[]{:S(2)}, u32[]{:S(2)}) collective-permute-start(bf16[128,256]{1,0:T(8,128)(2,1)S(1)} %reduce_sum.12), channel_id=1, source_target_pairs={{0,2},{1,3},{2,0},{3,1},{4,6},{5,7},{6,4},{7,5},{8,10},{9,11},{10,... | collective-permute-start | bytes 196616 | tf_op jit(solution)/shard_map/ppermute | solution.py:277
  72.7 3.3 %copy-start.4 = (bf16[8,128,256]{2,1,0:T(8,128)(2,1)}, bf16[8,128,256]{2,1,0:T(8,128)(2,1)S(1)}, u32[]{:S(2)}) copy-start(bf16[8,128,256]{2,1,0:T(8,128)(2,1)S(1)} %all_to_all.22) | copy-start | bytes 1572868
  72.7 12.1 %copy-start.15 = (f32[1,256,128]{2,1,0:T(8,128)S(1)}, f32[1,256,128]{2,1,0:T(8,128)}, u32[]{:S(2)}) copy-start(f32[1,256,128]{2,1,0:T(8,128)} %param.16) | copy-start | bytes 393220
  72.7 21.4 %copy-start.14 = (s32[1,4]{1,0:T(1,128)S(1)}, s32[1,4]{1,0:T(1,128)}, u32[]{:S(2)}) copy-start(s32[1,4]{1,0:T(1,128)} %kept.1) | copy-start | bytes 52
  76.0 18.2 %all-to-all-start.2 = ((f32[16,1,128]{2,1,0:T(1,128)}), f32[16,1,128]{2,1,0:T(1,128)S(1)}, u32[]{:S(2)}, u32[]{:S(2)}) async-start(f32[16,1,128]{2,1,0:T(1,128)} %bitcast.8), calls=%async_computation.2 | async-start | bytes 16384 | tf_op jit(solution)/shard_map/all_to_all | solution.py:295
  94.2 1.0 copy-start.5
  95.2 1.2 %copy-start.13 = (f32[4,256,256]{2,1,0:T(8,128)S(1)}, f32[4,256,256]{2,1,0:T(8,128)}, u32[]{:S(2)}) copy-start(f32[4,256,256]{2,1,0:T(8,128)} %copy-done.12) | copy-start | bytes 3145732
  106.9 14.0 %collective-permute-start.2 = (bf16[4,128,256]{2,1,0:T(8,128)(2,1)S(1)}, bf16[4,128,256]{2,1,0:T(8,128)(2,1)S(1)}, u32[]{:S(2)}, u32[]{:S(2)}) collective-permute-start(bf16[4,128,256]{2,1,0:T(8,128)(2,1)S(1)} %get-tuple-element.17), channel_id=1, source_target_pairs={{0,16},{16,32},{32,48},{48,64},{64,80},{80,96},{96,112},{112,128},... | collective-permute-start | bytes 786440 | tf_op jit(solution)/shard_map/ppermute | solution.py:266

commit v3 on v2

v3 whole, which is shorter than its diff:
```python
import jax
import jax.numpy as jnp
from jax import lax
from jax.experimental import pallas as pl
from jax.experimental.pallas import tpu as pltpu
from jax.sharding import PartitionSpec as P

bf16, f32 = jnp.bfloat16, jnp.float32
HIGHEST = lax.Precision.HIGHEST
NN = (((1,), (0,)), ((), ()))
NT = (((1,), (1,)), ((), ()))

SMEM = pl.BlockSpec(memory_space=pltpu.SMEM)
VMEM = pl.BlockSpec(memory_space=pltpu.VMEM)
HBM = pl.BlockSpec(memory_space=pltpu.HBM)


def call(kernel, operands, in_specs, outs, out_specs, scratch=(), flops=0, moved=0):
    return pl.pallas_call(
        kernel,
        out_shape=tuple(jax.ShapeDtypeStruct(shape, dtype) for shape, dtype in outs),
        in_specs=in_specs,
        out_specs=tuple(out_specs),
        scratch_shapes=list(scratch),
        compiler_params=pltpu.CompilerParams(vmem_limit_bytes=24 * 2**20),
        cost_estimate=pl.CostEstimate(flops=flops, bytes_accessed=moved, transcendentals=0),
    )(*operands)


def prepare_kernel(left_part, inverse, lenv_hbm, renv_hbm, scaled, lenv, renv, sems):
    copies = []
    for slot in range(lenv.shape[0]):
        rows = pl.ds(slot * 256, 256)
        copies.append(pltpu.make_async_copy(lenv_hbm.at[slot], lenv.at[slot], sems.at[slot, 0]))
        copies.append(
            pltpu.make_async_copy(renv_hbm.at[slot], renv.at[:, rows, :], sems.at[slot, 1])
        )
    for copy in copies:
        copy.start()
    for b in range(left_part.shape[0]):
        scaled[b] = (left_part[b].astype(f32) * inverse[b : b + 1, :]).astype(bf16)
    for copy in copies:
        copy.wait()


def first_kernel(
    source, active, scaled, neighbour, lenv, renv,
    first_hbm, part, ray, first, inner, vector, image, sems,
):
    slots, sectors = lenv.shape[:2]
    count = sectors * 256 * 256
    squares = jnp.zeros((1, 256), f32)
    for b in range(sectors):
        center = jnp.dot(scaled[b], neighbour[b], preferred_element_type=f32)
        image[b] = center
        squares += jnp.sum(center * center, axis=0, keepdims=True)
    scale = lax.rsqrt(jnp.sum(squares, axis=1, keepdims=True) / count + 1e-06)
    out_copies = []
    for b in range(sectors):
        scaled_center = image[b] * scale
        first[b] = scaled_center
        out_copies.append(pltpu.make_async_copy(first.at[b], first_hbm.at[b], sems.at[b]))
        out_copies[b].start()
        vector[b] = scaled_center.astype(bf16)
    for slot in range(slots):
        flag = active[slot].astype(f32)
        for b in range(sectors):
            product = jnp.dot(
                lenv[slot, b], vector[source[slot, b]], preferred_element_type=f32
            )
            inner[b, :, slot * 256 : (slot + 1) * 256] = (product * flag).astype(bf16)
    dots = jnp.zeros((1, 256), f32)
    for b in range(sectors):
        own = jnp.dot(inner[b], renv[b], preferred_element_type=f32)
        image[b] = own
        dots += jnp.sum(first[b] * own, axis=0, keepdims=True)
    own_ray = jnp.sum(dots, axis=1, keepdims=True) / count
    for b in range(sectors):
        part[b] = (image[b] - own_ray * first[b]).astype(bf16)
    ray[...] = jnp.broadcast_to(own_ray, ray.shape)
    for copy in out_copies:
        copy.wait()


def second_kernel(source, active, resid, first_ray, lenv, renv, rays, coupling, inner, vector):
    slots, sectors = lenv.shape[:2]
    count = sectors * 256 * 256
    squares = jnp.zeros((1, 256), f32)
    for b in range(sectors):
        piece = resid[b].astype(f32)
        squares += jnp.sum(piece * piece, axis=0, keepdims=True)
    mean_square = jnp.sum(squares, axis=1, keepdims=True) / count + 1e-06
    scale = lax.rsqrt(mean_square)
    for b in range(sectors):
        vector[b] = (resid[b].astype(f32) * scale).astype(bf16)
    for slot in range(slots):
        flag = active[slot].astype(f32)
        for b in range(sectors):
            product = jnp.dot(
                lenv[slot, b], vector[source[slot, b]], preferred_element_type=f32
            )
            inner[b, :, slot * 256 : (slot + 1) * 256] = (product * flag).astype(bf16)
    dots = jnp.zeros((1, 256), f32)
    for b in range(sectors):
        own = jnp.dot(inner[b, :, :256], renv[0, b], preferred_element_type=f32)
        for slot in range(1, slots):
            lanes = slice(slot * 256, (slot + 1) * 256)
            own += jnp.dot(inner[b, :, lanes], renv[slot, b], preferred_element_type=f32)
        dots += jnp.sum(resid[b].astype(f32) * own, axis=0, keepdims=True)
    own_ray = jnp.sum(dots, axis=1, keepdims=True) * scale / count
    lane = lax.broadcasted_iota(jnp.int32, rays.shape, 1)
    rays[...] = jnp.where(lane == 0, first_ray[0:1, :], jnp.broadcast_to(own_ray, rays.shape))
    coupling[...] = jnp.broadcast_to(jnp.sqrt(mean_square), coupling.shape)


def split(array):
    high = array.astype(bf16)
    return high, (array - high.astype(f32)).astype(bf16)


def dot(left, right, dims=NN):
    return lax.dot_general(left, right, dims, preferred_element_type=f32)


def fine_dot(left, right, dims=NN):
    return dot(left[0], right[0], dims) + (
        dot(left[0], right[1], dims) + dot(left[1], right[0], dims)
    )


def exact_dot(left, right, dims=NN):
    return lax.dot_general(left, right, dims, precision=HIGHEST, preferred_element_type=f32)


def quadratic_kernel(kept, first, resid, sketch, images, grams, corr_ff, corr_x, corr_ss):
    sectors, size = first.shape[:2]
    cols = sketch.shape[0]
    tests = split(sketch[...])
    row = lax.broadcasted_iota(jnp.int32, (cols, size), 0)
    for b in range(sectors):
        wide = row < kept[0, b]
        other = resid[b]
        ground = split(first[b])
        of_first = jnp.where(wide, fine_dot(tests, ground, NT), 0.0)
        of_resid = jnp.where(wide, dot(tests[0], other, NT) + dot(tests[1], other, NT), 0.0)
        images[b, :cols] = of_first
        images[b, cols:] = of_resid
        both = split(images[b])
        grams[b] = fine_dot(both, both, NT)
        with_first = fine_dot(both, ground)
        with_resid = dot(both[0], other) + dot(both[1], other)
        corr_ff[b] = with_first[:cols]
        corr_x[b] = with_first[cols:] + with_resid[:cols]
        corr_ss[b] = with_resid[cols:]


def invert_blocks(packed):
    size = packed.shape[0]
    row = lax.broadcasted_iota(jnp.int32, packed.shape, 0)
    lane = lax.broadcasted_iota(jnp.int32, packed.shape, 1)
    place = lane % size
    start = lane - place

    def column(array, k):
        return jnp.take_along_axis(array, start + k, axis=1)

    here = column(packed, 0)
    for k in range(size):
        ahead = column(packed, k + 1) if k + 1 < size else None
        inverse = 1.0 / here[k : k + 1, :]
        pivot_row = jnp.where(place[k : k + 1, :] == k, 1.0, packed[k : k + 1, :]) * inverse
        packed = jnp.where(place == k, 0.0, packed) - here * pivot_row
        packed = jnp.where(row == k, pivot_row, packed)
        if ahead is not None:
            factor = here[k + 1 : k + 2, :] * inverse
            here = jnp.where(row == k, factor, ahead - here * factor)
    return packed


def invert(gram):
    sectors, cols, size = len(gram), gram[0].shape[0], 32
    row = lax.broadcasted_iota(jnp.int32, (cols, cols), 0)
    lane = lax.broadcasted_iota(jnp.int32, (cols, cols), 1)
    same = (row // size) == (lane // size)
    unit = jnp.where(row % size == lane % size, 1.0, 0.0).astype(f32)
    block_lane = lax.broadcasted_iota(jnp.int32, (size, cols), 1) // size
    for p in range(cols // size):
        rows = slice(p * size, (p + 1) * size)
        packed = jnp.zeros((size, cols), f32)
        for s in range(sectors):
            shift = ((s - p) * size) % cols
            turned = pltpu.roll(gram[s][rows], shift, 1) if shift else gram[s][rows]
            packed = jnp.where(block_lane == s, turned, packed)
        inverse = invert_blocks(packed)
        inverse = jnp.where(same, jnp.concatenate([inverse] * sectors, axis=0), 0.0)
        stacked = jnp.concatenate([g[rows] for g in gram], axis=0)
        stacked = jnp.where(lane // size == p, unit, stacked)
        panel = exact_dot(inverse, stacked)
        for s in range(sectors):
            own = panel[s * size : (s + 1) * size]
            tiled = jnp.concatenate([own] * (cols // size), axis=0)
            factor = jnp.where((lane // size == p) & (row // size != p), gram[s], 0.0)
            rest = jnp.where(lane // size == p, 0.0, gram[s])
            rest = jnp.where(row // size == p, tiled, rest)
            gram[s] = rest - exact_dot(factor, tiled)
    return gram


def solve_kernel(
    kept, rays, coupling, images, grams, corr_ff, corr_x, corr_ss, right, right_low, image
):
    sectors, size = corr_x.shape[0], corr_x.shape[2]
    cols = corr_x.shape[1]
    sums = jnp.sum(rays[...], axis=0, keepdims=True)
    ray_first, ray_second = sums[:, 0:1], sums[:, 1:2]
    between = coupling[0:1, 0:1]
    half = 0.5 * (ray_second - ray_first)
    weight = half + jnp.sqrt(half * half + between * between)
    length = lax.rsqrt(weight * weight + between * between)
    of_first, of_resid = weight * length, -length
    ff, fs, ss = of_first * of_first, of_first * of_resid, of_resid * of_resid
    row = lax.broadcasted_iota(jnp.int32, (cols, cols), 0)
    lane = lax.broadcasted_iota(jnp.int32, (cols, cols), 1)
    gram = []
    for b in range(sectors):
        empty = jnp.where((row == lane) & (row >= kept[0, b]), 1.0, 0.0)
        mixed = grams[b, :cols, cols:] + grams[b, cols:, :cols]
        own = ff * grams[b, :cols, :cols] + fs * mixed + ss * grams[b, cols:, cols:]
        gram.append(own * (1.0 / (size * size)) + empty)
    gram = invert(gram)
    for b in range(sectors):
        correlation = ff * corr_ff[b] + fs * corr_x[b] + ss * corr_ss[b]
        own = exact_dot(gram[b], correlation) * (1.0 / size)
        right[b] = own
        right_low[b] = own.astype(bf16)
        image[b] = of_first * images[b, :cols] + of_resid * images[b, cols:]


def plane_groups():
    return [[x * 4 + z * 2 + c for x in range(4) for c in range(2)] for z in range(2)]


def across_seg(array, by):
    segs, ops = lax.axis_size("seg"), lax.axis_size("op")
    pairs = []
    for seg in range(segs):
        for op in range(ops):
            other = op if 0 <= seg + by < segs else op ^ 2
            pairs.append((seg * ops + op, (seg + by) % segs * ops + other))
    return lax.ppermute(array, ("seg", "op"), pairs)


def sum_over_op(part):
    chunks = part.reshape(8, 128, 256)
    chunks = lax.all_to_all(chunks, "op", 0, 0, axis_index_groups=plane_groups(), tiled=True)
    own = jnp.sum(chunks.astype(f32), axis=0).astype(bf16)
    other = lax.ppermute(own, "op", [(i, i ^ 2) for i in range(16)])
    both = (own.astype(f32) + other.astype(f32)).astype(bf16)
    spread = jnp.broadcast_to(both[None], (8, 128, 256))
    whole = lax.all_to_all(spread, "op", 0, 0, axis_index_groups=plane_groups(), tiled=True)
    return whole.reshape(4, 256, 256)


def shards(
    left_part, right_part, inverse_values, left_env, right_env, source, term_active, sketch, kept
):
    lenv, renv = left_env[0], right_env[0]
    slots, sectors = lenv.shape[:2]
    whole, cols = (sectors, 256, 256), sketch.shape[2]
    neighbour = across_seg(right_part[0], -1)
    tests = sketch[0].T
    scaled, lenv_near, renv_near = call(
        prepare_kernel,
        (left_part[0], inverse_values[0], lenv, renv),
        [VMEM, VMEM, HBM, HBM],
        [(whole, bf16), (lenv.shape, bf16), ((sectors, slots * 256, 256), bf16)],
        [VMEM] * 3,
        [pltpu.SemaphoreType.DMA((slots, 2))],
        moved=8_000_000,
    )
    inner = pltpu.VMEM((sectors, 256, slots * 256), bf16)
    first, part, ray = call(
        first_kernel,
        (source, term_active, scaled, neighbour, lenv_near, renv_near),
        [SMEM, SMEM] + [VMEM] * 4,
        [(whole, f32), (whole, bf16), ((8, 128), f32)],
        [HBM, VMEM, VMEM],
        [
            pltpu.VMEM(whole, f32), inner, pltpu.VMEM(whole, bf16), pltpu.VMEM(whole, f32),
            pltpu.SemaphoreType.DMA((sectors,)),
        ],
        flops=940_000_000, moved=6_000_000,
    )
    resid = sum_over_op(part)
    rays, coupling = call(
        second_kernel,
        (source, term_active, resid, ray, lenv, renv),
        [SMEM, SMEM] + [VMEM] * 4,
        [((16, 128), f32), ((8, 128), f32)],
        [VMEM] * 2,
        [inner, pltpu.VMEM(whole, bf16)],
        flops=800_000_000, moved=4_000_000,
    )
    rays = lax.all_to_all(rays, "op", 0, 0, tiled=True)
    quadratic = call(
        quadratic_kernel,
        (kept, first, resid, tests),
        [SMEM] + [VMEM] * 3,
        [((sectors, 2 * cols, 256), f32)] * 2 + [((sectors, cols, 256), f32)] * 3,
        [VMEM] * 5,
        flops=1_600_000_000, moved=6_000_000,
    )
    right, right_low, image = call(
        solve_kernel,
        (kept, rays, coupling) + tuple(quadratic),
        [SMEM] + [VMEM] * 7,
        [((sectors, cols, 256), f32), ((sectors, cols, 256), bf16), ((sectors, cols, 256), f32)],
        [VMEM] * 3,
        flops=800_000_000, moved=5_000_000,
    )
    handed = across_seg(right_low, 1)
    kept_state = jnp.einsum("bki,bkj->bij", image, right, precision=HIGHEST) / 256
    return (kept_state.astype(bf16)[None], handed[None])


def solution(mesh):
    placed = (
        P("seg", None, None, None),
        P("seg", None, None, None),
        P("seg", None, None),
        P("seg", "op", None, None, None),
        P("seg", "op", None, None, None),
        P("op", None),
        P("op"),
        P("seg", None, None),
        P("seg", None),
    )
    return jax.shard_map(
        shards,
        mesh=mesh,
        in_specs=placed,
        out_specs=(P("seg", None, None, None), P("seg", None, None, None)),
        check_vma=False,
    )
```

time: 122 us -> 114 us (0.934)
  blocking collectives: 29 us -> 15.2 us
  waiting for transfers between devices: 31.9 us -> 36.9 us
  Pallas kernels: 16.8 us -> 18.8 us
  starting transfers between devices: 30.1 us -> 28.2 us
    all_to_all x1 -> x0, blocking collectives: 13.7 us -> none  [sum_over_op(): lax.all_to_all(spread, 'op', 0, 0, axis_index_groups=plane_groups(), tile...]
    all_to_all x0 -> x1, waiting for transfers between devices: none -> 9.5 us  [sum_over_op(): lax.all_to_all(spread, 'op', 0, 0, axis_index_groups=plane_groups(), tile...]
    ppermute x1, waiting for transfers between devices: 1.64 us -> 7.67 us  [sum_over_op(): other = lax.ppermute(own, 'op', [(i, i ^ 2) for i in range(16)])]
    ppermute x1, starting transfers between devices: 7.94 us -> 1.92 us  [sum_over_op(): other = lax.ppermute(own, 'op', [(i, i ^ 2) for i in range(16)])]
    all_to_all x0 -> x1, starting transfers between devices: none -> 5.86 us  [sum_over_op(): lax.all_to_all(spread, 'op', 0, 0, axis_index_groups=plane_groups(), tile...]
    all_to_all x1, waiting for transfers between devices: 9.21 us -> 3.69 us  [shards(): rays = lax.all_to_all(rays, 'op', 0, 0, tiled=True)]
    ppermute x2, waiting for transfers between devices: 21.1 us -> 16.1 us  [across_seg(): return lax.ppermute(array, ('seg', 'op'), pairs)]
    all_to_all x1, starting transfers between devices: 8.86 us -> 4.13 us  [shards(): rays = lax.all_to_all(rays, 'op', 0, 0, tiled=True)]
  transfers between devices with their start and end apart: 4 -> 5, of which waited for: 4 -> 5; matrix products, arithmetic and copies ran while one was open for 2% -> 2% of each run, Pallas kernels for 0% -> 4%
where the time goes in v3:
time: 114 us; the launch traced here: 113 us
  waiting for transfers between devices  36.9 us (32%)
  starting transfers between devices  28.2 us (25%)
  Pallas kernels  18.8 us (16%)
  blocking collectives  15.2 us (13%)
  local copies, waits for them, and re-layouts  10.2 us (9%)
  matrix products  1.83 us (2%)
  other arithmetic  1.25 us (1%)
    pallas_call x5, Pallas kernels, call(): pl.pallas_call(kernel, out_shape=tuple((jax.ShapeDtypeStruct(shape, dtype...  18.8 us
    ppermute x2, starting transfers between devices, across_seg(): return lax.ppermute(array, ('seg', 'op'), pairs)  16.3 us
    ppermute x2, waiting for transfers between devices, across_seg(): return lax.ppermute(array, ('seg', 'op'), pairs)  16.1 us
    all_to_all x1, blocking collectives, sum_over_op(): lax.all_to_all(chunks, 'op', 0, 0, axis_index_groups=plane_groups(), tile...  15.2 us
    all_to_all x1, waiting for transfers between devices, sum_over_op(): lax.all_to_all(spread, 'op', 0, 0, axis_index_groups=plane_groups(), tile...  9.5 us
    unnamed x30, local copies, waits for them, and re-layouts  9.39 us
    ppermute x1, waiting for transfers between devices, sum_over_op(): other = lax.ppermute(own, 'op', [(i, i ^ 2) for i in range(16)])  7.67 us
    all_to_all x1, starting transfers between devices, sum_over_op(): lax.all_to_all(spread, 'op', 0, 0, axis_index_groups=plane_groups(), tile...  5.86 us
  transfers between devices with their start and end apart: 5, of which 5 were waited for; matrix products, arithmetic and copies ran while one was open for 2% of the time, Pallas kernels for 4%

profile of v3, /device:TPU:1, one launch (start us, length us, event | category | flops | bytes accessed | tf_op | source)
XLA Modules:
  0.0 113.3 jit_solution(4480853274285684895)
XLA Ops:
  0.6 14.4 %collective-permute-start = (bf16[4,256,256]{2,1,0:T(8,128)(2,1)}, bf16[4,256,256]{2,1,0:T(8,128)(2,1)S(1)}, u32[]{:S(2)}, u32[]{:S(2)}) collective-permute-start(bf16[4,256,256]{2,1,0:T(8,128)(2,1)} %bitcast.29), channel_id=1, source_target_pairs={{0,498},{1,499},{2,496},{3,497},{4,502},{5,503},{6,500},{7,501},{8... | collective-permute-start | bytes 1572872 | tf_op jit(solution)/shard_map/ppermute | solution.py:250
  15.0 0.0 copy-start
  15.1 1.4 %copy-done = bf16[1,3,4,256,256]{4,3,2,1,0:T(8,128)(2,1)S(1)} copy-done((bf16[1,3,4,256,256]{4,3,2,1,0:T(8,128)(2,1)S(1)}, bf16[1,3,4,256,256]{4,3,2,1,0:T(8,128)(2,1)}, u32[]{:S(2)}) %copy-start) | copy-done | bytes 1572888
  16.5 0.0 copy-start.2
  16.5 1.4 %copy-done.2 = bf16[1,3,4,256,256]{4,3,2,1,0:T(8,128)(2,1)S(1)} copy-done((bf16[1,3,4,256,256]{4,3,2,1,0:T(8,128)(2,1)S(1)}, bf16[1,3,4,256,256]{4,3,2,1,0:T(8,128)(2,1)}, u32[]{:S(2)}) %copy-start.2) | copy-done | bytes 1572888
  17.9 0.0 copy-start.6
  17.9 1.0 copy-done.6
  18.9 0.0 copy-start.8
  18.9 0.7 copy-done.8
  19.6 0.0 copy-start.7
  19.6 0.0 copy-start.9
  19.6 0.4 shard_map.104
  20.0 6.0 %collective-permute-done.neighbour = bf16[4,256,256]{2,1,0:T(8,128)(2,1)S(1)} collective-permute-done((bf16[4,256,256]{2,1,0:T(8,128)(2,1)}, bf16[4,256,256]{2,1,0:T(8,128)(2,1)S(1)}, u32[]{:S(2)}, u32[]{:S(2)}) %collective-permute-start) | collective-permute-done | bytes 524320 | tf_op jit(solution)/shard_map/ppermute | solution.py:250
  25.9 0.0 copy-done.7
  25.9 0.0 copy-done.9
  25.9 2.4 %shard_map.105 = (f32[4,256,256]{2,1,0:T(8,128)S(1)}, bf16[4,256,256]{2,1,0:T(8,128)(2,1)S(1)}, f32[8,128]{1,0:T(8,128)S(1)}) custom-call(s32[3,4]{1,0:T(4,128)S(1)} %copy-done.7, s32[3]{0:T(128)S(1)} %copy-done.9, bf16[4,256,256]{2,1,0:T(8,128)(2,1)S(1)} %get-tuple-element.18.scaled, bf16[4,256,256]{2,1,0:T(8,128)(2,1)S(1)} %collective-permute-done.neighbour, ...), custom_call_target="tpu_custom_call" | custom-call | flops 940000000 | bytes 6000000 | tf_op jit(solution)/shard_map/pallas_call | solution.py:19
  28.4 0.0 copy-start.11
  28.4 1.0 copy-done.11
  29.4 0.0 copy-start.13
  29.4 0.0 copy-start.3
  29.4 15.2 %all_to_all.21 = bf16[8,128,256]{2,1,0:T(8,128)(2,1)} all-to-all(bf16[8,128,256]{2,1,0:T(8,128)(2,1)S(1)} %bitcast.23), channel_id=1, replica_groups={{0,1,4,5,8,9,12,13},{2,3,6,7,10,11,14,15},{16,17,20,21,24,25,28,29},{18..., dimensions={0} | all-to-all | bytes 1048576 | tf_op jit(solution)/shard_map/all_to_all | solution.py:255
  44.6 0.0 copy-start.1
  44.6 1.2 %reduce_sum.12 = bf16[128,256]{1,0:T(8,128)(2,1)S(1)} reduce(bf16[8,128,256]{2,1,0:T(8,128)(2,1)} %all_to_all.21, bf16[]{:T(256)} %constant.4.clone.1), dimensions={0}, to_apply=%region_0.0 | reduce | flops 229376 | bytes 589826 | tf_op jit(solution)/shard_map/reduce_sum | solution.py:256
  45.8 1.9 %collective-permute-start.1 = (bf16[128,256]{1,0:T(8,128)(2,1)S(1)}, bf16[128,256]{1,0:T(8,128)(2,1)S(1)}, u32[]{:S(2)}, u32[]{:S(2)}) collective-permute-start(bf16[128,256]{1,0:T(8,128)(2,1)S(1)} %reduce_sum.12), channel_id=1, source_target_pairs={{0,2},{1,3},{2,0},{3,1},{4,6},{5,7},{6,4},{7,5},{8,10},{9,11},{10,... | collective-permute-start | bytes 196616 | tf_op jit(solution)/shard_map/ppermute | solution.py:257
  47.8 7.7 %collective-permute-done.1 = bf16[128,256]{1,0:T(8,128)(2,1)S(1)} collective-permute-done((bf16[128,256]{1,0:T(8,128)(2,1)S(1)}, bf16[128,256]{1,0:T(8,128)(2,1)S(1)}, u32[]{:S(2)}, u32[]{:S(2)}) %collective-permute-start.1) | collective-permute-done | bytes 65568 | tf_op jit(solution)/shard_map/ppermute | solution.py:257
  55.4 0.8 broadcast_in_dim.12
  56.3 5.9 %all-to-all-start.1 = ((bf16[8,128,256]{2,1,0:T(8,128)(2,1)}), bf16[8,128,256]{2,1,0:T(8,128)(2,1)}, u32[]{:S(2)}, u32[]{:S(2)}) async-start(bf16[8,128,256]{2,1,0:T(8,128)(2,1)} %broadcast_in_dim.12), calls=%async_computation.1 | async-start | bytes 1048576 | tf_op jit(solution)/shard_map/all_to_all | solution.py:260
  62.1 0.0 copy-done.13
  62.1 0.1 copy.14
  62.2 9.5 %all-to-all-done.1 = bf16[8,128,256]{2,1,0:T(8,128)(2,1)} async-done(((bf16[8,128,256]{2,1,0:T(8,128)(2,1)}), bf16[8,128,256]{2,1,0:T(8,128)(2,1)}, u32[]{:S(2)}, u32[]{:S(2)}) %all-to-all-start.1) | async-done | bytes 524320 | tf_op jit(solution)/shard_map/all_to_all | solution.py:260
  71.7 0.0 copy-done.3
  71.7 0.0 copy-done.1
  71.7 0.0 copy-start.10
  71.7 3.0 %shard_map.106 = (f32[16,128]{1,0:T(8,128)}, f32[8,128]{1,0:T(8,128)S(1)}) custom-call(s32[3,4]{1,0:T(4,128)S(1)} %copy-done.7, s32[3]{0:T(128)S(1)} %copy-done.9, bf16[4,256,256]{2,1,0:T(8,128)(2,1)} %bitcast.6.resid, f32[8,128]{1,0:T(8,128)S(1)} %get-tuple-element.22.first_ray, bf16[3,4,256,256]{3,2,1,0:T(8,128)(2,1)S(1)} %bitcast.20, ...), custom_call_target="tpu_custom_call" | custom-call | flops 800000000 | bytes 4000000 | tf_op jit(solution)/shard_map/pallas_call | solution.py:19
  74.8 4.1 %all-to-all-start.2 = ((f32[16,1,128]{2,1,0:T(1,128)}), f32[16,1,128]{2,1,0:T(1,128)S(1)}, u32[]{:S(2)}, u32[]{:S(2)}) async-start(f32[16,1,128]{2,1,0:T(1,128)} %bitcast.8), calls=%async_computation.2 | async-start | bytes 16384 | tf_op jit(solution)/shard_map/all_to_all | solution.py:304
  78.9 0.0 copy-done.10
  78.9 0.0 copy-start.12
  78.9 1.2 %copy-done.12 = f32[4,256,256]{2,1,0:T(8,128)S(1)} copy-done((f32[4,256,256]{2,1,0:T(8,128)S(1)}, f32[4,256,256]{2,1,0:T(8,128)}, u32[]{:S(2)}) %copy-start.12) | copy-done | bytes 1048600
  80.1 3.7 %shard_map.107 = (f32[4,256,256]{2,1,0:T(8,128)S(1)}, f32[4,256,256]{2,1,0:T(8,128)S(1)}, f32[4,128,256]{2,1,0:T(8,128)S(1)}, f32[4,128,256]{2,1,0:T(8,128)S(1)}, f32[4,128,256]{2,1,0:T(8,128)S(1)}) custom-call(s32[1,4]{1,0:T(1,128)S(1)} %copy-done.10, f32[4,256,256]{2,1,0:T(8,128)S(1)} %copy-done.12, bf16[4,256,256]{2,1,0:T(8,128)(2,1)} %bitcast.6.resid, ...), custom_call_target="tpu_custom_call" | custom-call | flops 1600000000 | bytes 6000000 | tf_op jit(solution)/shard_map/pallas_call | solution.py:19
  83.8 0.0 copy-start.4
  83.8 0.8 copy-done.4
  84.6 3.7 %all-to-all-done.2 = f32[16,1,128]{2,1,0:T(1,128)S(1)} async-done(((f32[16,1,128]{2,1,0:T(1,128)}), f32[16,1,128]{2,1,0:T(1,128)S(1)}, u32[]{:S(2)}, u32[]{:S(2)}) %all-to-all-start.2) | async-done | bytes 8224 | tf_op jit(solution)/shard_map/all_to_all | solution.py:304
  88.3 0.0 copy-start.5
  88.3 1.0 copy-done.5
  89.3 9.4 %shard_map.108 = (f32[4,128,256]{2,1,0:T(8,128)S(1)}, bf16[4,128,256]{2,1,0:T(8,128)(2,1)S(1)}, f32[4,128,256]{2,1,0:T(8,128)S(1)}) custom-call(s32[1,4]{1,0:T(1,128)S(1)} %copy-done.10, f32[16,128]{1,0:T(8,128)S(1)} %bitcast.26, f32[8,128]{1,0:T(8,128)S(1)} %get-tuple-element.24.coupling, f32[4,256,256]{2,1,0:T(8,128)S(1)} %get-tuple-element.26.images, ...), custom_call_target="tpu_custom_call" | custom-call | flops 800000000 | bytes 5000000 | tf_op jit(solution)/shard_map/pallas_call | solution.py:19
  98.7 1.9 %collective-permute-start.2 = (bf16[4,128,256]{2,1,0:T(8,128)(2,1)S(1)}, bf16[4,128,256]{2,1,0:T(8,128)(2,1)S(1)}, u32[]{:S(2)}, u32[]{:S(2)}) collective-permute-start(bf16[4,128,256]{2,1,0:T(8,128)(2,1)S(1)} %get-tuple-element.33), channel_id=1, source_target_pairs={{0,16},{1,17},{2,18},{3,19},{4,20},{5,21},{6,22},{7,23},{8,24},{9,... | collective-permute-start | bytes 786440 | tf_op jit(solution)/shard_map/ppermute | solution.py:250
  100.6 1.8 %fusion.1 = bf16[1,4,256,256]{3,2,1,0:T(8,128)(2,1)} fusion(f32[4,128,256]{2,1,0:T(8,128)S(1)} %get-tuple-element.31, f32[4,128,256]{2,1,0:T(8,128)S(1)} %get-tuple-element.32), kind=kOutput, calls=%fused_computation.2 | convolution fusion | flops 403177472 | bytes 1572864 | tf_op jit(solution)/shard_map/bki,bkj->bij/dot_general | solution.py:322
  102.4 10.1 %collective-permute-done.2 = bf16[4,128,256]{2,1,0:T(8,128)(2,1)S(1)} collective-permute-done((bf16[4,128,256]{2,1,0:T(8,128)(2,1)S(1)}, bf16[4,128,256]{2,1,0:T(8,128)(2,1)S(1)}, u32[]{:S(2)}, u32[]{:S(2)}) %collective-permute-start.2) | collective-permute-done | bytes 262176 | tf_op jit(solution)/shard_map/ppermute | solution.py:250
  112.5 0.7 copy.18
  (1 shorter events, 0.0 us)
Async XLA Ops:
  0.6 25.3 %collective-permute-start = (bf16[4,256,256]{2,1,0:T(8,128)(2,1)}, bf16[4,256,256]{2,1,0:T(8,128)(2,1)S(1)}, u32[]{:S(2)}, u32[]{:S(2)}) collective-permute-start(bf16[4,256,256]{2,1,0:T(8,128)(2,1)} %bitcast.29), channel_id=1, source_target_pairs={{0,498},{1,499},{2,496},{3,497},{4,502},{5,503},{6,500},{7,501},{8... | collective-permute-start | bytes 1572872 | tf_op jit(solution)/shard_map/ppermute | solution.py:250
  15.0 1.4 %copy-start = (bf16[1,3,4,256,256]{4,3,2,1,0:T(8,128)(2,1)S(1)}, bf16[1,3,4,256,256]{4,3,2,1,0:T(8,128)(2,1)}, u32[]{:S(2)}) copy-start(bf16[1,3,4,256,256]{4,3,2,1,0:T(8,128)(2,1)} %param.12) | copy-start | bytes 4718596
  16.5 1.4 %copy-start.2 = (bf16[1,3,4,256,256]{4,3,2,1,0:T(8,128)(2,1)S(1)}, bf16[1,3,4,256,256]{4,3,2,1,0:T(8,128)(2,1)}, u32[]{:S(2)}) copy-start(bf16[1,3,4,256,256]{4,3,2,1,0:T(8,128)(2,1)} %param.13) | copy-start | bytes 4718596
  17.9 1.0 copy-start.6
  18.9 0.7 copy-start.8
  19.6 6.3 %copy-start.7 = (s32[3,4]{1,0:T(4,128)S(1)}, s32[3,4]{1,0:T(4,128)}, u32[]{:S(2)}) copy-start(s32[3,4]{1,0:T(4,128)} %source.3) | copy-start | bytes 148
  19.6 6.3 %copy-start.9 = (s32[3]{0:T(128)S(1)}, s32[3]{0:T(128)}, u32[]{:S(2)}) copy-start(s32[3]{0:T(128)} %active.3) | copy-start | bytes 40
  28.4 1.0 copy-start.11
  29.4 32.8 %copy-start.13 = (f32[1,256,128]{2,1,0:T(8,128)S(1)}, f32[1,256,128]{2,1,0:T(8,128)}, u32[]{:S(2)}) copy-start(f32[1,256,128]{2,1,0:T(8,128)} %param.16) | copy-start | bytes 393220
  29.4 42.4 %copy-start.3 = (bf16[1,3,4,256,256]{4,3,2,1,0:T(8,128)(2,1)S(1)}, bf16[1,3,4,256,256]{4,3,2,1,0:T(8,128)(2,1)}, u32[]{:S(2)}) copy-start(bf16[1,3,4,256,256]{4,3,2,1,0:T(8,128)(2,1)} %param.13) | copy-start | bytes 4718596
  44.6 27.2 %copy-start.1 = (bf16[1,3,4,256,256]{4,3,2,1,0:T(8,128)(2,1)S(1)}, bf16[1,3,4,256,256]{4,3,2,1,0:T(8,128)(2,1)}, u32[]{:S(2)}) copy-start(bf16[1,3,4,256,256]{4,3,2,1,0:T(8,128)(2,1)} %param.12) | copy-start | bytes 4718596
  45.8 9.6 %collective-permute-start.1 = (bf16[128,256]{1,0:T(8,128)(2,1)S(1)}, bf16[128,256]{1,0:T(8,128)(2,1)S(1)}, u32[]{:S(2)}, u32[]{:S(2)}) collective-permute-start(bf16[128,256]{1,0:T(8,128)(2,1)S(1)} %reduce_sum.12), channel_id=1, source_target_pairs={{0,2},{1,3},{2,0},{3,1},{4,6},{5,7},{6,4},{7,5},{8,10},{9,11},{10,... | collective-permute-start | bytes 196616 | tf_op jit(solution)/shard_map/ppermute | solution.py:257
  56.3 15.5 %all-to-all-start.1 = ((bf16[8,128,256]{2,1,0:T(8,128)(2,1)}), bf16[8,128,256]{2,1,0:T(8,128)(2,1)}, u32[]{:S(2)}, u32[]{:S(2)}) async-start(bf16[8,128,256]{2,1,0:T(8,128)(2,1)} %broadcast_in_dim.12), calls=%async_computation.1 | async-start | bytes 1048576 | tf_op jit(solution)/shard_map/all_to_all | solution.py:260
  71.7 7.1 %copy-start.10 = (s32[1,4]{1,0:T(1,128)S(1)}, s32[1,4]{1,0:T(1,128)}, u32[]{:S(2)}) copy-start(s32[1,4]{1,0:T(1,128)} %kept.3) | copy-start | bytes 52
  74.8 13.5 %all-to-all-start.2 = ((f32[16,1,128]{2,1,0:T(1,128)}), f32[16,1,128]{2,1,0:T(1,128)S(1)}, u32[]{:S(2)}, u32[]{:S(2)}) async-start(f32[16,1,128]{2,1,0:T(1,128)} %bitcast.8), calls=%async_computation.2 | async-start | bytes 16384 | tf_op jit(solution)/shard_map/all_to_all | solution.py:304
  78.9 1.2 %copy-start.12 = (f32[4,256,256]{2,1,0:T(8,128)S(1)}, f32[4,256,256]{2,1,0:T(8,128)}, u32[]{:S(2)}) copy-start(f32[4,256,256]{2,1,0:T(8,128)} %copy-done.11) | copy-start | bytes 3145732
  83.8 0.8 copy-start.4
  88.3 1.0 copy-start.5
  98.7 13.9 %collective-permute-start.2 = (bf16[4,128,256]{2,1,0:T(8,128)(2,1)S(1)}, bf16[4,128,256]{2,1,0:T(8,128)(2,1)S(1)}, u32[]{:S(2)}, u32[]{:S(2)}) collective-permute-start(bf16[4,128,256]{2,1,0:T(8,128)(2,1)S(1)} %get-tuple-element.33), channel_id=1, source_target_pairs={{0,16},{1,17},{2,18},{3,19},{4,20},{5,21},{6,22},{7,23},{8,24},{9,... | collective-permute-start | bytes 786440 | tf_op jit(solution)/shard_map/ppermute | solution.py:250

commit v4 on v3

--- a/solution.py
+++ b/solution.py
@@ -9,6 +9,7 @@
 HIGHEST = lax.Precision.HIGHEST
 NN = (((1,), (0,)), ((), ()))
 NT = (((1,), (1,)), ((), ()))
+AHEAD = 2
 
 SMEM = pl.BlockSpec(memory_space=pltpu.SMEM)
 VMEM = pl.BlockSpec(memory_space=pltpu.VMEM)
@@ -27,7 +28,7 @@
     )(*operands)
 
 
-def prepare_kernel(left_part, inverse, lenv_hbm, renv_hbm, scaled, lenv, renv, sems):
+def prepare_kernel(left_part, inverse, sketch, lenv_hbm, renv_hbm, scaled, tests, lenv, renv, sems):
     copies = []
     for slot in range(lenv.shape[0]):
         rows = pl.ds(slot * 256, 256)
@@ -39,6 +40,7 @@
         copy.start()
     for b in range(left_part.shape[0]):
         scaled[b] = (left_part[b].astype(f32) * inverse[b : b + 1, :]).astype(bf16)
+    tests[...] = sketch[...].T
     for copy in copies:
         copy.wait()
 
@@ -82,32 +84,32 @@
         copy.wait()
 
 
-def second_kernel(source, active, resid, first_ray, lenv, renv, rays, coupling, inner, vector):
+def sum_kernel(chunks, total):
+    summed = chunks[0].astype(f32)
+    for i in range(1, chunks.shape[0]):
+        summed += chunks[i].astype(f32)
+    total[...] = summed.astype(bf16)
+
+
+def second_kernel(source, active, resid, first_ray, lenv, renv, rays, coupling, inner):
     slots, sectors = lenv.shape[:2]
     count = sectors * 256 * 256
-    squares = jnp.zeros((1, 256), f32)
-    for b in range(sectors):
-        piece = resid[b].astype(f32)
-        squares += jnp.sum(piece * piece, axis=0, keepdims=True)
-    mean_square = jnp.sum(squares, axis=1, keepdims=True) / count + 1e-06
-    scale = lax.rsqrt(mean_square)
-    for b in range(sectors):
-        vector[b] = (resid[b].astype(f32) * scale).astype(bf16)
     for slot in range(slots):
         flag = active[slot].astype(f32)
         for b in range(sectors):
             product = jnp.dot(
-                lenv[slot, b], vector[source[slot, b]], preferred_element_type=f32
+                lenv[slot, b], resid[source[slot, b]], preferred_element_type=f32
             )
             inner[b, :, slot * 256 : (slot + 1) * 256] = (product * flag).astype(bf16)
-    dots = jnp.zeros((1, 256), f32)
-    for b in range(sectors):
-        own = jnp.dot(inner[b, :, :256], renv[0, b], preferred_element_type=f32)
-        for slot in range(1, slots):
-            lanes = slice(slot * 256, (slot + 1) * 256)
-            own += jnp.dot(inner[b, :, lanes], renv[slot, b], preferred_element_type=f32)
-        dots += jnp.sum(resid[b].astype(f32) * own, axis=0, keepdims=True)
-    own_ray = jnp.sum(dots, axis=1, keepdims=True) * scale / count
+    dots, squares = jnp.zeros((1, 256), f32), jnp.zeros((1, 256), f32)
+    for b in range(sectors):
+        below = jnp.concatenate([renv[slot, b] for slot in range(slots)], axis=0)
+        own = jnp.dot(inner[b], below, preferred_element_type=f32)
+        piece = resid[b].astype(f32)
+        dots += jnp.sum(piece * own, axis=0, keepdims=True)
+        squares += jnp.sum(piece * piece, axis=0, keepdims=True)
+    mean_square = jnp.sum(squares, axis=1, keepdims=True) / count + 1e-06
+    own_ray = jnp.sum(dots, axis=1, keepdims=True) / count / mean_square
     lane = lax.broadcasted_iota(jnp.int32, rays.shape, 1)
     rays[...] = jnp.where(lane == 0, first_ray[0:1, :], jnp.broadcast_to(own_ray, rays.shape))
     coupling[...] = jnp.broadcast_to(jnp.sqrt(mean_square), coupling.shape)
@@ -132,7 +134,9 @@
     return lax.dot_general(left, right, dims, precision=HIGHEST, preferred_element_type=f32)
 
 
-def quadratic_kernel(kept, first, resid, sketch, images, grams, corr_ff, corr_x, corr_ss):
+def quadratic_kernel(
+    kept, first, resid, sketch, images, gram_ff, gram_x, gram_ss, corr_ff, corr_x, corr_ss
+):
     sectors, size = first.shape[:2]
     cols = sketch.shape[0]
     tests = split(sketch[...])
@@ -146,7 +150,10 @@
         images[b, :cols] = of_first
         images[b, cols:] = of_resid
         both = split(images[b])
-        grams[b] = fine_dot(both, both, NT)
+        gram = fine_dot(both, both, NT)
+        gram_ff[b] = gram[:cols, :cols]
+        gram_x[b] = gram[:cols, cols:] + gram[cols:, :cols]
+        gram_ss[b] = gram[cols:, cols:]
         with_first = fine_dot(both, ground)
         with_resid = dot(both[0], other) + dot(both[1], other)
         corr_ff[b] = with_first[:cols]
@@ -160,20 +167,34 @@
     lane = lax.broadcasted_iota(jnp.int32, packed.shape, 1)
     place = lane % size
     start = lane - place
+    spot = place[0:1, :]
 
     def column(array, k):
         return jnp.take_along_axis(array, start + k, axis=1)
 
-    here = column(packed, 0)
-    for k in range(size):
-        ahead = column(packed, k + 1) if k + 1 < size else None
-        inverse = 1.0 / here[k : k + 1, :]
-        pivot_row = jnp.where(place[k : k + 1, :] == k, 1.0, packed[k : k + 1, :]) * inverse
-        packed = jnp.where(place == k, 0.0, packed) - here * pivot_row
-        packed = jnp.where(row == k, pivot_row, packed)
-        if ahead is not None:
-            factor = here[k + 1 : k + 2, :] * inverse
-            here = jnp.where(row == k, factor, ahead - here * factor)
+    queue = [(column(packed, k), column(packed, k + 1)) for k in range(0, 2 * AHEAD, 2)]
+    for k in range(0, size, 2):
+        left, right = queue.pop(0)
+        if k + 2 * AHEAD < size:
+            queue.append((column(packed, k + 2 * AHEAD), column(packed, k + 2 * AHEAD + 1)))
+        top, cross, low = left[k : k + 1, :], left[k + 1 : k + 2, :], right[k + 1 : k + 2, :]
+        scale = 1.0 / (top * low - cross * cross)
+        top, cross, low = top * scale, cross * scale, low * scale
+        upper = jnp.where(spot == k, 1.0, jnp.where(spot == k + 1, 0.0, packed[k : k + 1, :]))
+        lower = jnp.where(spot == k, 0.0, jnp.where(spot == k + 1, 1.0, packed[k + 1 : k + 2, :]))
+        upper, lower = low * upper - cross * lower, top * lower - cross * upper
+        packed = jnp.where((place == k) | (place == k + 1), 0.0, packed)
+        packed = packed - left * upper - right * lower
+        packed = jnp.where(row == k, upper, jnp.where(row == k + 1, lower, packed))
+        for place_in_queue, pair in enumerate(queue):
+            news = []
+            for side, old in enumerate(pair):
+                j = k + 2 * place_in_queue + 2 + side
+                first, second = left[j : j + 1, :], right[j : j + 1, :]
+                first, second = low * first - cross * second, top * second - cross * first
+                new = old - left * first - right * second
+                news.append(jnp.where(row == k, first, jnp.where(row == k + 1, second, new)))
+            queue[place_in_queue] = tuple(news)
     return packed
 
 
@@ -207,7 +228,8 @@
 
 
 def solve_kernel(
-    kept, rays, coupling, images, grams, corr_ff, corr_x, corr_ss, right, right_low, image
+    kept, rays, coupling, images, gram_ff, gram_x, gram_ss, corr_ff, corr_x, corr_ss,
+    right, right_low, image,
 ):
     sectors, size = corr_x.shape[0], corr_x.shape[2]
     cols = corr_x.shape[1]
@@ -224,8 +246,7 @@
     gram = []
     for b in range(sectors):
         empty = jnp.where((row == lane) & (row >= kept[0, b]), 1.0, 0.0)
-        mixed = grams[b, :cols, cols:] + grams[b, cols:, :cols]
-        own = ff * grams[b, :cols, :cols] + fs * mixed + ss * grams[b, cols:, cols:]
+        own = ff * gram_ff[b] + fs * gram_x[b] + ss * gram_ss[b]
         gram.append(own * (1.0 / (size * size)) + empty)
     gram = invert(gram)
     for b in range(sectors):
@@ -240,12 +261,12 @@
     return [[x * 4 + z * 2 + c for x in range(4) for c in range(2)] for z in range(2)]
 
 
-def across_seg(array, by):
+def across_seg(array, by, swap):
     segs, ops = lax.axis_size("seg"), lax.axis_size("op")
     pairs = []
     for seg in range(segs):
         for op in range(ops):
-            other = op if 0 <= seg + by < segs else op ^ 2
+            other = op ^ 2 if swap and not 0 <= seg + by < segs else op
             pairs.append((seg * ops + op, (seg + by) % segs * ops + other))
     return lax.ppermute(array, ("seg", "op"), pairs)
 
@@ -253,7 +274,9 @@
 def sum_over_op(part):
     chunks = part.reshape(8, 128, 256)
     chunks = lax.all_to_all(chunks, "op", 0, 0, axis_index_groups=plane_groups(), tiled=True)
-    own = jnp.sum(chunks.astype(f32), axis=0).astype(bf16)
+    (own,) = call(
+        sum_kernel, (chunks,), [VMEM], [((128, 256), bf16)], [VMEM], flops=1_000_000, moved=600_000
+    )
     other = lax.ppermute(own, "op", [(i, i ^ 2) for i in range(16)])
     both = (own.astype(f32) + other.astype(f32)).astype(bf16)
     spread = jnp.broadcast_to(both[None], (8, 128, 256))
@@ -267,14 +290,13 @@
     lenv, renv = left_env[0], right_env[0]
     slots, sectors = lenv.shape[:2]
     whole, cols = (sectors, 256, 256), sketch.shape[2]
-    neighbour = across_seg(right_part[0], -1)
-    tests = sketch[0].T
-    scaled, lenv_near, renv_near = call(
+    neighbour = across_seg(right_part, -1, False)[0]
+    scaled, tests, lenv_near, renv_near = call(
         prepare_kernel,
-        (left_part[0], inverse_values[0], lenv, renv),
-        [VMEM, VMEM, HBM, HBM],
-        [(whole, bf16), (lenv.shape, bf16), ((sectors, slots * 256, 256), bf16)],
-        [VMEM] * 3,
+        (left_part[0], inverse_values[0], sketch[0], lenv, renv),
+        [VMEM] * 3 + [HBM] * 2,
+        [(whole, bf16), ((cols, 256), f32), (lenv.shape, bf16), ((sectors, slots * 256, 256), bf16)],
+        [VMEM] * 4,
         [pltpu.SemaphoreType.DMA((slots, 2))],
         moved=8_000_000,
     )
@@ -298,7 +320,7 @@
         [SMEM, SMEM] + [VMEM] * 4,
         [((16, 128), f32), ((8, 128), f32)],
         [VMEM] * 2,
-        [inner, pltpu.VMEM(whole, bf16)],
+        [inner],
         flops=800_000_000, moved=4_000_000,
     )
     rays = lax.all_to_all(rays, "op", 0, 0, tiled=True)
@@ -306,21 +328,23 @@
         quadratic_kernel,
         (kept, first, resid, tests),
         [SMEM] + [VMEM] * 3,
-        [((sectors, 2 * cols, 256), f32)] * 2 + [((sectors, cols, 256), f32)] * 3,
-        [VMEM] * 5,
+        [((sectors, 2 * cols, 256), f32)]
+        + [((sectors, cols, cols), f32)] * 3
+        + [((sectors, cols, 256), f32)] * 3,
+        [VMEM] * 7,
         flops=1_600_000_000, moved=6_000_000,
     )
     right, right_low, image = call(
         solve_kernel,
         (kept, rays, coupling) + tuple(quadratic),
-        [SMEM] + [VMEM] * 7,
+        [SMEM] + [VMEM] * 9,
         [((sectors, cols, 256), f32), ((sectors, cols, 256), bf16), ((sectors, cols, 256), f32)],
         [VMEM] * 3,
         flops=800_000_000, moved=5_000_000,
     )
-    handed = across_seg(right_low, 1)
+    handed = across_seg(right_low[None], 1, True)
     kept_state = jnp.einsum("bki,bkj->bij", image, right, precision=HIGHEST) / 256
-    return (kept_state.astype(bf16)[None], handed[None])
+    return (kept_state.astype(bf16)[None], handed)
 
 
 def solution(mesh):

time: 114 us -> 107 us (0.939)
  waiting for transfers between devices: 36.9 us -> 18.9 us
  blocking collectives: 15.2 us -> 28.9 us
  Pallas kernels: 18.8 us -> 14.7 us
  starting transfers between devices: 28.2 us -> 30.1 us
  local copies, waits for them, and re-layouts: 10.2 us -> 11.7 us
  other arithmetic: 1.25 us -> 0.02 us
    all_to_all x0 -> x1, blocking collectives: none -> 13.7 us  [sum_over_op(): lax.all_to_all(spread, 'op', 0, 0, axis_index_groups=plane_groups(), tile...]
    all_to_all x1 -> x0, waiting for transfers between devices: 9.5 us -> none  [sum_over_op(): lax.all_to_all(spread, 'op', 0, 0, axis_index_groups=plane_groups(), tile...]
    ppermute x1, waiting for transfers between devices: 7.67 us -> 1.64 us  [sum_over_op(): other = lax.ppermute(own, 'op', [(i, i ^ 2) for i in range(16)])]
    ppermute x1, starting transfers between devices: 1.92 us -> 7.94 us  [sum_over_op(): other = lax.ppermute(own, 'op', [(i, i ^ 2) for i in range(16)])]
    all_to_all x1 -> x0, starting transfers between devices: 5.86 us -> none  [sum_over_op(): lax.all_to_all(spread, 'op', 0, 0, axis_index_groups=plane_groups(), tile...]
    all_to_all x1, starting transfers between devices: 4.13 us -> 8.85 us  [shards(): rays = lax.all_to_all(rays, 'op', 0, 0, tiled=True)]
    pallas_call x5 -> x6, Pallas kernels: 18.8 us -> 14.7 us  [call(): pl.pallas_call(kernel, out_shape=tuple((jax.ShapeDtypeStruct(shape, dtype...]
    ppermute x2, starting transfers between devices: 16.3 us -> 13.3 us  [across_seg(): return lax.ppermute(array, ('seg', 'op'), pairs)]
  transfers between devices with their start and end apart: 5 -> 4, of which waited for: 5 -> 4; matrix products, arithmetic and copies ran while one was open for 2% -> 2% of each run, Pallas kernels for 4% -> 3%
where the time goes in v4:
time: 107 us
  starting transfers between devices  30.1 us (28%)
  blocking collectives  28.9 us (27%)
  waiting for transfers between devices  18.9 us (18%)
  Pallas kernels  14.7 us (14%)
  local copies, waits for them, and re-layouts  11.7 us (11%)
  matrix products  1.85 us (2%)
    all_to_all x1, blocking collectives, sum_over_op(): lax.all_to_all(chunks, 'op', 0, 0, axis_index_groups=plane_groups(), tile...  15.2 us
    pallas_call x6, Pallas kernels, call(): pl.pallas_call(kernel, out_shape=tuple((jax.ShapeDtypeStruct(shape, dtype...  14.7 us
    all_to_all x1, blocking collectives, sum_over_op(): lax.all_to_all(spread, 'op', 0, 0, axis_index_groups=plane_groups(), tile...  13.7 us
    ppermute x2, waiting for transfers between devices, across_seg(): return lax.ppermute(array, ('seg', 'op'), pairs)  13.6 us
    ppermute x2, starting transfers between devices, across_seg(): return lax.ppermute(array, ('seg', 'op'), pairs)  13.3 us
    unnamed x33, local copies, waits for them, and re-layouts  11.7 us
    all_to_all x1, starting transfers between devices, shards(): rays = lax.all_to_all(rays, 'op', 0, 0, tiled=True)  8.85 us
    ppermute x1, starting transfers between devices, sum_over_op(): other = lax.ppermute(own, 'op', [(i, i ^ 2) for i in range(16)])  7.94 us
  transfers between devices with their start and end apart: 4, of which 4 were waited for; matrix products, arithmetic and copies ran while one was open for 2% of the time, Pallas kernels for 3%

profile of v4, /device:TPU:1, one launch (start us, length us, event | category | flops | bytes accessed | tf_op | source)
XLA Modules:
  0.0 106.9 jit_solution(4485657355326682076)
XLA Ops:
  0.6 11.4 %collective-permute-start = (bf16[1,4,256,256]{3,2,1,0:T(8,128)(2,1)}, bf16[1,4,256,256]{3,2,1,0:T(8,128)(2,1)S(1)}, u32[]{:S(2)}, u32[]{:S(2)}) collective-permute-start(bf16[1,4,256,256]{3,2,1,0:T(8,128)(2,1)} %param.10), channel_id=1, source_target_pairs={{0,496},{1,497},{2,498},{3,499},{4,500},{5,501},{6,502},{7,503},{8... | collective-permute-start | bytes 1572872 | tf_op jit(solution)/shard_map/ppermute | solution.py:271
  12.0 0.0 copy-start
  12.0 1.4 %copy-done = bf16[1,3,4,256,256]{4,3,2,1,0:T(8,128)(2,1)S(1)} copy-done((bf16[1,3,4,256,256]{4,3,2,1,0:T(8,128)(2,1)S(1)}, bf16[1,3,4,256,256]{4,3,2,1,0:T(8,128)(2,1)}, u32[]{:S(2)}) %copy-start) | copy-done | bytes 1572888
  13.4 0.0 copy-start.2
  13.4 1.4 %copy-done.2 = bf16[1,3,4,256,256]{4,3,2,1,0:T(8,128)(2,1)S(1)} copy-done((bf16[1,3,4,256,256]{4,3,2,1,0:T(8,128)(2,1)S(1)}, bf16[1,3,4,256,256]{4,3,2,1,0:T(8,128)(2,1)}, u32[]{:S(2)}) %copy-start.2) | copy-done | bytes 1572888
  14.8 0.0 copy-start.4
  14.8 1.0 copy-done.4
  15.9 0.0 copy-start.9
  15.9 0.9 copy-done.9
  16.8 0.0 copy-start.11
  16.8 0.7 copy-done.11
  17.4 0.0 copy-start.10
  17.4 0.0 copy-start.12
  17.4 0.4 shard_map.104
  17.9 5.0 %collective-permute-done = bf16[1,4,256,256]{3,2,1,0:T(8,128)(2,1)S(1)} collective-permute-done((bf16[1,4,256,256]{3,2,1,0:T(8,128)(2,1)}, bf16[1,4,256,256]{3,2,1,0:T(8,128)(2,1)S(1)}, u32[]{:S(2)}, u32[]{:S(2)}) %collective-permute-start) | collective-permute-done | bytes 524320 | tf_op jit(solution)/shard_map/ppermute | solution.py:271
  22.9 0.0 copy-done.10
  22.9 0.0 copy-done.12
  22.9 2.5 %shard_map.105 = (f32[4,256,256]{2,1,0:T(8,128)S(1)}, bf16[4,256,256]{2,1,0:T(8,128)(2,1)S(1)}, f32[8,128]{1,0:T(8,128)S(1)}) custom-call(s32[3,4]{1,0:T(4,128)S(1)} %copy-done.10, s32[3]{0:T(128)S(1)} %copy-done.12, bf16[4,256,256]{2,1,0:T(8,128)(2,1)S(1)} %get-tuple-element.21.scaled, bf16[4,256,256]{2,1,0:T(8,128)(2,1)S(1)} %bitcast.25, ...), custom_call_target="tpu_custom_call" | custom-call | flops 940000000 | bytes 6000000 | tf_op jit(solution)/shard_map/pallas_call | solution.py:20
  25.4 0.0 copy-start.14
  25.4 1.0 copy-done.14
  26.4 0.0 copy-start.1
  26.4 0.0 copy-start.3
  26.4 15.2 %all_to_all.21.chunks = bf16[8,128,256]{2,1,0:T(8,128)(2,1)S(1)} all-to-all(bf16[8,128,256]{2,1,0:T(8,128)(2,1)S(1)} %bitcast.23), channel_id=1, replica_groups={{0,1,4,5,8,9,12,13},{2,3,6,7,10,11,14,15},{16,17,20,21,24,25,28,29},{18..., dimensions={0} | all-to-all | bytes 1048576 | tf_op jit(solution)/shard_map/all_to_all | solution.py:276
  41.6 0.1 shard_map.106
  41.7 7.9 %collective-permute-start.1 = (bf16[128,256]{1,0:T(8,128)(2,1)S(1)}, bf16[128,256]{1,0:T(8,128)(2,1)S(1)}, u32[]{:S(2)}, u32[]{:S(2)}) collective-permute-start(bf16[128,256]{1,0:T(8,128)(2,1)S(1)} %shard_map.106), channel_id=1, source_target_pairs={{0,2},{1,3},{2,0},{3,1},{4,6},{5,7},{6,4},{7,5},{8,10},{9,11},{10,... | collective-permute-start | bytes 196616 | tf_op jit(solution)/shard_map/ppermute | solution.py:280
  49.6 1.6 %collective-permute-done.1 = bf16[128,256]{1,0:T(8,128)(2,1)S(1)} collective-permute-done((bf16[128,256]{1,0:T(8,128)(2,1)S(1)}, bf16[128,256]{1,0:T(8,128)(2,1)S(1)}, u32[]{:S(2)}, u32[]{:S(2)}) %collective-permute-start.1) | collective-permute-done | bytes 65568 | tf_op jit(solution)/shard_map/ppermute | solution.py:280
  51.4 13.7 %all_to_all.22 = bf16[8,128,256]{2,1,0:T(8,128)(2,1)S(1)} all-to-all(bf16[8,128,256]{2,1,0:T(8,128)(2,1)S(1)} %broadcast_in_dim.12), channel_id=1, replica_groups={{0,1,4,5,8,9,12,13},{2,3,6,7,10,11,14,15},{16,17,20,21,24,25,28,29},{18..., dimensions={0} | all-to-all | bytes 1048576 | tf_op jit(solution)/shard_map/all_to_all | solution.py:283
  65.0 0.0 copy-done.1
  65.0 0.0 copy-done.3
  65.0 0.0 copy-start.13
  65.0 2.3 %shard_map.107 = (f32[16,128]{1,0:T(8,128)}, f32[8,128]{1,0:T(8,128)S(1)}) custom-call(s32[3,4]{1,0:T(4,128)S(1)} %copy-done.10, s32[3]{0:T(128)S(1)} %copy-done.12, bf16[4,256,256]{2,1,0:T(8,128)(2,1)S(1)} %bitcast.21, f32[8,128]{1,0:T(8,128)S(1)} %get-tuple-element.25.first_ray, bf16[3,4,256,256]{3,2,1,0:T(8,128)(2,1)S(1)} %bitcast.18, ...), custom_call_target="tpu_custom_call" | custom-call | flops 800000000 | bytes 4000000 | tf_op jit(solution)/shard_map/pallas_call | solution.py:20
  67.3 8.8 %all-to-all-start.2 = ((f32[16,1,128]{2,1,0:T(1,128)}), f32[16,1,128]{2,1,0:T(1,128)S(1)}, u32[]{:S(2)}, u32[]{:S(2)}) async-start(f32[16,1,128]{2,1,0:T(1,128)} %bitcast.9), calls=%async_computation.2 | async-start | bytes 16384 | tf_op jit(solution)/shard_map/all_to_all | solution.py:326
  76.1 0.0 copy-done.13
  76.2 0.0 copy-start.15
  76.2 1.2 %copy-done.15 = f32[4,256,256]{2,1,0:T(8,128)S(1)} copy-done((f32[4,256,256]{2,1,0:T(8,128)S(1)}, f32[4,256,256]{2,1,0:T(8,128)}, u32[]{:S(2)}) %copy-start.15) | copy-done | bytes 1048600
  77.4 3.1 %shard_map.108 = (f32[4,256,256]{2,1,0:T(8,128)S(1)}, f32[4,128,128]{2,1,0:T(8,128)S(1)}, f32[4,128,128]{2,1,0:T(8,128)S(1)}, f32[4,128,128]{2,1,0:T(8,128)S(1)}...) custom-call(s32[1,4]{1,0:T(1,128)S(1)} %copy-done.13, ...), custom_call_target="tpu_custom_call" | custom-call | flops 1600000000 | bytes 6000000 | tf_op jit(solution)/shard_map/pallas_call | solution.py:20
  80.5 0.0 copy-start.5
  80.5 0.7 copy-done.5
  81.2 0.0 copy-start.7
  81.2 0.7 copy-done.7
  81.9 3.6 %all-to-all-done.2 = f32[16,1,128]{2,1,0:T(1,128)S(1)} async-done(((f32[16,1,128]{2,1,0:T(1,128)}), f32[16,1,128]{2,1,0:T(1,128)S(1)}, u32[]{:S(2)}, u32[]{:S(2)}) %all-to-all-start.2) | async-done | bytes 8224 | tf_op jit(solution)/shard_map/all_to_all | solution.py:326
  85.5 0.0 copy-start.6
  85.5 0.9 copy-done.6
  86.5 0.0 copy-start.8
  86.5 0.9 copy-done.8
  87.4 6.4 %shard_map.109 = (f32[4,128,256]{2,1,0:T(8,128)S(1)}, bf16[4,128,256]{2,1,0:T(8,128)(2,1)S(1)}, f32[4,128,256]{2,1,0:T(8,128)S(1)}) custom-call(s32[1,4]{1,0:T(1,128)S(1)} %copy-done.13, f32[16,128]{1,0:T(8,128)S(1)} %bitcast.27, f32[8,128]{1,0:T(8,128)S(1)} %get-tuple-element.27.coupling, f32[4,256,256]{2,1,0:T(8,128)S(1)} %get-tuple-element.30.images, ...), custom_call_target="tpu_custom_call" | custom-call | flops 800000000 | bytes 5000000 | tf_op jit(solution)/shard_map/pallas_call | solution.py:20
  93.8 1.9 %collective-permute-start.2 = (bf16[1,4,128,256]{3,2,1,0:T(8,128)(2,1)S(1)}, bf16[1,4,128,256]{3,2,1,0:T(8,128)(2,1)S(1)}, u32[]{:S(2)}, u32[]{:S(2)}) collective-permute-start(bf16[1,4,128,256]{3,2,1,0:T(8,128)(2,1)S(1)} %bitcast.29), channel_id=1, source_target_pairs={{0,16},{1,17},{2,18},{3,19},{4,20},{5,21},{6,22},{7,23},{8,24},{9,... | collective-permute-start | bytes 786440 | tf_op jit(solution)/shard_map/ppermute | solution.py:271
  95.7 1.8 %fusion.1 = bf16[1,4,256,256]{3,2,1,0:T(8,128)(2,1)} fusion(f32[4,128,256]{2,1,0:T(8,128)S(1)} %get-tuple-element.37, f32[4,128,256]{2,1,0:T(8,128)S(1)} %get-tuple-element.38), kind=kOutput, calls=%fused_computation.2 | convolution fusion | flops 403177472 | bytes 1572864 | tf_op jit(solution)/shard_map/bki,bkj->bij/dot_general | solution.py:346
  97.6 8.6 %collective-permute-done.2 = bf16[1,4,128,256]{3,2,1,0:T(8,128)(2,1)S(1)} collective-permute-done((bf16[1,4,128,256]{3,2,1,0:T(8,128)(2,1)S(1)}, bf16[1,4,128,256]{3,2,1,0:T(8,128)(2,1)S(1)}, u32[]{:S(2)}, u32[]{:S(2)}) %collective-permute-start.2) | collective-permute-done | bytes 262176 | tf_op jit(solution)/shard_map/ppermute | solution.py:271
  106.2 0.7 copy.16
  (2 shorter events, 0.1 us)
Async XLA Ops:
  0.6 22.2 %collective-permute-start = (bf16[1,4,256,256]{3,2,1,0:T(8,128)(2,1)}, bf16[1,4,256,256]{3,2,1,0:T(8,128)(2,1)S(1)}, u32[]{:S(2)}, u32[]{:S(2)}) collective-permute-start(bf16[1,4,256,256]{3,2,1,0:T(8,128)(2,1)} %param.10), channel_id=1, source_target_pairs={{0,496},{1,497},{2,498},{3,499},{4,500},{5,501},{6,502},{7,503},{8... | collective-permute-start | bytes 1572872 | tf_op jit(solution)/shard_map/ppermute | solution.py:271
  12.0 1.4 %copy-start = (bf16[1,3,4,256,256]{4,3,2,1,0:T(8,128)(2,1)S(1)}, bf16[1,3,4,256,256]{4,3,2,1,0:T(8,128)(2,1)}, u32[]{:S(2)}) copy-start(bf16[1,3,4,256,256]{4,3,2,1,0:T(8,128)(2,1)} %param.12) | copy-start | bytes 4718596
  13.4 1.4 %copy-start.2 = (bf16[1,3,4,256,256]{4,3,2,1,0:T(8,128)(2,1)S(1)}, bf16[1,3,4,256,256]{4,3,2,1,0:T(8,128)(2,1)}, u32[]{:S(2)}) copy-start(bf16[1,3,4,256,256]{4,3,2,1,0:T(8,128)(2,1)} %param.13) | copy-start | bytes 4718596
  14.8 1.0 copy-start.4
  15.9 0.9 copy-start.9
  16.8 0.7 copy-start.11
  17.4 5.4 %copy-start.10 = (s32[3,4]{1,0:T(4,128)S(1)}, s32[3,4]{1,0:T(4,128)}, u32[]{:S(2)}) copy-start(s32[3,4]{1,0:T(4,128)} %source.3) | copy-start | bytes 148
  17.4 5.4 %copy-start.12 = (s32[3]{0:T(128)S(1)}, s32[3]{0:T(128)}, u32[]{:S(2)}) copy-start(s32[3]{0:T(128)} %active.3) | copy-start | bytes 40
  25.4 1.0 copy-start.14
  26.4 38.7 %copy-start.1 = (bf16[1,3,4,256,256]{4,3,2,1,0:T(8,128)(2,1)S(1)}, bf16[1,3,4,256,256]{4,3,2,1,0:T(8,128)(2,1)}, u32[]{:S(2)}) copy-start(bf16[1,3,4,256,256]{4,3,2,1,0:T(8,128)(2,1)} %param.12) | copy-start | bytes 4718596
  26.4 38.7 %copy-start.3 = (bf16[1,3,4,256,256]{4,3,2,1,0:T(8,128)(2,1)S(1)}, bf16[1,3,4,256,256]{4,3,2,1,0:T(8,128)(2,1)}, u32[]{:S(2)}) copy-start(bf16[1,3,4,256,256]{4,3,2,1,0:T(8,128)(2,1)} %param.13) | copy-start | bytes 4718596
  41.7 9.6 %collective-permute-start.1 = (bf16[128,256]{1,0:T(8,128)(2,1)S(1)}, bf16[128,256]{1,0:T(8,128)(2,1)S(1)}, u32[]{:S(2)}, u32[]{:S(2)}) collective-permute-start(bf16[128,256]{1,0:T(8,128)(2,1)S(1)} %shard_map.106), channel_id=1, source_target_pairs={{0,2},{1,3},{2,0},{3,1},{4,6},{5,7},{6,4},{7,5},{8,10},{9,11},{10,... | collective-permute-start | bytes 196616 | tf_op jit(solution)/shard_map/ppermute | solution.py:280
  65.0 11.1 %copy-start.13 = (s32[1,4]{1,0:T(1,128)S(1)}, s32[1,4]{1,0:T(1,128)}, u32[]{:S(2)}) copy-start(s32[1,4]{1,0:T(1,128)} %kept.3) | copy-start | bytes 52
  67.3 18.2 %all-to-all-start.2 = ((f32[16,1,128]{2,1,0:T(1,128)}), f32[16,1,128]{2,1,0:T(1,128)S(1)}, u32[]{:S(2)}, u32[]{:S(2)}) async-start(f32[16,1,128]{2,1,0:T(1,128)} %bitcast.9), calls=%async_computation.2 | async-start | bytes 16384 | tf_op jit(solution)/shard_map/all_to_all | solution.py:326
  76.2 1.2 %copy-start.15 = (f32[4,256,256]{2,1,0:T(8,128)S(1)}, f32[4,256,256]{2,1,0:T(8,128)}, u32[]{:S(2)}) copy-start(f32[4,256,256]{2,1,0:T(8,128)} %copy-done.14) | copy-start | bytes 3145732
  80.5 0.7 copy-start.5
  81.2 0.7 copy-start.7
  85.5 1.0 copy-start.6
  86.5 0.9 copy-start.8
  93.8 12.4 %collective-permute-start.2 = (bf16[1,4,128,256]{3,2,1,0:T(8,128)(2,1)S(1)}, bf16[1,4,128,256]{3,2,1,0:T(8,128)(2,1)S(1)}, u32[]{:S(2)}, u32[]{:S(2)}) collective-permute-start(bf16[1,4,128,256]{3,2,1,0:T(8,128)(2,1)S(1)} %bitcast.29), channel_id=1, source_target_pairs={{0,16},{1,17},{2,18},{3,19},{4,20},{5,21},{6,22},{7,23},{8,24},{9,... | collective-permute-start | bytes 786440 | tf_op jit(solution)/shard_map/ppermute | solution.py:271

commit v5 on v4

--- a/solution.py
+++ b/solution.py
@@ -132,33 +132,6 @@
 
 def exact_dot(left, right, dims=NN):
     return lax.dot_general(left, right, dims, precision=HIGHEST, preferred_element_type=f32)
-
-
-def quadratic_kernel(
-    kept, first, resid, sketch, images, gram_ff, gram_x, gram_ss, corr_ff, corr_x, corr_ss
-):
-    sectors, size = first.shape[:2]
-    cols = sketch.shape[0]
-    tests = split(sketch[...])
-    row = lax.broadcasted_iota(jnp.int32, (cols, size), 0)
-    for b in range(sectors):
-        wide = row < kept[0, b]
-        other = resid[b]
-        ground = split(first[b])
-        of_first = jnp.where(wide, fine_dot(tests, ground, NT), 0.0)
-        of_resid = jnp.where(wide, dot(tests[0], other, NT) + dot(tests[1], other, NT), 0.0)
-        images[b, :cols] = of_first
-        images[b, cols:] = of_resid
-        both = split(images[b])
-        gram = fine_dot(both, both, NT)
-        gram_ff[b] = gram[:cols, :cols]
-        gram_x[b] = gram[:cols, cols:] + gram[cols:, :cols]
-        gram_ss[b] = gram[cols:, cols:]
-        with_first = fine_dot(both, ground)
-        with_resid = dot(both[0], other) + dot(both[1], other)
-        corr_ff[b] = with_first[:cols]
-        corr_x[b] = with_first[cols:] + with_resid[:cols]
-        corr_ss[b] = with_resid[cols:]
 
 
 def invert_blocks(packed):
@@ -227,34 +200,34 @@
     return gram
 
 
-def solve_kernel(
-    kept, rays, coupling, images, gram_ff, gram_x, gram_ss, corr_ff, corr_x, corr_ss,
-    right, right_low, image,
-):
-    sectors, size = corr_x.shape[0], corr_x.shape[2]
-    cols = corr_x.shape[1]
+def truncate_kernel(kept, rays, coupling, first, resid, sketch, right, right_low, image):
+    sectors, size = first.shape[:2]
+    cols = sketch.shape[0]
     sums = jnp.sum(rays[...], axis=0, keepdims=True)
     ray_first, ray_second = sums[:, 0:1], sums[:, 1:2]
     between = coupling[0:1, 0:1]
     half = 0.5 * (ray_second - ray_first)
     weight = half + jnp.sqrt(half * half + between * between)
     length = lax.rsqrt(weight * weight + between * between)
-    of_first, of_resid = weight * length, -length
-    ff, fs, ss = of_first * of_first, of_first * of_resid, of_resid * of_resid
+    of_first, of_resid = weight * length, length
+    tests = split(sketch[...])
     row = lax.broadcasted_iota(jnp.int32, (cols, cols), 0)
     lane = lax.broadcasted_iota(jnp.int32, (cols, cols), 1)
-    gram = []
-    for b in range(sectors):
+    wide_row = lax.broadcasted_iota(jnp.int32, (cols, size), 0)
+    gram, correlation = [], []
+    for b in range(sectors):
+        ground = split(of_first * first[b] - of_resid * resid[b].astype(f32))
+        own = jnp.where(wide_row < kept[0, b], fine_dot(tests, ground, NT), 0.0)
+        image[b] = own
+        own = split(own)
         empty = jnp.where((row == lane) & (row >= kept[0, b]), 1.0, 0.0)
-        own = ff * gram_ff[b] + fs * gram_x[b] + ss * gram_ss[b]
-        gram.append(own * (1.0 / (size * size)) + empty)
+        gram.append(fine_dot(own, own, NT) * (1.0 / (size * size)) + empty)
+        correlation.append(fine_dot(own, ground))
     gram = invert(gram)
     for b in range(sectors):
-        correlation = ff * corr_ff[b] + fs * corr_x[b] + ss * corr_ss[b]
-        own = exact_dot(gram[b], correlation) * (1.0 / size)
+        own = exact_dot(gram[b], correlation[b]) * (1.0 / size)
         right[b] = own
         right_low[b] = own.astype(bf16)
-        image[b] = of_first * images[b, :cols] + of_resid * images[b, cols:]
 
 
 def plane_groups():
@@ -324,23 +297,13 @@
         flops=800_000_000, moved=4_000_000,
     )
     rays = lax.all_to_all(rays, "op", 0, 0, tiled=True)
-    quadratic = call(
-        quadratic_kernel,
-        (kept, first, resid, tests),
-        [SMEM] + [VMEM] * 3,
-        [((sectors, 2 * cols, 256), f32)]
-        + [((sectors, cols, cols), f32)] * 3
-        + [((sectors, cols, 256), f32)] * 3,
-        [VMEM] * 7,
-        flops=1_600_000_000, moved=6_000_000,
-    )
     right, right_low, image = call(
-        solve_kernel,
-        (kept, rays, coupling) + tuple(quadratic),
-        [SMEM] + [VMEM] * 9,
+        truncate_kernel,
+        (kept, rays, coupling, first, resid, tests),
+        [SMEM] + [VMEM] * 5,
         [((sectors, cols, 256), f32), ((sectors, cols, 256), bf16), ((sectors, cols, 256), f32)],
         [VMEM] * 3,
-        flops=800_000_000, moved=5_000_000,
+        flops=1_200_000_000, moved=4_000_000,
     )
     handed = across_seg(right_low[None], 1, True)
     kept_state = jnp.einsum("bki,bkj->bij", image, right, precision=HIGHEST) / 256

time: 107 us -> 105 us (0.981)
  blocking collectives: 28.9 us -> 47 us
  starting transfers between devices: 30.1 us -> 21.2 us
  local copies, waits for them, and re-layouts: 11.7 us -> 6.2 us
  waiting for transfers between devices: 18.9 us -> 15.3 us
  Pallas kernels: 14.7 us -> 12.2 us
    all_to_all x0 -> x1, blocking collectives: none -> 18 us  [shards(): rays = lax.all_to_all(rays, 'op', 0, 0, tiled=True)]
    all_to_all x1 -> x0, starting transfers between devices: 8.85 us -> none  [shards(): rays = lax.all_to_all(rays, 'op', 0, 0, tiled=True)]
    unnamed x33 -> x21, local copies, waits for them, and re-layouts: 11.7 us -> 6.17 us
    all_to_all x1 -> x0, waiting for transfers between devices: 3.6 us -> none  [shards(): rays = lax.all_to_all(rays, 'op', 0, 0, tiled=True)]
    pallas_call x6 -> x5, Pallas kernels: 14.7 us -> 12.2 us  [call(): pl.pallas_call(kernel, out_shape=tuple((jax.ShapeDtypeStruct(shape, dtype...]
  transfers between devices with their start and end apart: 4 -> 3, of which waited for: 4 -> 3; matrix products, arithmetic and copies ran while one was open for 2% -> 2% of each run, Pallas kernels for 3% -> 0%
where the time goes in v5:
time: 105 us; the launch traced here: 104 us
  blocking collectives  47 us (45%)
  starting transfers between devices  21.2 us (20%)
  waiting for transfers between devices  15.3 us (15%)
  Pallas kernels  12.2 us (12%)
  local copies, waits for them, and re-layouts  6.2 us (6%)
  matrix products  1.83 us (2%)
    all_to_all x1, blocking collectives, shards(): rays = lax.all_to_all(rays, 'op', 0, 0, tiled=True)  18 us
    all_to_all x1, blocking collectives, sum_over_op(): lax.all_to_all(chunks, 'op', 0, 0, axis_index_groups=plane_groups(), tile...  15.3 us
    all_to_all x1, blocking collectives, sum_over_op(): lax.all_to_all(spread, 'op', 0, 0, axis_index_groups=plane_groups(), tile...  13.7 us
    ppermute x2, waiting for transfers between devices, across_seg(): return lax.ppermute(array, ('seg', 'op'), pairs)  13.6 us
    ppermute x2, starting transfers between devices, across_seg(): return lax.ppermute(array, ('seg', 'op'), pairs)  13.3 us
    pallas_call x5, Pallas kernels, call(): pl.pallas_call(kernel, out_shape=tuple((jax.ShapeDtypeStruct(shape, dtype...  12.2 us
    ppermute x1, starting transfers between devices, sum_over_op(): other = lax.ppermute(own, 'op', [(i, i ^ 2) for i in range(16)])  7.94 us
    unnamed x21, local copies, waits for them, and re-layouts  6.17 us
  transfers between devices with their start and end apart: 3, of which 3 were waited for; matrix products, arithmetic and copies ran while one was open for 2% of the time, Pallas kernels for 0%

profile of v5, /device:TPU:1, one launch (start us, length us, event | category | flops | bytes accessed | tf_op | source)
XLA Modules:
  0.0 104.4 jit_solution(15543861851059516325)
XLA Ops:
  0.6 11.4 %collective-permute-start = (bf16[1,4,256,256]{3,2,1,0:T(8,128)(2,1)}, bf16[1,4,256,256]{3,2,1,0:T(8,128)(2,1)S(1)}, u32[]{:S(2)}, u32[]{:S(2)}) collective-permute-start(bf16[1,4,256,256]{3,2,1,0:T(8,128)(2,1)} %param.10), channel_id=1, source_target_pairs={{0,496},{1,497},{2,498},{3,499},{4,500},{5,501},{6,502},{7,503},{8... | collective-permute-start | bytes 1572872 | tf_op jit(solution)/shard_map/ppermute | solution.py:244
  12.0 0.0 copy-start
  12.0 1.4 %copy-done = bf16[1,3,4,256,256]{4,3,2,1,0:T(8,128)(2,1)S(1)} copy-done((bf16[1,3,4,256,256]{4,3,2,1,0:T(8,128)(2,1)S(1)}, bf16[1,3,4,256,256]{4,3,2,1,0:T(8,128)(2,1)}, u32[]{:S(2)}) %copy-start) | copy-done | bytes 1572888
  13.4 0.0 copy-start.2
  13.4 1.4 %copy-done.2 = bf16[1,3,4,256,256]{4,3,2,1,0:T(8,128)(2,1)S(1)} copy-done((bf16[1,3,4,256,256]{4,3,2,1,0:T(8,128)(2,1)S(1)}, bf16[1,3,4,256,256]{4,3,2,1,0:T(8,128)(2,1)}, u32[]{:S(2)}) %copy-start.2) | copy-done | bytes 1572888
  14.8 0.0 copy-start.4
  14.8 1.0 copy-done.4
  15.9 0.0 copy-start.5
  15.9 0.9 copy-done.5
  16.8 0.0 copy-start.7
  16.8 0.7 copy-done.7
  17.4 0.0 copy-start.6
  17.4 0.0 copy-start.8
  17.4 0.4 shard_map.104
  17.9 5.0 %collective-permute-done = bf16[1,4,256,256]{3,2,1,0:T(8,128)(2,1)S(1)} collective-permute-done((bf16[1,4,256,256]{3,2,1,0:T(8,128)(2,1)}, bf16[1,4,256,256]{3,2,1,0:T(8,128)(2,1)S(1)}, u32[]{:S(2)}, u32[]{:S(2)}) %collective-permute-start) | collective-permute-done | bytes 524320 | tf_op jit(solution)/shard_map/ppermute | solution.py:244
  22.9 0.0 copy-done.6
  22.9 0.0 copy-done.8
  22.9 2.5 %shard_map.105 = (f32[4,256,256]{2,1,0:T(8,128)S(1)}, bf16[4,256,256]{2,1,0:T(8,128)(2,1)S(1)}, f32[8,128]{1,0:T(8,128)S(1)}) custom-call(s32[3,4]{1,0:T(4,128)S(1)} %copy-done.6, s32[3]{0:T(128)S(1)} %copy-done.8, bf16[4,256,256]{2,1,0:T(8,128)(2,1)S(1)} %get-tuple-element.14.scaled, bf16[4,256,256]{2,1,0:T(8,128)(2,1)S(1)} %bitcast.25, ...), custom_call_target="tpu_custom_call" | custom-call | flops 940000000 | bytes 6000000 | tf_op jit(solution)/shard_map/pallas_call | solution.py:20
  25.4 0.0 copy-start.1
  25.4 0.0 copy-start.3
  25.4 15.3 %all_to_all.21.chunks = bf16[8,128,256]{2,1,0:T(8,128)(2,1)S(1)} all-to-all(bf16[8,128,256]{2,1,0:T(8,128)(2,1)S(1)} %bitcast.23), channel_id=1, replica_groups={{0,1,4,5,8,9,12,13},{2,3,6,7,10,11,14,15},{16,17,20,21,24,25,28,29},{18..., dimensions={0} | all-to-all | bytes 1048576 | tf_op jit(solution)/shard_map/all_to_all | solution.py:249
  40.7 0.1 shard_map.106
  40.7 7.9 %collective-permute-start.1 = (bf16[128,256]{1,0:T(8,128)(2,1)S(1)}, bf16[128,256]{1,0:T(8,128)(2,1)S(1)}, u32[]{:S(2)}, u32[]{:S(2)}) collective-permute-start(bf16[128,256]{1,0:T(8,128)(2,1)S(1)} %shard_map.106), channel_id=1, source_target_pairs={{0,2},{1,3},{2,0},{3,1},{4,6},{5,7},{6,4},{7,5},{8,10},{9,11},{10,... | collective-permute-start | bytes 196616 | tf_op jit(solution)/shard_map/ppermute | solution.py:253
  48.7 1.6 %collective-permute-done.1 = bf16[128,256]{1,0:T(8,128)(2,1)S(1)} collective-permute-done((bf16[128,256]{1,0:T(8,128)(2,1)S(1)}, bf16[128,256]{1,0:T(8,128)(2,1)S(1)}, u32[]{:S(2)}, u32[]{:S(2)}) %collective-permute-start.1) | collective-permute-done | bytes 65568 | tf_op jit(solution)/shard_map/ppermute | solution.py:253
  50.4 13.7 %all_to_all.22 = bf16[8,128,256]{2,1,0:T(8,128)(2,1)S(1)} all-to-all(bf16[8,128,256]{2,1,0:T(8,128)(2,1)S(1)} %broadcast_in_dim.12), channel_id=1, replica_groups={{0,1,4,5,8,9,12,13},{2,3,6,7,10,11,14,15},{16,17,20,21,24,25,28,29},{18..., dimensions={0} | all-to-all | bytes 1048576 | tf_op jit(solution)/shard_map/all_to_all | solution.py:256
  64.1 0.0 copy-done.1
  64.1 0.0 copy-done.3
  64.1 0.0 copy-start.9
  64.1 1.7 %shard_map.107 = (f32[16,128]{1,0:T(8,128)S(1)}, f32[8,128]{1,0:T(8,128)S(1)}) custom-call(s32[3,4]{1,0:T(4,128)S(1)} %copy-done.6, s32[3]{0:T(128)S(1)} %copy-done.8, bf16[4,256,256]{2,1,0:T(8,128)(2,1)S(1)} %bitcast.21, f32[8,128]{1,0:T(8,128)S(1)} %get-tuple-element.18.first_ray, bf16[3,4,256,256]{3,2,1,0:T(8,128)(2,1)S(1)} %bitcast.18, ...), custom_call_target="tpu_custom_call" | custom-call | flops 800000000 | bytes 4000000 | tf_op jit(solution)/shard_map/pallas_call | solution.py:20
  65.7 18.0 %all_to_all.23 = f32[16,1,128]{2,1,0:T(1,128)S(1)} all-to-all(f32[16,1,128]{2,1,0:T(1,128)S(1)} %bitcast.28), channel_id=1, replica_groups=mesh['seg'=32,'op'=16] {'op'}, dimensions={0} | all-to-all | bytes 16384 | tf_op jit(solution)/shard_map/all_to_all | solution.py:299
  83.8 0.0 copy-done.9
  83.8 7.5 %shard_map.108 = (f32[4,128,256]{2,1,0:T(8,128)S(1)}, bf16[4,128,256]{2,1,0:T(8,128)(2,1)S(1)}, f32[4,128,256]{2,1,0:T(8,128)S(1)}) custom-call(s32[1,4]{1,0:T(1,128)S(1)} %copy-done.9, f32[16,128]{1,0:T(8,128)S(1)} %bitcast.27, f32[8,128]{1,0:T(8,128)S(1)} %get-tuple-element.20.coupling, f32[4,256,256]{2,1,0:T(8,128)S(1)} %get-tuple-element.21.first, ...), custom_call_target="tpu_custom_call" | custom-call | flops 1200000000 | bytes 4000000 | tf_op jit(solution)/shard_map/pallas_call | solution.py:20
  91.3 1.9 %collective-permute-start.2 = (bf16[1,4,128,256]{3,2,1,0:T(8,128)(2,1)S(1)}, bf16[1,4,128,256]{3,2,1,0:T(8,128)(2,1)S(1)}, u32[]{:S(2)}, u32[]{:S(2)}) collective-permute-start(bf16[1,4,128,256]{3,2,1,0:T(8,128)(2,1)S(1)} %bitcast.30), channel_id=1, source_target_pairs={{0,16},{1,17},{2,18},{3,19},{4,20},{5,21},{6,22},{7,23},{8,24},{9,... | collective-permute-start | bytes 786440 | tf_op jit(solution)/shard_map/ppermute | solution.py:244
  93.2 1.8 %fusion.1 = bf16[1,4,256,256]{3,2,1,0:T(8,128)(2,1)} fusion(f32[4,128,256]{2,1,0:T(8,128)S(1)} %get-tuple-element.23, f32[4,128,256]{2,1,0:T(8,128)S(1)} %get-tuple-element.24), kind=kOutput, calls=%fused_computation.2 | convolution fusion | flops 403177472 | bytes 1572864 | tf_op jit(solution)/shard_map/bki,bkj->bij/dot_general | solution.py:309
  95.0 8.6 %collective-permute-done.2 = bf16[1,4,128,256]{3,2,1,0:T(8,128)(2,1)S(1)} collective-permute-done((bf16[1,4,128,256]{3,2,1,0:T(8,128)(2,1)S(1)}, bf16[1,4,128,256]{3,2,1,0:T(8,128)(2,1)S(1)}, u32[]{:S(2)}, u32[]{:S(2)}) %collective-permute-start.2) | collective-permute-done | bytes 262176 | tf_op jit(solution)/shard_map/ppermute | solution.py:244
  103.7 0.7 copy.16
  (2 shorter events, 0.1 us)
Async XLA Ops:
  0.6 22.2 %collective-permute-start = (bf16[1,4,256,256]{3,2,1,0:T(8,128)(2,1)}, bf16[1,4,256,256]{3,2,1,0:T(8,128)(2,1)S(1)}, u32[]{:S(2)}, u32[]{:S(2)}) collective-permute-start(bf16[1,4,256,256]{3,2,1,0:T(8,128)(2,1)} %param.10), channel_id=1, source_target_pairs={{0,496},{1,497},{2,498},{3,499},{4,500},{5,501},{6,502},{7,503},{8... | collective-permute-start | bytes 1572872 | tf_op jit(solution)/shard_map/ppermute | solution.py:244
  12.0 1.4 %copy-start = (bf16[1,3,4,256,256]{4,3,2,1,0:T(8,128)(2,1)S(1)}, bf16[1,3,4,256,256]{4,3,2,1,0:T(8,128)(2,1)}, u32[]{:S(2)}) copy-start(bf16[1,3,4,256,256]{4,3,2,1,0:T(8,128)(2,1)} %param.12) | copy-start | bytes 4718596
  13.4 1.4 %copy-start.2 = (bf16[1,3,4,256,256]{4,3,2,1,0:T(8,128)(2,1)S(1)}, bf16[1,3,4,256,256]{4,3,2,1,0:T(8,128)(2,1)}, u32[]{:S(2)}) copy-start(bf16[1,3,4,256,256]{4,3,2,1,0:T(8,128)(2,1)} %param.13) | copy-start | bytes 4718596
  14.8 1.0 copy-start.4
  15.9 0.9 copy-start.5
  16.8 0.7 copy-start.7
  17.4 5.4 %copy-start.6 = (s32[3,4]{1,0:T(4,128)S(1)}, s32[3,4]{1,0:T(4,128)}, u32[]{:S(2)}) copy-start(s32[3,4]{1,0:T(4,128)} %source.3) | copy-start | bytes 148
  17.4 5.4 %copy-start.8 = (s32[3]{0:T(128)S(1)}, s32[3]{0:T(128)}, u32[]{:S(2)}) copy-start(s32[3]{0:T(128)} %active.3) | copy-start | bytes 40
  25.4 38.7 %copy-start.1 = (bf16[1,3,4,256,256]{4,3,2,1,0:T(8,128)(2,1)S(1)}, bf16[1,3,4,256,256]{4,3,2,1,0:T(8,128)(2,1)}, u32[]{:S(2)}) copy-start(bf16[1,3,4,256,256]{4,3,2,1,0:T(8,128)(2,1)} %param.12) | copy-start | bytes 4718596
  25.4 38.7 %copy-start.3 = (bf16[1,3,4,256,256]{4,3,2,1,0:T(8,128)(2,1)S(1)}, bf16[1,3,4,256,256]{4,3,2,1,0:T(8,128)(2,1)}, u32[]{:S(2)}) copy-start(bf16[1,3,4,256,256]{4,3,2,1,0:T(8,128)(2,1)} %param.13) | copy-start | bytes 4718596
  40.7 9.6 %collective-permute-start.1 = (bf16[128,256]{1,0:T(8,128)(2,1)S(1)}, bf16[128,256]{1,0:T(8,128)(2,1)S(1)}, u32[]{:S(2)}, u32[]{:S(2)}) collective-permute-start(bf16[128,256]{1,0:T(8,128)(2,1)S(1)} %shard_map.106), channel_id=1, source_target_pairs={{0,2},{1,3},{2,0},{3,1},{4,6},{5,7},{6,4},{7,5},{8,10},{9,11},{10,... | collective-permute-start | bytes 196616 | tf_op jit(solution)/shard_map/ppermute | solution.py:253
  64.1 19.7 %copy-start.9 = (s32[1,4]{1,0:T(1,128)S(1)}, s32[1,4]{1,0:T(1,128)}, u32[]{:S(2)}) copy-start(s32[1,4]{1,0:T(1,128)} %kept.1) | copy-start | bytes 52
  91.3 12.4 %collective-permute-start.2 = (bf16[1,4,128,256]{3,2,1,0:T(8,128)(2,1)S(1)}, bf16[1,4,128,256]{3,2,1,0:T(8,128)(2,1)S(1)}, u32[]{:S(2)}, u32[]{:S(2)}) collective-permute-start(bf16[1,4,128,256]{3,2,1,0:T(8,128)(2,1)S(1)} %bitcast.30), channel_id=1, source_target_pairs={{0,16},{1,17},{2,18},{3,19},{4,20},{5,21},{6,22},{7,23},{8,24},{9,... | collective-permute-start | bytes 786440 | tf_op jit(solution)/shard_map/ppermute | solution.py:244

commit v6 on v5

--- a/solution.py
+++ b/solution.py
@@ -130,10 +130,6 @@
     )
 
 
-def exact_dot(left, right, dims=NN):
-    return lax.dot_general(left, right, dims, precision=HIGHEST, preferred_element_type=f32)
-
-
 def invert_blocks(packed):
     size = packed.shape[0]
     row = lax.broadcasted_iota(jnp.int32, packed.shape, 0)
@@ -152,22 +148,24 @@
             queue.append((column(packed, k + 2 * AHEAD), column(packed, k + 2 * AHEAD + 1)))
         top, cross, low = left[k : k + 1, :], left[k + 1 : k + 2, :], right[k + 1 : k + 2, :]
         scale = 1.0 / (top * low - cross * cross)
-        top, cross, low = top * scale, cross * scale, low * scale
+
+        def eliminate(old, upper, lower):
+            upper, lower = low * upper - cross * lower, top * lower - cross * upper
+            new = old - (left * upper + right * lower) * scale
+            return jnp.where(
+                row == k, upper * scale, jnp.where(row == k + 1, lower * scale, new)
+            )
+
         upper = jnp.where(spot == k, 1.0, jnp.where(spot == k + 1, 0.0, packed[k : k + 1, :]))
         lower = jnp.where(spot == k, 0.0, jnp.where(spot == k + 1, 1.0, packed[k + 1 : k + 2, :]))
-        upper, lower = low * upper - cross * lower, top * lower - cross * upper
-        packed = jnp.where((place == k) | (place == k + 1), 0.0, packed)
-        packed = packed - left * upper - right * lower
-        packed = jnp.where(row == k, upper, jnp.where(row == k + 1, lower, packed))
-        for place_in_queue, pair in enumerate(queue):
-            news = []
-            for side, old in enumerate(pair):
-                j = k + 2 * place_in_queue + 2 + side
-                first, second = left[j : j + 1, :], right[j : j + 1, :]
-                first, second = low * first - cross * second, top * second - cross * first
-                new = old - left * first - right * second
-                news.append(jnp.where(row == k, first, jnp.where(row == k + 1, second, new)))
-            queue[place_in_queue] = tuple(news)
+        rest = jnp.where((place == k) | (place == k + 1), 0.0, packed)
+        packed = eliminate(rest, upper, lower)
+        for i, pair in enumerate(queue):
+            j = k + 2 * i + 2
+            queue[i] = tuple(
+                eliminate(old, left[n : n + 1, :], right[n : n + 1, :])
+                for old, n in zip(pair, (j, j + 1), strict=True)
+            )
     return packed
 
 
@@ -189,14 +187,14 @@
         inverse = jnp.where(same, jnp.concatenate([inverse] * sectors, axis=0), 0.0)
         stacked = jnp.concatenate([g[rows] for g in gram], axis=0)
         stacked = jnp.where(lane // size == p, unit, stacked)
-        panel = exact_dot(inverse, stacked)
+        panel = fine_dot(split(inverse), split(stacked))
         for s in range(sectors):
             own = panel[s * size : (s + 1) * size]
             tiled = jnp.concatenate([own] * (cols // size), axis=0)
             factor = jnp.where((lane // size == p) & (row // size != p), gram[s], 0.0)
             rest = jnp.where(lane // size == p, 0.0, gram[s])
             rest = jnp.where(row // size == p, tiled, rest)
-            gram[s] = rest - exact_dot(factor, tiled)
+            gram[s] = rest - fine_dot(split(factor), split(tiled))
     return gram
 
 
@@ -225,13 +223,18 @@
         correlation.append(fine_dot(own, ground))
     gram = invert(gram)
     for b in range(sectors):
-        own = exact_dot(gram[b], correlation[b]) * (1.0 / size)
+        own = fine_dot(split(gram[b]), split(correlation[b])) * (1.0 / size)
         right[b] = own
         right_low[b] = own.astype(bf16)
 
 
 def plane_groups():
     return [[x * 4 + z * 2 + c for x in range(4) for c in range(2)] for z in range(2)]
+
+
+def upper_half_first():
+    first, second = plane_groups()
+    return [second + first]
 
 
 def across_seg(array, by, swap):
@@ -296,7 +299,7 @@
         [inner],
         flops=800_000_000, moved=4_000_000,
     )
-    rays = lax.all_to_all(rays, "op", 0, 0, tiled=True)
+    rays = lax.all_to_all(rays, "op", 0, 0, axis_index_groups=upper_half_first(), tiled=True)
     right, right_low, image = call(
         truncate_kernel,
         (kept, rays, coupling, first, resid, tests),

time: 105 us -> 103 us (0.981)
  blocking collectives: 47 us -> 42.4 us
  waiting for transfers between devices: 15.3 us -> 19 us
    all_to_all x1, blocking collectives: 18 us -> 13.4 us  [shards(): lax.all_to_all(rays, 'op', 0, 0, axis_index_groups=upper_half_first(), ti...]
    ppermute x2, waiting for transfers between devices: 13.6 us -> 17.3 us  [across_seg(): return lax.ppermute(array, ('seg', 'op'), pairs)]
where the time goes in v6:
time: 103 us; the launch traced here: 102 us
  blocking collectives  42.4 us (41%)
  starting transfers between devices  21.2 us (21%)
  waiting for transfers between devices  19 us (18%)
  Pallas kernels  11.2 us (11%)
  local copies, waits for them, and re-layouts  6.2 us (6%)
  matrix products  1.83 us (2%)
    ppermute x2, waiting for transfers between devices, across_seg(): return lax.ppermute(array, ('seg', 'op'), pairs)  17.3 us
    all_to_all x1, blocking collectives, sum_over_op(): lax.all_to_all(chunks, 'op', 0, 0, axis_index_groups=plane_groups(), tile...  15.3 us
    all_to_all x1, blocking collectives, sum_over_op(): lax.all_to_all(spread, 'op', 0, 0, axis_index_groups=plane_groups(), tile...  13.7 us
    all_to_all x1, blocking collectives, shards(): lax.all_to_all(rays, 'op', 0, 0, axis_index_groups=upper_half_first(), ti...  13.4 us
    ppermute x2, starting transfers between devices, across_seg(): return lax.ppermute(array, ('seg', 'op'), pairs)  13.3 us
    pallas_call x5, Pallas kernels, call(): pl.pallas_call(kernel, out_shape=tuple((jax.ShapeDtypeStruct(shape, dtype...  11.2 us
    ppermute x1, starting transfers between devices, sum_over_op(): other = lax.ppermute(own, 'op', [(i, i ^ 2) for i in range(16)])  7.94 us
    unnamed x21, local copies, waits for them, and re-layouts  6.17 us
  transfers between devices with their start and end apart: 3, of which 3 were waited for; matrix products, arithmetic and copies ran while one was open for 2% of the time, Pallas kernels for 0%

profile of v6, /device:TPU:1, one launch (start us, length us, event | category | flops | bytes accessed | tf_op | source)
XLA Modules:
  0.0 102.5 jit_solution(15372323292004436028)
XLA Ops:
  0.6 11.4 %collective-permute-start = (bf16[1,4,256,256]{3,2,1,0:T(8,128)(2,1)}, bf16[1,4,256,256]{3,2,1,0:T(8,128)(2,1)S(1)}, u32[]{:S(2)}, u32[]{:S(2)}) collective-permute-start(bf16[1,4,256,256]{3,2,1,0:T(8,128)(2,1)} %param.10), channel_id=1, source_target_pairs={{0,496},{1,497},{2,498},{3,499},{4,500},{5,501},{6,502},{7,503},{8... | collective-permute-start | bytes 1572872 | tf_op jit(solution)/shard_map/ppermute | solution.py:247
  12.0 0.0 copy-start
  12.0 1.4 %copy-done = bf16[1,3,4,256,256]{4,3,2,1,0:T(8,128)(2,1)S(1)} copy-done((bf16[1,3,4,256,256]{4,3,2,1,0:T(8,128)(2,1)S(1)}, bf16[1,3,4,256,256]{4,3,2,1,0:T(8,128)(2,1)}, u32[]{:S(2)}) %copy-start) | copy-done | bytes 1572888
  13.4 0.0 copy-start.2
  13.4 1.4 %copy-done.2 = bf16[1,3,4,256,256]{4,3,2,1,0:T(8,128)(2,1)S(1)} copy-done((bf16[1,3,4,256,256]{4,3,2,1,0:T(8,128)(2,1)S(1)}, bf16[1,3,4,256,256]{4,3,2,1,0:T(8,128)(2,1)}, u32[]{:S(2)}) %copy-start.2) | copy-done | bytes 1572888
  14.8 0.0 copy-start.4
  14.8 1.0 %copy-done.4 = bf16[1,4,256,256]{3,2,1,0:T(8,128)(2,1)S(1)} copy-done((bf16[1,4,256,256]{3,2,1,0:T(8,128)(2,1)S(1)}, bf16[1,4,256,256]{3,2,1,0:T(8,128)(2,1)}, u32[]{:S(2)}) %copy-start.4) | copy-done | bytes 524312
  15.9 0.0 copy-start.5
  15.9 0.9 copy-done.5
  16.8 0.0 copy-start.7
  16.8 0.7 copy-done.7
  17.4 0.0 copy-start.6
  17.4 0.0 copy-start.8
  17.4 0.4 shard_map.104
  17.9 5.0 %collective-permute-done = bf16[1,4,256,256]{3,2,1,0:T(8,128)(2,1)S(1)} collective-permute-done((bf16[1,4,256,256]{3,2,1,0:T(8,128)(2,1)}, bf16[1,4,256,256]{3,2,1,0:T(8,128)(2,1)S(1)}, u32[]{:S(2)}, u32[]{:S(2)}) %collective-permute-start) | collective-permute-done | bytes 524320 | tf_op jit(solution)/shard_map/ppermute | solution.py:247
  22.9 0.0 copy-done.6
  22.9 0.0 copy-done.8
  22.9 2.5 %shard_map.105 = (f32[4,256,256]{2,1,0:T(8,128)S(1)}, bf16[4,256,256]{2,1,0:T(8,128)(2,1)S(1)}, f32[8,128]{1,0:T(8,128)S(1)}) custom-call(s32[3,4]{1,0:T(4,128)S(1)} %copy-done.6, s32[3]{0:T(128)S(1)} %copy-done.8, bf16[4,256,256]{2,1,0:T(8,128)(2,1)S(1)} %get-tuple-element.14.scaled, bf16[4,256,256]{2,1,0:T(8,128)(2,1)S(1)} %bitcast.25, ...), custom_call_target="tpu_custom_call" | custom-call | flops 940000000 | bytes 6000000 | tf_op jit(solution)/shard_map/pallas_call | solution.py:20
  25.4 0.0 copy-start.1
  25.4 0.0 copy-start.3
  25.4 15.3 %all_to_all.21.chunks = bf16[8,128,256]{2,1,0:T(8,128)(2,1)S(1)} all-to-all(bf16[8,128,256]{2,1,0:T(8,128)(2,1)S(1)} %bitcast.23), channel_id=1, replica_groups={{0,1,4,5,8,9,12,13},{2,3,6,7,10,11,14,15},{16,17,20,21,24,25,28,29},{18..., dimensions={0} | all-to-all | bytes 1048576 | tf_op jit(solution)/shard_map/all_to_all | solution.py:252
  40.7 0.1 shard_map.106
  40.7 7.9 %collective-permute-start.1 = (bf16[128,256]{1,0:T(8,128)(2,1)S(1)}, bf16[128,256]{1,0:T(8,128)(2,1)S(1)}, u32[]{:S(2)}, u32[]{:S(2)}) collective-permute-start(bf16[128,256]{1,0:T(8,128)(2,1)S(1)} %shard_map.106), channel_id=1, source_target_pairs={{0,2},{1,3},{2,0},{3,1},{4,6},{5,7},{6,4},{7,5},{8,10},{9,11},{10,... | collective-permute-start | bytes 196616 | tf_op jit(solution)/shard_map/ppermute | solution.py:256
  48.7 1.6 %collective-permute-done.1 = bf16[128,256]{1,0:T(8,128)(2,1)S(1)} collective-permute-done((bf16[128,256]{1,0:T(8,128)(2,1)S(1)}, bf16[128,256]{1,0:T(8,128)(2,1)S(1)}, u32[]{:S(2)}, u32[]{:S(2)}) %collective-permute-start.1) | collective-permute-done | bytes 65568 | tf_op jit(solution)/shard_map/ppermute | solution.py:256
  50.4 13.7 %all_to_all.22 = bf16[8,128,256]{2,1,0:T(8,128)(2,1)S(1)} all-to-all(bf16[8,128,256]{2,1,0:T(8,128)(2,1)S(1)} %broadcast_in_dim.12), channel_id=1, replica_groups={{0,1,4,5,8,9,12,13},{2,3,6,7,10,11,14,15},{16,17,20,21,24,25,28,29},{18..., dimensions={0} | all-to-all | bytes 1048576 | tf_op jit(solution)/shard_map/all_to_all | solution.py:259
  64.1 0.0 copy-done.1
  64.1 0.0 copy-done.3
  64.1 0.0 copy-start.9
  64.1 1.7 %shard_map.107 = (f32[16,128]{1,0:T(8,128)S(1)}, f32[8,128]{1,0:T(8,128)S(1)}) custom-call(s32[3,4]{1,0:T(4,128)S(1)} %copy-done.6, s32[3]{0:T(128)S(1)} %copy-done.8, bf16[4,256,256]{2,1,0:T(8,128)(2,1)S(1)} %bitcast.21, f32[8,128]{1,0:T(8,128)S(1)} %get-tuple-element.18.first_ray, bf16[3,4,256,256]{3,2,1,0:T(8,128)(2,1)S(1)} %bitcast.18, ...), custom_call_target="tpu_custom_call" | custom-call | flops 800000000 | bytes 4000000 | tf_op jit(solution)/shard_map/pallas_call | solution.py:20
  65.7 13.4 %all_to_all.23 = f32[16,1,128]{2,1,0:T(1,128)S(1)} all-to-all(f32[16,1,128]{2,1,0:T(1,128)S(1)} %bitcast.28), channel_id=1, replica_groups={{2,3,6,7,10,11,14,15,0,1,4,5,8,9,12,13},{18,19,22,23,26,27,30,31,16,17,..., dimensions={0} | all-to-all | bytes 16384 | tf_op jit(solution)/shard_map/all_to_all | solution.py:302
  79.2 0.0 copy-done.9
  79.2 6.5 %shard_map.108 = (f32[4,128,256]{2,1,0:T(8,128)S(1)}, bf16[4,128,256]{2,1,0:T(8,128)(2,1)S(1)}, f32[4,128,256]{2,1,0:T(8,128)S(1)}) custom-call(s32[1,4]{1,0:T(1,128)S(1)} %copy-done.9, f32[16,128]{1,0:T(8,128)S(1)} %bitcast.27, f32[8,128]{1,0:T(8,128)S(1)} %get-tuple-element.20.coupling, f32[4,256,256]{2,1,0:T(8,128)S(1)} %get-tuple-element.21.first, ...), custom_call_target="tpu_custom_call" | custom-call | flops 1200000000 | bytes 4000000 | tf_op jit(solution)/shard_map/pallas_call | solution.py:20
  85.7 1.9 %collective-permute-start.2 = (bf16[1,4,128,256]{3,2,1,0:T(8,128)(2,1)S(1)}, bf16[1,4,128,256]{3,2,1,0:T(8,128)(2,1)S(1)}, u32[]{:S(2)}, u32[]{:S(2)}) collective-permute-start(bf16[1,4,128,256]{3,2,1,0:T(8,128)(2,1)S(1)} %bitcast.30), channel_id=1, source_target_pairs={{0,16},{1,17},{2,18},{3,19},{4,20},{5,21},{6,22},{7,23},{8,24},{9,... | collective-permute-start | bytes 786440 | tf_op jit(solution)/shard_map/ppermute | solution.py:247
  87.6 1.8 %fusion.1 = bf16[1,4,256,256]{3,2,1,0:T(8,128)(2,1)} fusion(f32[4,128,256]{2,1,0:T(8,128)S(1)} %get-tuple-element.23, f32[4,128,256]{2,1,0:T(8,128)S(1)} %get-tuple-element.24), kind=kOutput, calls=%fused_computation.2 | convolution fusion | flops 403177472 | bytes 1572864 | tf_op jit(solution)/shard_map/bki,bkj->bij/dot_general | solution.py:312
  89.4 12.3 %collective-permute-done.2 = bf16[1,4,128,256]{3,2,1,0:T(8,128)(2,1)S(1)} collective-permute-done((bf16[1,4,128,256]{3,2,1,0:T(8,128)(2,1)S(1)}, bf16[1,4,128,256]{3,2,1,0:T(8,128)(2,1)S(1)}, u32[]{:S(2)}, u32[]{:S(2)}) %collective-permute-start.2) | collective-permute-done | bytes 262176 | tf_op jit(solution)/shard_map/ppermute | solution.py:247
  101.8 0.7 copy.16
  (2 shorter events, 0.1 us)
Async XLA Ops:
  0.6 22.2 %collective-permute-start = (bf16[1,4,256,256]{3,2,1,0:T(8,128)(2,1)}, bf16[1,4,256,256]{3,2,1,0:T(8,128)(2,1)S(1)}, u32[]{:S(2)}, u32[]{:S(2)}) collective-permute-start(bf16[1,4,256,256]{3,2,1,0:T(8,128)(2,1)} %param.10), channel_id=1, source_target_pairs={{0,496},{1,497},{2,498},{3,499},{4,500},{5,501},{6,502},{7,503},{8... | collective-permute-start | bytes 1572872 | tf_op jit(solution)/shard_map/ppermute | solution.py:247
  12.0 1.4 %copy-start = (bf16[1,3,4,256,256]{4,3,2,1,0:T(8,128)(2,1)S(1)}, bf16[1,3,4,256,256]{4,3,2,1,0:T(8,128)(2,1)}, u32[]{:S(2)}) copy-start(bf16[1,3,4,256,256]{4,3,2,1,0:T(8,128)(2,1)} %param.12) | copy-start | bytes 4718596
  13.4 1.4 %copy-start.2 = (bf16[1,3,4,256,256]{4,3,2,1,0:T(8,128)(2,1)S(1)}, bf16[1,3,4,256,256]{4,3,2,1,0:T(8,128)(2,1)}, u32[]{:S(2)}) copy-start(bf16[1,3,4,256,256]{4,3,2,1,0:T(8,128)(2,1)} %param.13) | copy-start | bytes 4718596
  14.8 1.0 %copy-start.4 = (bf16[1,4,256,256]{3,2,1,0:T(8,128)(2,1)S(1)}, bf16[1,4,256,256]{3,2,1,0:T(8,128)(2,1)}, u32[]{:S(2)}) copy-start(bf16[1,4,256,256]{3,2,1,0:T(8,128)(2,1)} %param.9) | copy-start | bytes 1572868
  15.9 0.9 copy-start.5
  16.8 0.7 copy-start.7
  17.4 5.4 %copy-start.6 = (s32[3,4]{1,0:T(4,128)S(1)}, s32[3,4]{1,0:T(4,128)}, u32[]{:S(2)}) copy-start(s32[3,4]{1,0:T(4,128)} %source.3) | copy-start | bytes 148
  17.4 5.4 %copy-start.8 = (s32[3]{0:T(128)S(1)}, s32[3]{0:T(128)}, u32[]{:S(2)}) copy-start(s32[3]{0:T(128)} %active.3) | copy-start | bytes 40
  25.4 38.7 %copy-start.1 = (bf16[1,3,4,256,256]{4,3,2,1,0:T(8,128)(2,1)S(1)}, bf16[1,3,4,256,256]{4,3,2,1,0:T(8,128)(2,1)}, u32[]{:S(2)}) copy-start(bf16[1,3,4,256,256]{4,3,2,1,0:T(8,128)(2,1)} %param.12) | copy-start | bytes 4718596
  25.4 38.7 %copy-start.3 = (bf16[1,3,4,256,256]{4,3,2,1,0:T(8,128)(2,1)S(1)}, bf16[1,3,4,256,256]{4,3,2,1,0:T(8,128)(2,1)}, u32[]{:S(2)}) copy-start(bf16[1,3,4,256,256]{4,3,2,1,0:T(8,128)(2,1)} %param.13) | copy-start | bytes 4718596
  40.7 9.6 %collective-permute-start.1 = (bf16[128,256]{1,0:T(8,128)(2,1)S(1)}, bf16[128,256]{1,0:T(8,128)(2,1)S(1)}, u32[]{:S(2)}, u32[]{:S(2)}) collective-permute-start(bf16[128,256]{1,0:T(8,128)(2,1)S(1)} %shard_map.106), channel_id=1, source_target_pairs={{0,2},{1,3},{2,0},{3,1},{4,6},{5,7},{6,4},{7,5},{8,10},{9,11},{10,... | collective-permute-start | bytes 196616 | tf_op jit(solution)/shard_map/ppermute | solution.py:256
  64.1 15.1 %copy-start.9 = (s32[1,4]{1,0:T(1,128)S(1)}, s32[1,4]{1,0:T(1,128)}, u32[]{:S(2)}) copy-start(s32[1,4]{1,0:T(1,128)} %kept.1) | copy-start | bytes 52
  85.7 16.1 %collective-permute-start.2 = (bf16[1,4,128,256]{3,2,1,0:T(8,128)(2,1)S(1)}, bf16[1,4,128,256]{3,2,1,0:T(8,128)(2,1)S(1)}, u32[]{:S(2)}, u32[]{:S(2)}) collective-permute-start(bf16[1,4,128,256]{3,2,1,0:T(8,128)(2,1)S(1)} %bitcast.30), channel_id=1, source_target_pairs={{0,16},{1,17},{2,18},{3,19},{4,20},{5,21},{6,22},{7,23},{8,24},{9,... | collective-permute-start | bytes 786440 | tf_op jit(solution)/shard_map/ppermute | solution.py:247

commit v7 on v6

--- a/solution.py
+++ b/solution.py
@@ -16,19 +16,19 @@
 HBM = pl.BlockSpec(memory_space=pltpu.HBM)
 
 
-def call(kernel, operands, in_specs, outs, out_specs, scratch=(), flops=0, moved=0):
+def call(kernel, operands, in_specs, outs, out_specs, scratch=(), flops=0, moved=0, vmem=24):
     return pl.pallas_call(
         kernel,
         out_shape=tuple(jax.ShapeDtypeStruct(shape, dtype) for shape, dtype in outs),
         in_specs=in_specs,
         out_specs=tuple(out_specs),
         scratch_shapes=list(scratch),
-        compiler_params=pltpu.CompilerParams(vmem_limit_bytes=24 * 2**20),
+        compiler_params=pltpu.CompilerParams(vmem_limit_bytes=vmem * 2**20),
         cost_estimate=pl.CostEstimate(flops=flops, bytes_accessed=moved, transcendentals=0),
     )(*operands)
 
 
-def prepare_kernel(left_part, inverse, sketch, lenv_hbm, renv_hbm, scaled, tests, lenv, renv, sems):
+def prepare_kernel(left_part, inverse, lenv_hbm, renv_hbm, scaled, lenv, renv, sems):
     copies = []
     for slot in range(lenv.shape[0]):
         rows = pl.ds(slot * 256, 256)
@@ -40,20 +40,26 @@
         copy.start()
     for b in range(left_part.shape[0]):
         scaled[b] = (left_part[b].astype(f32) * inverse[b : b + 1, :]).astype(bf16)
-    tests[...] = sketch[...].T
     for copy in copies:
         copy.wait()
 
 
+def transpose_kernel(array, turned):
+    turned[...] = array[...].T
+
+
 def first_kernel(
-    source, active, scaled, neighbour, lenv, renv,
+    core, source, active, scaled, own_half, other_half, lenv, renv,
     first_hbm, part, ray, first, inner, vector, image, sems,
 ):
     slots, sectors = lenv.shape[:2]
     count = sectors * 256 * 256
     squares = jnp.zeros((1, 256), f32)
-    for b in range(sectors):
-        center = jnp.dot(scaled[b], neighbour[b], preferred_element_type=f32)
+    half = sectors // 2
+    for i in range(sectors):
+        b = (half * core[0] + i) % sectors
+        neighbour = own_half[i] if i < half else other_half[i - half]
+        center = jnp.dot(scaled[b], neighbour, preferred_element_type=f32)
         image[b] = center
         squares += jnp.sum(center * center, axis=0, keepdims=True)
     scale = lax.rsqrt(jnp.sum(squares, axis=1, keepdims=True) / count + 1e-06)
@@ -237,27 +243,24 @@
     return [second + first]
 
 
-def across_seg(array, by, swap):
-    segs, ops = lax.axis_size("seg"), lax.axis_size("op")
-    pairs = []
-    for seg in range(segs):
-        for op in range(ops):
-            other = op ^ 2 if swap and not 0 <= seg + by < segs else op
-            pairs.append((seg * ops + op, (seg + by) % segs * ops + other))
-    return lax.ppermute(array, ("seg", "op"), pairs)
-
-
-def sum_over_op(part):
+def from_seg(array, by):
+    size = lax.axis_size("seg")
+    return lax.ppermute(array, "seg", [(i, (i + by) % size) for i in range(size)])
+
+
+def sum_over_op(part, sketch):
     chunks = part.reshape(8, 128, 256)
     chunks = lax.all_to_all(chunks, "op", 0, 0, axis_index_groups=plane_groups(), tiled=True)
     (own,) = call(
         sum_kernel, (chunks,), [VMEM], [((128, 256), bf16)], [VMEM], flops=1_000_000, moved=600_000
     )
     other = lax.ppermute(own, "op", [(i, i ^ 2) for i in range(16)])
+    (turned,) = call(transpose_kernel, (sketch,), [VMEM], [(sketch.shape[::-1], f32)], [VMEM])
+    own, turned = lax.optimization_barrier((own, turned))
     both = (own.astype(f32) + other.astype(f32)).astype(bf16)
     spread = jnp.broadcast_to(both[None], (8, 128, 256))
     whole = lax.all_to_all(spread, "op", 0, 0, axis_index_groups=plane_groups(), tiled=True)
-    return whole.reshape(4, 256, 256)
+    return whole.reshape(4, 256, 256), turned
 
 
 def shards(
@@ -266,21 +269,27 @@
     lenv, renv = left_env[0], right_env[0]
     slots, sectors = lenv.shape[:2]
     whole, cols = (sectors, 256, 256), sketch.shape[2]
-    neighbour = across_seg(right_part, -1, False)[0]
-    scaled, tests, lenv_near, renv_near = call(
+    core = lax.axis_index("op") % 2
+    half = sectors // 2
+    own_half = lax.dynamic_slice_in_dim(right_part[0], half * core, half, 0)
+    own_half = from_seg(own_half, -1)
+    scaled, lenv_near, renv_near = call(
         prepare_kernel,
-        (left_part[0], inverse_values[0], sketch[0], lenv, renv),
-        [VMEM] * 3 + [HBM] * 2,
-        [(whole, bf16), ((cols, 256), f32), (lenv.shape, bf16), ((sectors, slots * 256, 256), bf16)],
-        [VMEM] * 4,
+        (left_part[0], inverse_values[0], lenv, renv),
+        [VMEM] * 2 + [HBM] * 2,
+        [(whole, bf16), (lenv.shape, bf16), ((sectors, slots * 256, 256), bf16)],
+        [VMEM] * 3,
         [pltpu.SemaphoreType.DMA((slots, 2))],
         moved=8_000_000,
     )
     inner = pltpu.VMEM((sectors, 256, slots * 256), bf16)
+    own_half, scaled = lax.optimization_barrier((own_half, scaled))
+    other_half = lax.ppermute(own_half, "op", [(i, i ^ 1) for i in range(lax.axis_size("op"))])
+    core = core.astype(jnp.int32).reshape(1)
     first, part, ray = call(
         first_kernel,
-        (source, term_active, scaled, neighbour, lenv_near, renv_near),
-        [SMEM, SMEM] + [VMEM] * 4,
+        (core, source, term_active, scaled, own_half, other_half, lenv_near, renv_near),
+        [SMEM] * 3 + [VMEM] * 5,
         [(whole, f32), (whole, bf16), ((8, 128), f32)],
         [HBM, VMEM, VMEM],
         [
@@ -289,7 +298,7 @@
         ],
         flops=940_000_000, moved=6_000_000,
     )
-    resid = sum_over_op(part)
+    resid, tests = sum_over_op(part, sketch[0])
     rays, coupling = call(
         second_kernel,
         (source, term_active, resid, ray, lenv, renv),
@@ -308,9 +317,9 @@
         [VMEM] * 3,
         flops=1_200_000_000, moved=4_000_000,
     )
-    handed = across_seg(right_low[None], 1, True)
+    handed = from_seg(right_low, 1)
     kept_state = jnp.einsum("bki,bkj->bij", image, right, precision=HIGHEST) / 256
-    return (kept_state.astype(bf16)[None], handed)
+    return (kept_state.astype(bf16)[None], handed[None])
 
 
 def solution(mesh):

time: 103 us -> 99.5 us (0.966)
  waiting for transfers between devices: 19 us -> 13 us
  starting transfers between devices: 21.2 us -> 24.8 us
  blocking collectives: 42.4 us -> 41.1 us
    ppermute x2 -> x3, waiting for transfers between devices: 17.3 us -> 11.4 us  [the longest x2 10.3 us: from_seg(): lax.ppermute(array, 'seg', [(i, (i + by) % size) for i in range(size)])]
    ppermute x2 -> x3, starting transfers between devices: 13.3 us -> 16.7 us  [the longest x2 13.3 us: from_seg(): lax.ppermute(array, 'seg', [(i, (i + by) % size) for i in range(size)])]
    all_to_all x1, blocking collectives: 15.3 us -> 14 us  [sum_over_op(): lax.all_to_all(chunks, 'op', 0, 0, axis_index_groups=plane_groups(), tile...]
    unnamed x21 -> x23, local copies, waits for them, and re-layouts: 6.17 us -> 6.29 us
    pallas_call x5 -> x6, Pallas kernels: 11.2 us -> 11.2 us  [call(): pl.pallas_call(kernel, out_shape=tuple((jax.ShapeDtypeStruct(shape, dtype...]
  transfers between devices with their start and end apart: 3 -> 4, of which waited for: 3 -> 3; matrix products, arithmetic and copies ran while one was open for 2% -> 2% of each run, Pallas kernels for 0% -> 0%
where the time goes in v7:
time: 99.5 us; the launch traced here: 99 us
  blocking collectives  41.1 us (41%)
  starting transfers between devices  24.8 us (25%)
  waiting for transfers between devices  13 us (13%)
  Pallas kernels  11.2 us (11%)
  local copies, waits for them, and re-layouts  6.35 us (6%)
  matrix products  1.83 us (2%)
    all_to_all x1, blocking collectives, sum_over_op(): lax.all_to_all(chunks, 'op', 0, 0, axis_index_groups=plane_groups(), tile...  14 us
    all_to_all x1, blocking collectives, sum_over_op(): lax.all_to_all(spread, 'op', 0, 0, axis_index_groups=plane_groups(), tile...  13.7 us
    all_to_all x1, blocking collectives, shards(): lax.all_to_all(rays, 'op', 0, 0, axis_index_groups=upper_half_first(), ti...  13.4 us
    ppermute x2, starting transfers between devices, from_seg(): lax.ppermute(array, 'seg', [(i, (i + by) % size) for i in range(size)])  13.3 us
    pallas_call x6, Pallas kernels, call(): pl.pallas_call(kernel, out_shape=tuple((jax.ShapeDtypeStruct(shape, dtype...  11.2 us
    ppermute x2, waiting for transfers between devices, from_seg(): lax.ppermute(array, 'seg', [(i, (i + by) % size) for i in range(size)])  10.3 us
    ppermute x1, starting transfers between devices, sum_over_op(): other = lax.ppermute(own, 'op', [(i, i ^ 2) for i in range(16)])  8.07 us
    unnamed x23, local copies, waits for them, and re-layouts  6.29 us
  transfers between devices with their start and end apart: 4, of which 3 were waited for; matrix products, arithmetic and copies ran while one was open for 2% of the time, Pallas kernels for 0%

profile of v7, /device:TPU:1, one launch (start us, length us, event | category | flops | bytes accessed | tf_op | source)
XLA Modules:
  0.0 99.0 jit_solution(14425888154855833055)
XLA Ops:
  0.6 0.0 copy-start
  0.7 1.0 %copy-done = bf16[1,4,256,256]{3,2,1,0:T(8,128)(2,1)S(1)} copy-done((bf16[1,4,256,256]{3,2,1,0:T(8,128)(2,1)S(1)}, bf16[1,4,256,256]{3,2,1,0:T(8,128)(2,1)}, u32[]{:S(2)}) %copy-start) | copy-done | bytes 524312
  1.7 11.4 %collective-permute-start = (bf16[2,256,256]{2,1,0:T(8,128)(2,1)S(1)}, bf16[2,256,256]{2,1,0:T(8,128)(2,1)S(1)}, u32[]{:S(2)}, u32[]{:S(2)}) collective-permute-start(bf16[2,256,256]{2,1,0:T(8,128)(2,1)S(1)} %dynamic-slice_bitcast_fusion), channel_id=1, source_target_pairs={{0,496},{16,0},{32,16},{48,32},{64,48},{80,64},{96,80},{112,96},{1... | collective-permute-start | bytes 786440 | tf_op jit(solution)/shard_map/ppermute | solution.py:248
  13.1 0.0 copy-start.1
  13.1 1.4 %copy-done.1 = bf16[1,3,4,256,256]{4,3,2,1,0:T(8,128)(2,1)S(1)} copy-done((bf16[1,3,4,256,256]{4,3,2,1,0:T(8,128)(2,1)S(1)}, bf16[1,3,4,256,256]{4,3,2,1,0:T(8,128)(2,1)}, u32[]{:S(2)}) %copy-start.1) | copy-done | bytes 1572888
  14.5 0.0 copy-start.3
  14.5 1.4 %copy-done.3 = bf16[1,3,4,256,256]{4,3,2,1,0:T(8,128)(2,1)S(1)} copy-done((bf16[1,3,4,256,256]{4,3,2,1,0:T(8,128)(2,1)S(1)}, bf16[1,3,4,256,256]{4,3,2,1,0:T(8,128)(2,1)}, u32[]{:S(2)}) %copy-start.3) | copy-done | bytes 1572888
  15.9 0.0 copy-start.5
  15.9 1.0 %copy-done.5 = bf16[1,4,256,256]{3,2,1,0:T(8,128)(2,1)S(1)} copy-done((bf16[1,4,256,256]{3,2,1,0:T(8,128)(2,1)S(1)}, bf16[1,4,256,256]{3,2,1,0:T(8,128)(2,1)}, u32[]{:S(2)}) %copy-start.5) | copy-done | bytes 524312
  16.9 0.0 copy-start.8
  16.9 0.7 copy-done.8
  17.6 0.0 copy-start.7
  17.6 0.0 copy-start.9
  17.6 0.4 shard_map.104
  18.0 0.0 collective-permute-done.own_half
  18.0 3.4 %collective-permute-start.1 = (bf16[2,256,256]{2,1,0:T(8,128)(2,1)S(1)}, bf16[2,256,256]{2,1,0:T(8,128)(2,1)S(1)}, u32[]{:S(2)}, u32[]{:S(2)}) collective-permute-start(bf16[2,256,256]{2,1,0:T(8,128)(2,1)S(1)} %collective-permute-done.own_half), channel_id=1, source_target_pairs={{0,1},{1,0},{2,3},{3,2},{4,5},{5,4},{6,7},{7,6},{8,9},{9,8},{10,11... | collective-permute-start | bytes 786440 | tf_op jit(solution)/shard_map/ppermute | solution.py:287
  21.5 1.1 %collective-permute-done.1.other_half = bf16[2,256,256]{2,1,0:T(8,128)(2,1)S(1)} collective-permute-done((bf16[2,256,256]{2,1,0:T(8,128)(2,1)S(1)}, bf16[2,256,256]{2,1,0:T(8,128)(2,1)S(1)}, u32[]{:S(2)}, u32[]{:S(2)}) %collective-permute-start.1) | collective-permute-done | bytes 262176 | tf_op jit(solution)/shard_map/ppermute | solution.py:287
  22.6 0.0 copy-done.7
  22.6 0.0 copy-done.9
  22.6 2.5 %shard_map.105 = (f32[4,256,256]{2,1,0:T(8,128)S(1)}, bf16[4,256,256]{2,1,0:T(8,128)(2,1)S(1)}, f32[8,128]{1,0:T(8,128)S(1)}) custom-call(s32[1]{0:T(128)} %bitcast.core, s32[3,4]{1,0:T(4,128)S(1)} %copy-done.7, s32[3]{0:T(128)S(1)} %copy-done.9, bf16[4,256,256]{2,1,0:T(8,128)(2,1)S(1)} %get-tuple-element.18.scaled, ...), custom_call_target="tpu_custom_call" | custom-call | flops 940000000 | bytes 6000000 | tf_op jit(solution)/shard_map/pallas_call | solution.py:20
  25.1 0.0 copy-start.6
  25.1 0.0 copy-start.4
  25.1 14.0 %all_to_all.21.chunks = bf16[8,128,256]{2,1,0:T(8,128)(2,1)S(1)} all-to-all(bf16[8,128,256]{2,1,0:T(8,128)(2,1)S(1)} %bitcast.25), channel_id=1, replica_groups={{0,1,4,5,8,9,12,13},{2,3,6,7,10,11,14,15},{16,17,20,21,24,25,28,29},{18..., dimensions={0} | all-to-all | bytes 1048576 | tf_op jit(solution)/shard_map/all_to_all | solution.py:253
  39.1 0.0 copy-start.2
  39.1 0.1 shard_map.106
  39.1 8.1 %collective-permute-start.2 = (bf16[128,256]{1,0:T(8,128)(2,1)S(1)}, bf16[128,256]{1,0:T(8,128)(2,1)S(1)}, u32[]{:S(2)}, u32[]{:S(2)}) collective-permute-start(bf16[128,256]{1,0:T(8,128)(2,1)S(1)} %shard_map.106), channel_id=1, source_target_pairs={{0,2},{1,3},{2,0},{3,1},{4,6},{5,7},{6,4},{7,5},{8,10},{9,11},{10,... | collective-permute-start | bytes 196616 | tf_op jit(solution)/shard_map/ppermute | solution.py:257
  47.2 0.0 copy-done.6
  47.2 0.1 shard_map.107.sketch
  47.3 1.5 %collective-permute-done.2 = bf16[128,256]{1,0:T(8,128)(2,1)S(1)} collective-permute-done((bf16[128,256]{1,0:T(8,128)(2,1)S(1)}, bf16[128,256]{1,0:T(8,128)(2,1)S(1)}, u32[]{:S(2)}, u32[]{:S(2)}) %collective-permute-start.2) | collective-permute-done | bytes 65568 | tf_op jit(solution)/shard_map/ppermute | solution.py:257
  48.9 13.7 %all_to_all.22 = bf16[8,128,256]{2,1,0:T(8,128)(2,1)S(1)} all-to-all(bf16[8,128,256]{2,1,0:T(8,128)(2,1)S(1)} %broadcast_in_dim.12), channel_id=1, replica_groups={{0,1,4,5,8,9,12,13},{2,3,6,7,10,11,14,15},{16,17,20,21,24,25,28,29},{18..., dimensions={0} | all-to-all | bytes 1048576 | tf_op jit(solution)/shard_map/all_to_all | solution.py:262
  62.6 0.0 copy-done.4
  62.6 0.0 copy-done.2
  62.6 0.0 copy-start.10
  62.6 1.7 %shard_map.108 = (f32[16,128]{1,0:T(8,128)S(1)}, f32[8,128]{1,0:T(8,128)S(1)}) custom-call(s32[3,4]{1,0:T(4,128)S(1)} %copy-done.7, s32[3]{0:T(128)S(1)} %copy-done.9, bf16[4,256,256]{2,1,0:T(8,128)(2,1)S(1)} %bitcast.23, f32[8,128]{1,0:T(8,128)S(1)} %get-tuple-element.24.first_ray, bf16[3,4,256,256]{3,2,1,0:T(8,128)(2,1)S(1)} %bitcast.20, ...), custom_call_target="tpu_custom_call" | custom-call | flops 800000000 | bytes 4000000 | tf_op jit(solution)/shard_map/pallas_call | solution.py:20
  64.3 13.4 %all_to_all.23 = f32[16,1,128]{2,1,0:T(1,128)S(1)} all-to-all(f32[16,1,128]{2,1,0:T(1,128)S(1)} %bitcast.29), channel_id=1, replica_groups={{2,3,6,7,10,11,14,15,0,1,4,5,8,9,12,13},{18,19,22,23,26,27,30,31,16,17,..., dimensions={0} | all-to-all | bytes 16384 | tf_op jit(solution)/shard_map/all_to_all | solution.py:311
  77.7 0.0 copy-done.10
  77.7 6.5 %shard_map.109 = (f32[4,128,256]{2,1,0:T(8,128)S(1)}, bf16[4,128,256]{2,1,0:T(8,128)(2,1)S(1)}, f32[4,128,256]{2,1,0:T(8,128)S(1)}) custom-call(s32[1,4]{1,0:T(1,128)S(1)} %copy-done.10, f32[16,128]{1,0:T(8,128)S(1)} %bitcast.28, f32[8,128]{1,0:T(8,128)S(1)} %get-tuple-element.26.coupling, f32[4,256,256]{2,1,0:T(8,128)S(1)} %get-tuple-element.27.first, ...), custom_call_target="tpu_custom_call" | custom-call | flops 1200000000 | bytes 4000000 | tf_op jit(solution)/shard_map/pallas_call | solution.py:20
  84.2 1.9 %collective-permute-start.3 = (bf16[4,128,256]{2,1,0:T(8,128)(2,1)S(1)}, bf16[4,128,256]{2,1,0:T(8,128)(2,1)S(1)}, u32[]{:S(2)}, u32[]{:S(2)}) collective-permute-start(bf16[4,128,256]{2,1,0:T(8,128)(2,1)S(1)} %get-tuple-element.31), channel_id=1, source_target_pairs={{0,16},{16,32},{32,48},{48,64},{64,80},{80,96},{96,112},{112,128},... | collective-permute-start | bytes 786440 | tf_op jit(solution)/shard_map/ppermute | solution.py:248
  86.2 1.8 %fusion.1 = bf16[1,4,256,256]{3,2,1,0:T(8,128)(2,1)} fusion(f32[4,128,256]{2,1,0:T(8,128)S(1)} %get-tuple-element.29, f32[4,128,256]{2,1,0:T(8,128)S(1)} %get-tuple-element.30), kind=kOutput, calls=%fused_computation.2 | convolution fusion | flops 403177472 | bytes 1572864 | tf_op jit(solution)/shard_map/bki,bkj->bij/dot_general | solution.py:321
  88.0 10.3 %collective-permute-done.3 = bf16[4,128,256]{2,1,0:T(8,128)(2,1)S(1)} collective-permute-done((bf16[4,128,256]{2,1,0:T(8,128)(2,1)S(1)}, bf16[4,128,256]{2,1,0:T(8,128)(2,1)S(1)}, u32[]{:S(2)}, u32[]{:S(2)}) %collective-permute-start.3) | collective-permute-done | bytes 262176 | tf_op jit(solution)/shard_map/ppermute | solution.py:248
  98.3 0.7 copy.16
  (3 shorter events, 0.1 us)
Async XLA Ops:
  0.6 1.0 %copy-start = (bf16[1,4,256,256]{3,2,1,0:T(8,128)(2,1)S(1)}, bf16[1,4,256,256]{3,2,1,0:T(8,128)(2,1)}, u32[]{:S(2)}) copy-start(bf16[1,4,256,256]{3,2,1,0:T(8,128)(2,1)} %param.10) | copy-start | bytes 1572868
  1.7 16.3 %collective-permute-start = (bf16[2,256,256]{2,1,0:T(8,128)(2,1)S(1)}, bf16[2,256,256]{2,1,0:T(8,128)(2,1)S(1)}, u32[]{:S(2)}, u32[]{:S(2)}) collective-permute-start(bf16[2,256,256]{2,1,0:T(8,128)(2,1)S(1)} %dynamic-slice_bitcast_fusion), channel_id=1, source_target_pairs={{0,496},{16,0},{32,16},{48,32},{64,48},{80,64},{96,80},{112,96},{1... | collective-permute-start | bytes 786440 | tf_op jit(solution)/shard_map/ppermute | solution.py:248
  13.1 1.4 %copy-start.1 = (bf16[1,3,4,256,256]{4,3,2,1,0:T(8,128)(2,1)S(1)}, bf16[1,3,4,256,256]{4,3,2,1,0:T(8,128)(2,1)}, u32[]{:S(2)}) copy-start(bf16[1,3,4,256,256]{4,3,2,1,0:T(8,128)(2,1)} %param.12) | copy-start | bytes 4718596
  14.5 1.4 %copy-start.3 = (bf16[1,3,4,256,256]{4,3,2,1,0:T(8,128)(2,1)S(1)}, bf16[1,3,4,256,256]{4,3,2,1,0:T(8,128)(2,1)}, u32[]{:S(2)}) copy-start(bf16[1,3,4,256,256]{4,3,2,1,0:T(8,128)(2,1)} %param.13) | copy-start | bytes 4718596
  15.9 1.0 %copy-start.5 = (bf16[1,4,256,256]{3,2,1,0:T(8,128)(2,1)S(1)}, bf16[1,4,256,256]{3,2,1,0:T(8,128)(2,1)}, u32[]{:S(2)}) copy-start(bf16[1,4,256,256]{3,2,1,0:T(8,128)(2,1)} %param.9) | copy-start | bytes 1572868
  16.9 0.7 copy-start.8
  17.6 5.0 %copy-start.7 = (s32[3,4]{1,0:T(4,128)S(1)}, s32[3,4]{1,0:T(4,128)}, u32[]{:S(2)}) copy-start(s32[3,4]{1,0:T(4,128)} %source.3) | copy-start | bytes 148
  17.6 5.0 %copy-start.9 = (s32[3]{0:T(128)S(1)}, s32[3]{0:T(128)}, u32[]{:S(2)}) copy-start(s32[3]{0:T(128)} %active.3) | copy-start | bytes 40
  18.0 4.6 %collective-permute-start.1 = (bf16[2,256,256]{2,1,0:T(8,128)(2,1)S(1)}, bf16[2,256,256]{2,1,0:T(8,128)(2,1)S(1)}, u32[]{:S(2)}, u32[]{:S(2)}) collective-permute-start(bf16[2,256,256]{2,1,0:T(8,128)(2,1)S(1)} %collective-permute-done.own_half), channel_id=1, source_target_pairs={{0,1},{1,0},{2,3},{3,2},{4,5},{5,4},{6,7},{7,6},{8,9},{9,8},{10,11... | collective-permute-start | bytes 786440 | tf_op jit(solution)/shard_map/ppermute | solution.py:287
  25.1 22.1 %copy-start.6 = (f32[1,256,128]{2,1,0:T(8,128)S(1)}, f32[1,256,128]{2,1,0:T(8,128)}, u32[]{:S(2)}) copy-start(f32[1,256,128]{2,1,0:T(8,128)} %param.16) | copy-start | bytes 393220
  25.1 37.5 %copy-start.4 = (bf16[1,3,4,256,256]{4,3,2,1,0:T(8,128)(2,1)S(1)}, bf16[1,3,4,256,256]{4,3,2,1,0:T(8,128)(2,1)}, u32[]{:S(2)}) copy-start(bf16[1,3,4,256,256]{4,3,2,1,0:T(8,128)(2,1)} %param.13) | copy-start | bytes 4718596
  39.1 23.5 %copy-start.2 = (bf16[1,3,4,256,256]{4,3,2,1,0:T(8,128)(2,1)S(1)}, bf16[1,3,4,256,256]{4,3,2,1,0:T(8,128)(2,1)}, u32[]{:S(2)}) copy-start(bf16[1,3,4,256,256]{4,3,2,1,0:T(8,128)(2,1)} %param.12) | copy-start | bytes 4718596
  39.1 9.7 %collective-permute-start.2 = (bf16[128,256]{1,0:T(8,128)(2,1)S(1)}, bf16[128,256]{1,0:T(8,128)(2,1)S(1)}, u32[]{:S(2)}, u32[]{:S(2)}) collective-permute-start(bf16[128,256]{1,0:T(8,128)(2,1)S(1)} %shard_map.106), channel_id=1, source_target_pairs={{0,2},{1,3},{2,0},{3,1},{4,6},{5,7},{6,4},{7,5},{8,10},{9,11},{10,... | collective-permute-start | bytes 196616 | tf_op jit(solution)/shard_map/ppermute | solution.py:257
  62.6 15.1 %copy-start.10 = (s32[1,4]{1,0:T(1,128)S(1)}, s32[1,4]{1,0:T(1,128)}, u32[]{:S(2)}) copy-start(s32[1,4]{1,0:T(1,128)} %kept.1) | copy-start | bytes 52
  84.2 14.0 %collective-permute-start.3 = (bf16[4,128,256]{2,1,0:T(8,128)(2,1)S(1)}, bf16[4,128,256]{2,1,0:T(8,128)(2,1)S(1)}, u32[]{:S(2)}, u32[]{:S(2)}) collective-permute-start(bf16[4,128,256]{2,1,0:T(8,128)(2,1)S(1)} %get-tuple-element.31), channel_id=1, source_target_pairs={{0,16},{16,32},{32,48},{48,64},{64,80},{80,96},{96,112},{112,128},... | collective-permute-start | bytes 786440 | tf_op jit(solution)/shard_map/ppermute | solution.py:248

commit v8 on v7

--- a/solution.py
+++ b/solution.py
@@ -109,8 +109,7 @@
             inner[b, :, slot * 256 : (slot + 1) * 256] = (product * flag).astype(bf16)
     dots, squares = jnp.zeros((1, 256), f32), jnp.zeros((1, 256), f32)
     for b in range(sectors):
-        below = jnp.concatenate([renv[slot, b] for slot in range(slots)], axis=0)
-        own = jnp.dot(inner[b], below, preferred_element_type=f32)
+        own = jnp.dot(inner[b], renv[b], preferred_element_type=f32)
         piece = resid[b].astype(f32)
         dots += jnp.sum(piece * own, axis=0, keepdims=True)
         squares += jnp.sum(piece * piece, axis=0, keepdims=True)
@@ -137,42 +136,48 @@
 
 
 def invert_blocks(packed):
-    size = packed.shape[0]
-    row = lax.broadcasted_iota(jnp.int32, packed.shape, 0)
-    lane = lax.broadcasted_iota(jnp.int32, packed.shape, 1)
+    size, lanes = packed.shape
+    tiles = range(size // 8)
+    row = lax.broadcasted_iota(jnp.int32, (8, lanes), 0)
+    lane = lax.broadcasted_iota(jnp.int32, (8, lanes), 1)
     place = lane % size
     start = lane - place
-    spot = place[0:1, :]
-
-    def column(array, k):
-        return jnp.take_along_axis(array, start + k, axis=1)
-
-    queue = [(column(packed, k), column(packed, k + 1)) for k in range(0, 2 * AHEAD, 2)]
+    packed = [packed[8 * t : 8 * t + 8] for t in tiles]
+
+    def column(k):
+        return [jnp.take_along_axis(packed[t], start + k, axis=1) for t in tiles]
+
+    def at(array, k):
+        return array[k // 8][k % 8 : k % 8 + 1, :]
+
+    queue = [(column(k), column(k + 1)) for k in range(0, 2 * AHEAD, 2)]
     for k in range(0, size, 2):
         left, right = queue.pop(0)
         if k + 2 * AHEAD < size:
-            queue.append((column(packed, k + 2 * AHEAD), column(packed, k + 2 * AHEAD + 1)))
-        top, cross, low = left[k : k + 1, :], left[k + 1 : k + 2, :], right[k + 1 : k + 2, :]
+            queue.append((column(k + 2 * AHEAD), column(k + 2 * AHEAD + 1)))
+        top, cross, low = at(left, k), at(left, k + 1), at(right, k + 1)
         scale = 1.0 / (top * low - cross * cross)
 
         def eliminate(old, upper, lower):
             upper, lower = low * upper - cross * lower, top * lower - cross * upper
-            new = old - (left * upper + right * lower) * scale
-            return jnp.where(
-                row == k, upper * scale, jnp.where(row == k + 1, lower * scale, new)
-            )
-
-        upper = jnp.where(spot == k, 1.0, jnp.where(spot == k + 1, 0.0, packed[k : k + 1, :]))
-        lower = jnp.where(spot == k, 0.0, jnp.where(spot == k + 1, 1.0, packed[k + 1 : k + 2, :]))
-        rest = jnp.where((place == k) | (place == k + 1), 0.0, packed)
-        packed = eliminate(rest, upper, lower)
+            new = [old[t] - (left[t] * upper + right[t] * lower) * scale for t in tiles]
+            own = jnp.where(row == k % 8, upper * scale, lower * scale)
+            new[k // 8] = jnp.where((row == k % 8) | (row == k % 8 + 1), own, new[k // 8])
+            return new
+
+        first, second = place == k, place == k + 1
+        upper = jnp.where(first[0:1], 1.0, jnp.where(second[0:1], 0.0, at(packed, k)))
+        lower = jnp.where(first[0:1], 0.0, jnp.where(second[0:1], 1.0, at(packed, k + 1)))
+        packed = eliminate(
+            [jnp.where(first | second, 0.0, packed[t]) for t in tiles], upper, lower
+        )
         for i, pair in enumerate(queue):
             j = k + 2 * i + 2
             queue[i] = tuple(
-                eliminate(old, left[n : n + 1, :], right[n : n + 1, :])
+                eliminate(old, at(left, n), at(right, n))
                 for old, n in zip(pair, (j, j + 1), strict=True)
             )
-    return packed
+    return jnp.concatenate(packed, axis=0)
 
 
 def invert(gram):
@@ -235,12 +240,12 @@
 
 
 def plane_groups():
-    return [[x * 4 + z * 2 + c for x in range(4) for c in range(2)] for z in range(2)]
+    return [[x * 4 + z * 2 + c for x in (2, 1, 3, 0) for c in (1, 0)] for z in range(2)]
 
 
 def upper_half_first():
-    first, second = plane_groups()
-    return [second + first]
+    lower, upper = plane_groups()
+    return [upper + lower]
 
 
 def from_seg(array, by):
@@ -301,7 +306,7 @@
     resid, tests = sum_over_op(part, sketch[0])
     rays, coupling = call(
         second_kernel,
-        (source, term_active, resid, ray, lenv, renv),
+        (source, term_active, resid, ray, lenv_near, renv_near),
         [SMEM, SMEM] + [VMEM] * 4,
         [((16, 128), f32), ((8, 128), f32)],
         [VMEM] * 2,

time: 99.5 us -> 95.3 us (0.958)
  blocking collectives: 41.1 us -> 36.5 us
    all_to_all x1, blocking collectives: 14 us -> 12.1 us  [sum_over_op(): lax.all_to_all(chunks, 'op', 0, 0, axis_index_groups=plane_groups(), tile...]
    all_to_all x1, blocking collectives: 13.7 us -> 12 us  [sum_over_op(): lax.all_to_all(spread, 'op', 0, 0, axis_index_groups=plane_groups(), tile...]
    unnamed x23 -> x19, local copies, waits for them, and re-layouts: 6.29 us -> 6.28 us
where the time goes in v8:
time: 95.3 us; the launch traced here: 94.8 us
  blocking collectives  36.5 us (38%)
  starting transfers between devices  24.7 us (26%)
  waiting for transfers between devices  13.5 us (14%)
  Pallas kernels  11.2 us (12%)
  local copies, waits for them, and re-layouts  6.34 us (7%)
  matrix products  1.83 us (2%)
    ppermute x2, starting transfers between devices, from_seg(): lax.ppermute(array, 'seg', [(i, (i + by) % size) for i in range(size)])  13.3 us
    all_to_all x1, blocking collectives, shards(): lax.all_to_all(rays, 'op', 0, 0, axis_index_groups=upper_half_first(), ti...  12.5 us
    all_to_all x1, blocking collectives, sum_over_op(): lax.all_to_all(chunks, 'op', 0, 0, axis_index_groups=plane_groups(), tile...  12.1 us
    all_to_all x1, blocking collectives, sum_over_op(): lax.all_to_all(spread, 'op', 0, 0, axis_index_groups=plane_groups(), tile...  12 us
    pallas_call x6, Pallas kernels, call(): pl.pallas_call(kernel, out_shape=tuple((jax.ShapeDtypeStruct(shape, dtype...  11.2 us
    ppermute x2, waiting for transfers between devices, from_seg(): lax.ppermute(array, 'seg', [(i, (i + by) % size) for i in range(size)])  10.3 us
    ppermute x1, starting transfers between devices, sum_over_op(): other = lax.ppermute(own, 'op', [(i, i ^ 2) for i in range(16)])  7.94 us
    unnamed x19, local copies, waits for them, and re-layouts  6.28 us
  transfers between devices with their start and end apart: 4, of which 3 were waited for; matrix products, arithmetic and copies ran while one was open for 2% of the time, Pallas kernels for 0%

profile of v8, /device:TPU:1, one launch (start us, length us, event | category | flops | bytes accessed | tf_op | source)
XLA Modules:
  0.0 94.8 jit_solution(5695545915011221671)
XLA Ops:
  0.6 0.0 copy-start
  0.7 1.0 %copy-done = bf16[1,4,256,256]{3,2,1,0:T(8,128)(2,1)S(1)} copy-done((bf16[1,4,256,256]{3,2,1,0:T(8,128)(2,1)S(1)}, bf16[1,4,256,256]{3,2,1,0:T(8,128)(2,1)}, u32[]{:S(2)}) %copy-start) | copy-done | bytes 524312
  1.7 11.4 %collective-permute-start = (bf16[2,256,256]{2,1,0:T(8,128)(2,1)S(1)}, bf16[2,256,256]{2,1,0:T(8,128)(2,1)S(1)}, u32[]{:S(2)}, u32[]{:S(2)}) collective-permute-start(bf16[2,256,256]{2,1,0:T(8,128)(2,1)S(1)} %dynamic-slice_bitcast_fusion), channel_id=1, source_target_pairs={{0,496},{16,0},{32,16},{48,32},{64,48},{80,64},{96,80},{112,96},{1... | collective-permute-start | bytes 786440 | tf_op jit(solution)/shard_map/ppermute | solution.py:253
  13.1 0.0 copy-start.1
  13.1 1.4 %copy-done.1 = bf16[1,3,4,256,256]{4,3,2,1,0:T(8,128)(2,1)S(1)} copy-done((bf16[1,3,4,256,256]{4,3,2,1,0:T(8,128)(2,1)S(1)}, bf16[1,3,4,256,256]{4,3,2,1,0:T(8,128)(2,1)}, u32[]{:S(2)}) %copy-start.1) | copy-done | bytes 1572888
  14.5 0.0 copy-start.2
  14.5 1.4 %copy-done.2 = bf16[1,3,4,256,256]{4,3,2,1,0:T(8,128)(2,1)S(1)} copy-done((bf16[1,3,4,256,256]{4,3,2,1,0:T(8,128)(2,1)S(1)}, bf16[1,3,4,256,256]{4,3,2,1,0:T(8,128)(2,1)}, u32[]{:S(2)}) %copy-start.2) | copy-done | bytes 1572888
  15.9 0.0 copy-start.3
  15.9 1.0 %copy-done.3 = bf16[1,4,256,256]{3,2,1,0:T(8,128)(2,1)S(1)} copy-done((bf16[1,4,256,256]{3,2,1,0:T(8,128)(2,1)S(1)}, bf16[1,4,256,256]{3,2,1,0:T(8,128)(2,1)}, u32[]{:S(2)}) %copy-start.3) | copy-done | bytes 524312
  16.9 0.0 copy-start.6
  16.9 0.7 copy-done.6
  17.6 0.0 copy-start.5
  17.6 0.0 copy-start.7
  17.6 0.4 shard_map.104
  18.0 0.0 collective-permute-done.own_half
  18.0 3.4 %collective-permute-start.1 = (bf16[2,256,256]{2,1,0:T(8,128)(2,1)S(1)}, bf16[2,256,256]{2,1,0:T(8,128)(2,1)S(1)}, u32[]{:S(2)}, u32[]{:S(2)}) collective-permute-start(bf16[2,256,256]{2,1,0:T(8,128)(2,1)S(1)} %collective-permute-done.own_half), channel_id=1, source_target_pairs={{0,1},{1,0},{2,3},{3,2},{4,5},{5,4},{6,7},{7,6},{8,9},{9,8},{10,11... | collective-permute-start | bytes 786440 | tf_op jit(solution)/shard_map/ppermute | solution.py:292
  21.5 1.1 %collective-permute-done.1.other_half = bf16[2,256,256]{2,1,0:T(8,128)(2,1)S(1)} collective-permute-done((bf16[2,256,256]{2,1,0:T(8,128)(2,1)S(1)}, bf16[2,256,256]{2,1,0:T(8,128)(2,1)S(1)}, u32[]{:S(2)}, u32[]{:S(2)}) %collective-permute-start.1) | collective-permute-done | bytes 262176 | tf_op jit(solution)/shard_map/ppermute | solution.py:292
  22.6 0.0 copy-done.5
  22.6 0.0 copy-done.7
  22.6 2.5 %shard_map.105 = (f32[4,256,256]{2,1,0:T(8,128)S(1)}, bf16[4,256,256]{2,1,0:T(8,128)(2,1)S(1)}, f32[8,128]{1,0:T(8,128)S(1)}) custom-call(s32[1]{0:T(128)} %bitcast.core, s32[3,4]{1,0:T(4,128)S(1)} %copy-done.5, s32[3]{0:T(128)S(1)} %copy-done.7, bf16[4,256,256]{2,1,0:T(8,128)(2,1)S(1)} %get-tuple-element.18.scaled, ...), custom_call_target="tpu_custom_call" | custom-call | flops 940000000 | bytes 6000000 | tf_op jit(solution)/shard_map/pallas_call | solution.py:20
  25.1 0.0 copy-start.4
  25.1 12.1 %all_to_all.21.chunks = bf16[8,128,256]{2,1,0:T(8,128)(2,1)S(1)} all-to-all(bf16[8,128,256]{2,1,0:T(8,128)(2,1)S(1)} %bitcast.23), channel_id=1, replica_groups={{9,8,5,4,13,12,1,0},{11,10,7,6,15,14,3,2},{25,24,21,20,29,28,17,16},{27..., dimensions={0} | all-to-all | bytes 1048576 | tf_op jit(solution)/shard_map/all_to_all | solution.py:258
  37.2 0.1 shard_map.106
  37.3 7.9 %collective-permute-start.2 = (bf16[128,256]{1,0:T(8,128)(2,1)S(1)}, bf16[128,256]{1,0:T(8,128)(2,1)S(1)}, u32[]{:S(2)}, u32[]{:S(2)}) collective-permute-start(bf16[128,256]{1,0:T(8,128)(2,1)S(1)} %shard_map.106), channel_id=1, source_target_pairs={{0,2},{1,3},{2,0},{3,1},{4,6},{5,7},{6,4},{7,5},{8,10},{9,11},{10,... | collective-permute-start | bytes 196616 | tf_op jit(solution)/shard_map/ppermute | solution.py:262
  45.2 0.0 copy-done.4
  45.2 0.1 shard_map.107.sketch
  45.3 2.1 %collective-permute-done.2 = bf16[128,256]{1,0:T(8,128)(2,1)S(1)} collective-permute-done((bf16[128,256]{1,0:T(8,128)(2,1)S(1)}, bf16[128,256]{1,0:T(8,128)(2,1)S(1)}, u32[]{:S(2)}, u32[]{:S(2)}) %collective-permute-start.2) | collective-permute-done | bytes 65568 | tf_op jit(solution)/shard_map/ppermute | solution.py:262
  47.5 12.0 %all_to_all.22 = bf16[8,128,256]{2,1,0:T(8,128)(2,1)S(1)} all-to-all(bf16[8,128,256]{2,1,0:T(8,128)(2,1)S(1)} %broadcast_in_dim.12), channel_id=1, replica_groups={{9,8,5,4,13,12,1,0},{11,10,7,6,15,14,3,2},{25,24,21,20,29,28,17,16},{27..., dimensions={0} | all-to-all | bytes 1048576 | tf_op jit(solution)/shard_map/all_to_all | solution.py:267
  59.4 0.0 copy-start.8
  59.4 1.7 %shard_map.108 = (f32[16,128]{1,0:T(8,128)S(1)}, f32[8,128]{1,0:T(8,128)S(1)}) custom-call(s32[3,4]{1,0:T(4,128)S(1)} %copy-done.5, s32[3]{0:T(128)S(1)} %copy-done.7, bf16[4,256,256]{2,1,0:T(8,128)(2,1)S(1)} %bitcast.19, f32[8,128]{1,0:T(8,128)S(1)} %get-tuple-element.24.first_ray, bf16[3,4,256,256]{3,2,1,0:T(8,128)(2,1)S(1)} %get-tuple-element.20.lenv, ...), custom_call_target="tpu_custom_call" | custom-call | flops 800000000 | bytes 4000000 | tf_op jit(solution)/shard_map/pallas_call | solution.py:20
  61.1 12.5 %all_to_all.23 = f32[16,1,128]{2,1,0:T(1,128)S(1)} all-to-all(f32[16,1,128]{2,1,0:T(1,128)S(1)} %bitcast.27), channel_id=1, replica_groups={{11,10,7,6,15,14,3,2,9,8,5,4,13,12,1,0},{27,26,23,22,31,30,19,18,25,24,..., dimensions={0} | all-to-all | bytes 16384 | tf_op jit(solution)/shard_map/all_to_all | solution.py:316
  73.6 0.0 copy-done.8
  73.6 6.5 %shard_map.109 = (f32[4,128,256]{2,1,0:T(8,128)S(1)}, bf16[4,128,256]{2,1,0:T(8,128)(2,1)S(1)}, f32[4,128,256]{2,1,0:T(8,128)S(1)}) custom-call(s32[1,4]{1,0:T(1,128)S(1)} %copy-done.8, f32[16,128]{1,0:T(8,128)S(1)} %bitcast.26, f32[8,128]{1,0:T(8,128)S(1)} %get-tuple-element.26.coupling, f32[4,256,256]{2,1,0:T(8,128)S(1)} %get-tuple-element.27.first, ...), custom_call_target="tpu_custom_call" | custom-call | flops 1200000000 | bytes 4000000 | tf_op jit(solution)/shard_map/pallas_call | solution.py:20
  80.1 1.9 %collective-permute-start.3 = (bf16[4,128,256]{2,1,0:T(8,128)(2,1)S(1)}, bf16[4,128,256]{2,1,0:T(8,128)(2,1)S(1)}, u32[]{:S(2)}, u32[]{:S(2)}) collective-permute-start(bf16[4,128,256]{2,1,0:T(8,128)(2,1)S(1)} %get-tuple-element.31), channel_id=1, source_target_pairs={{0,16},{16,32},{32,48},{48,64},{64,80},{80,96},{96,112},{112,128},... | collective-permute-start | bytes 786440 | tf_op jit(solution)/shard_map/ppermute | solution.py:253
  82.0 1.8 %fusion.1 = bf16[1,4,256,256]{3,2,1,0:T(8,128)(2,1)} fusion(f32[4,128,256]{2,1,0:T(8,128)S(1)} %get-tuple-element.29, f32[4,128,256]{2,1,0:T(8,128)S(1)} %get-tuple-element.30), kind=kOutput, calls=%fused_computation.2 | convolution fusion | flops 403177472 | bytes 1572864 | tf_op jit(solution)/shard_map/bki,bkj->bij/dot_general | solution.py:326
  83.8 10.3 %collective-permute-done.3 = bf16[4,128,256]{2,1,0:T(8,128)(2,1)S(1)} collective-permute-done((bf16[4,128,256]{2,1,0:T(8,128)(2,1)S(1)}, bf16[4,128,256]{2,1,0:T(8,128)(2,1)S(1)}, u32[]{:S(2)}, u32[]{:S(2)}) %collective-permute-start.3) | collective-permute-done | bytes 262176 | tf_op jit(solution)/shard_map/ppermute | solution.py:253
  94.1 0.7 copy.16
  (3 shorter events, 0.1 us)
Async XLA Ops:
  0.6 1.0 %copy-start = (bf16[1,4,256,256]{3,2,1,0:T(8,128)(2,1)S(1)}, bf16[1,4,256,256]{3,2,1,0:T(8,128)(2,1)}, u32[]{:S(2)}) copy-start(bf16[1,4,256,256]{3,2,1,0:T(8,128)(2,1)} %param.10) | copy-start | bytes 1572868
  1.7 16.3 %collective-permute-start = (bf16[2,256,256]{2,1,0:T(8,128)(2,1)S(1)}, bf16[2,256,256]{2,1,0:T(8,128)(2,1)S(1)}, u32[]{:S(2)}, u32[]{:S(2)}) collective-permute-start(bf16[2,256,256]{2,1,0:T(8,128)(2,1)S(1)} %dynamic-slice_bitcast_fusion), channel_id=1, source_target_pairs={{0,496},{16,0},{32,16},{48,32},{64,48},{80,64},{96,80},{112,96},{1... | collective-permute-start | bytes 786440 | tf_op jit(solution)/shard_map/ppermute | solution.py:253
  13.1 1.4 %copy-start.1 = (bf16[1,3,4,256,256]{4,3,2,1,0:T(8,128)(2,1)S(1)}, bf16[1,3,4,256,256]{4,3,2,1,0:T(8,128)(2,1)}, u32[]{:S(2)}) copy-start(bf16[1,3,4,256,256]{4,3,2,1,0:T(8,128)(2,1)} %param.12) | copy-start | bytes 4718596
  14.5 1.4 %copy-start.2 = (bf16[1,3,4,256,256]{4,3,2,1,0:T(8,128)(2,1)S(1)}, bf16[1,3,4,256,256]{4,3,2,1,0:T(8,128)(2,1)}, u32[]{:S(2)}) copy-start(bf16[1,3,4,256,256]{4,3,2,1,0:T(8,128)(2,1)} %param.13) | copy-start | bytes 4718596
  15.9 1.0 %copy-start.3 = (bf16[1,4,256,256]{3,2,1,0:T(8,128)(2,1)S(1)}, bf16[1,4,256,256]{3,2,1,0:T(8,128)(2,1)}, u32[]{:S(2)}) copy-start(bf16[1,4,256,256]{3,2,1,0:T(8,128)(2,1)} %param.9) | copy-start | bytes 1572868
  16.9 0.7 copy-start.6
  17.6 5.0 %copy-start.5 = (s32[3,4]{1,0:T(4,128)S(1)}, s32[3,4]{1,0:T(4,128)}, u32[]{:S(2)}) copy-start(s32[3,4]{1,0:T(4,128)} %source.3) | copy-start | bytes 148
  17.6 5.0 %copy-start.7 = (s32[3]{0:T(128)S(1)}, s32[3]{0:T(128)}, u32[]{:S(2)}) copy-start(s32[3]{0:T(128)} %active.3) | copy-start | bytes 40
  18.0 4.6 %collective-permute-start.1 = (bf16[2,256,256]{2,1,0:T(8,128)(2,1)S(1)}, bf16[2,256,256]{2,1,0:T(8,128)(2,1)S(1)}, u32[]{:S(2)}, u32[]{:S(2)}) collective-permute-start(bf16[2,256,256]{2,1,0:T(8,128)(2,1)S(1)} %collective-permute-done.own_half), channel_id=1, source_target_pairs={{0,1},{1,0},{2,3},{3,2},{4,5},{5,4},{6,7},{7,6},{8,9},{9,8},{10,11... | collective-permute-start | bytes 786440 | tf_op jit(solution)/shard_map/ppermute | solution.py:292
  25.1 20.1 %copy-start.4 = (f32[1,256,128]{2,1,0:T(8,128)S(1)}, f32[1,256,128]{2,1,0:T(8,128)}, u32[]{:S(2)}) copy-start(f32[1,256,128]{2,1,0:T(8,128)} %param.16) | copy-start | bytes 393220
  37.3 10.1 %collective-permute-start.2 = (bf16[128,256]{1,0:T(8,128)(2,1)S(1)}, bf16[128,256]{1,0:T(8,128)(2,1)S(1)}, u32[]{:S(2)}, u32[]{:S(2)}) collective-permute-start(bf16[128,256]{1,0:T(8,128)(2,1)S(1)} %shard_map.106), channel_id=1, source_target_pairs={{0,2},{1,3},{2,0},{3,1},{4,6},{5,7},{6,4},{7,5},{8,10},{9,11},{10,... | collective-permute-start | bytes 196616 | tf_op jit(solution)/shard_map/ppermute | solution.py:262
  59.4 14.2 %copy-start.8 = (s32[1,4]{1,0:T(1,128)S(1)}, s32[1,4]{1,0:T(1,128)}, u32[]{:S(2)}) copy-start(s32[1,4]{1,0:T(1,128)} %kept.1) | copy-start | bytes 52
  80.1 14.0 %collective-permute-start.3 = (bf16[4,128,256]{2,1,0:T(8,128)(2,1)S(1)}, bf16[4,128,256]{2,1,0:T(8,128)(2,1)S(1)}, u32[]{:S(2)}, u32[]{:S(2)}) collective-permute-start(bf16[4,128,256]{2,1,0:T(8,128)(2,1)S(1)} %get-tuple-element.31), channel_id=1, source_target_pairs={{0,16},{16,32},{32,48},{48,64},{64,80},{80,96},{96,112},{112,128},... | collective-permute-start | bytes 786440 | tf_op jit(solution)/shard_map/ppermute | solution.py:253

commit v9 on v8

--- a/solution.py
+++ b/solution.py
@@ -48,27 +48,34 @@
     turned[...] = array[...].T
 
 
+def center_kernel(core, scaled, neighbour, center, squares):
+    half = neighbour.shape[0]
+    total = jnp.zeros((1, 256), f32)
+    for i in range(half):
+        own = jnp.dot(scaled[half * core[0] + i], neighbour[i], preferred_element_type=f32)
+        center[i] = own
+        total += jnp.sum(own * own, axis=0, keepdims=True)
+    squares[...] = jnp.broadcast_to(total, squares.shape)
+
+
 def first_kernel(
-    core, source, active, scaled, own_half, other_half, lenv, renv,
-    first_hbm, part, ray, first, inner, vector, image, sems,
+    core, source, active, scaled, own_center, own_squares, other_half, lenv, renv,
+    first, part, ray, inner, vector, image,
 ):
     slots, sectors = lenv.shape[:2]
     count = sectors * 256 * 256
-    squares = jnp.zeros((1, 256), f32)
+    squares = own_squares[0:1, :]
     half = sectors // 2
-    for i in range(sectors):
-        b = (half * core[0] + i) % sectors
-        neighbour = own_half[i] if i < half else other_half[i - half]
-        center = jnp.dot(scaled[b], neighbour, preferred_element_type=f32)
+    for i in range(half):
+        image[half * core[0] + i] = own_center[i]
+        b = half * (1 - core[0]) + i
+        center = jnp.dot(scaled[b], other_half[i], preferred_element_type=f32)
         image[b] = center
         squares += jnp.sum(center * center, axis=0, keepdims=True)
     scale = lax.rsqrt(jnp.sum(squares, axis=1, keepdims=True) / count + 1e-06)
-    out_copies = []
     for b in range(sectors):
         scaled_center = image[b] * scale
         first[b] = scaled_center
-        out_copies.append(pltpu.make_async_copy(first.at[b], first_hbm.at[b], sems.at[b]))
-        out_copies[b].start()
         vector[b] = scaled_center.astype(bf16)
     for slot in range(slots):
         flag = active[slot].astype(f32)
@@ -86,8 +93,6 @@
     for b in range(sectors):
         part[b] = (image[b] - own_ray * first[b]).astype(bf16)
     ray[...] = jnp.broadcast_to(own_ray, ray.shape)
-    for copy in out_copies:
-        copy.wait()
 
 
 def sum_kernel(chunks, total):
@@ -291,16 +296,18 @@
     own_half, scaled = lax.optimization_barrier((own_half, scaled))
     other_half = lax.ppermute(own_half, "op", [(i, i ^ 1) for i in range(lax.axis_size("op"))])
     core = core.astype(jnp.int32).reshape(1)
+    own_center, own_squares = call(
+        center_kernel, (core, scaled, own_half), [SMEM] + [VMEM] * 2,
+        [((half, 256, 256), f32), ((8, 256), f32)], [VMEM] * 2,
+        flops=900_000_000, moved=1_000_000,
+    )
     first, part, ray = call(
         first_kernel,
-        (core, source, term_active, scaled, own_half, other_half, lenv_near, renv_near),
-        [SMEM] * 3 + [VMEM] * 5,
+        (core, source, term_active, scaled, own_center, own_squares, other_half, lenv_near, renv_near),
+        [SMEM] * 3 + [VMEM] * 6,
         [(whole, f32), (whole, bf16), ((8, 128), f32)],
-        [HBM, VMEM, VMEM],
-        [
-            pltpu.VMEM(whole, f32), inner, pltpu.VMEM(whole, bf16), pltpu.VMEM(whole, f32),
-            pltpu.SemaphoreType.DMA((sectors,)),
-        ],
+        [VMEM] * 3,
+        [inner, pltpu.VMEM(whole, bf16), pltpu.VMEM(whole, f32)],
         flops=940_000_000, moved=6_000_000,
     )
     resid, tests = sum_over_op(part, sketch[0])

time: 95.3 us -> 95.2 us (level)
    pallas_call x6 -> x7, Pallas kernels: 11.2 us -> 11.3 us  [call(): pl.pallas_call(kernel, out_shape=tuple((jax.ShapeDtypeStruct(shape, dtype...]
  transfers between devices with their start and end apart: 4 -> 4, of which waited for: 3 -> 3; matrix products, arithmetic and copies ran while one was open for 2% -> 2% of each run, Pallas kernels for 0% -> 1%
where the time goes in v9:
time: 95.2 us; the launch traced here: 94.7 us
  blocking collectives  36.5 us (38%)
  starting transfers between devices  24.7 us (26%)
  waiting for transfers between devices  13.3 us (14%)
  Pallas kernels  11.3 us (12%)
  local copies, waits for them, and re-layouts  6.34 us (7%)
  matrix products  1.83 us (2%)
    ppermute x2, starting transfers between devices, from_seg(): lax.ppermute(array, 'seg', [(i, (i + by) % size) for i in range(size)])  13.3 us
    all_to_all x1, blocking collectives, shards(): lax.all_to_all(rays, 'op', 0, 0, axis_index_groups=upper_half_first(), ti...  12.5 us
    all_to_all x1, blocking collectives, sum_over_op(): lax.all_to_all(chunks, 'op', 0, 0, axis_index_groups=plane_groups(), tile...  12.1 us
    all_to_all x1, blocking collectives, sum_over_op(): lax.all_to_all(spread, 'op', 0, 0, axis_index_groups=plane_groups(), tile...  12 us
    pallas_call x7, Pallas kernels, call(): pl.pallas_call(kernel, out_shape=tuple((jax.ShapeDtypeStruct(shape, dtype...  11.3 us
    ppermute x2, waiting for transfers between devices, from_seg(): lax.ppermute(array, 'seg', [(i, (i + by) % size) for i in range(size)])  10.3 us
    ppermute x1, starting transfers between devices, sum_over_op(): other = lax.ppermute(own, 'op', [(i, i ^ 2) for i in range(16)])  7.94 us
    unnamed x19, local copies, waits for them, and re-layouts  6.29 us
  transfers between devices with their start and end apart: 4, of which 3 were waited for; matrix products, arithmetic and copies ran while one was open for 2% of the time, Pallas kernels for 1%

profile of v9, /device:TPU:1, one launch (start us, length us, event | category | flops | bytes accessed | tf_op | source)
XLA Modules:
  0.0 94.7 jit_solution(1463795295082924914)
XLA Ops:
  0.6 0.0 copy-start
  0.7 1.0 %copy-done = bf16[1,4,256,256]{3,2,1,0:T(8,128)(2,1)S(1)} copy-done((bf16[1,4,256,256]{3,2,1,0:T(8,128)(2,1)S(1)}, bf16[1,4,256,256]{3,2,1,0:T(8,128)(2,1)}, u32[]{:S(2)}) %copy-start) | copy-done | bytes 524312
  1.7 11.4 %collective-permute-start = (bf16[2,256,256]{2,1,0:T(8,128)(2,1)S(1)}, bf16[2,256,256]{2,1,0:T(8,128)(2,1)S(1)}, u32[]{:S(2)}, u32[]{:S(2)}) collective-permute-start(bf16[2,256,256]{2,1,0:T(8,128)(2,1)S(1)} %dynamic-slice_bitcast_fusion), channel_id=1, source_target_pairs={{0,496},{16,0},{32,16},{48,32},{64,48},{80,64},{96,80},{112,96},{1... | collective-permute-start | bytes 786440 | tf_op jit(solution)/shard_map/ppermute | solution.py:258
  13.1 0.0 copy-start.1
  13.1 1.4 %copy-done.1 = bf16[1,3,4,256,256]{4,3,2,1,0:T(8,128)(2,1)S(1)} copy-done((bf16[1,3,4,256,256]{4,3,2,1,0:T(8,128)(2,1)S(1)}, bf16[1,3,4,256,256]{4,3,2,1,0:T(8,128)(2,1)}, u32[]{:S(2)}) %copy-start.1) | copy-done | bytes 1572888
  14.5 0.0 copy-start.2
  14.5 1.4 %copy-done.2 = bf16[1,3,4,256,256]{4,3,2,1,0:T(8,128)(2,1)S(1)} copy-done((bf16[1,3,4,256,256]{4,3,2,1,0:T(8,128)(2,1)S(1)}, bf16[1,3,4,256,256]{4,3,2,1,0:T(8,128)(2,1)}, u32[]{:S(2)}) %copy-start.2) | copy-done | bytes 1572888
  15.9 0.0 copy-start.3
  15.9 1.0 %copy-done.3 = bf16[1,4,256,256]{3,2,1,0:T(8,128)(2,1)S(1)} copy-done((bf16[1,4,256,256]{3,2,1,0:T(8,128)(2,1)S(1)}, bf16[1,4,256,256]{3,2,1,0:T(8,128)(2,1)}, u32[]{:S(2)}) %copy-start.3) | copy-done | bytes 524312
  16.9 0.0 copy-start.6
  16.9 0.7 copy-done.6
  17.6 0.4 shard_map.104
  18.0 0.0 collective-permute-done.neighbour
  18.0 3.4 %collective-permute-start.1 = (bf16[2,256,256]{2,1,0:T(8,128)(2,1)S(1)}, bf16[2,256,256]{2,1,0:T(8,128)(2,1)S(1)}, u32[]{:S(2)}, u32[]{:S(2)}) collective-permute-start(bf16[2,256,256]{2,1,0:T(8,128)(2,1)S(1)} %collective-permute-done.neighbour), channel_id=1, source_target_pairs={{0,1},{1,0},{2,3},{3,2},{4,5},{5,4},{6,7},{7,6},{8,9},{9,8},{10,11... | collective-permute-start | bytes 786440 | tf_op jit(solution)/shard_map/ppermute | solution.py:297
  21.5 0.0 copy-start.5
  21.5 0.0 copy-start.7
  21.5 0.2 shard_map.105
  21.7 0.9 collective-permute-done.1.other_half
  22.6 0.0 copy-done.5
  22.6 0.0 copy-done.7
  22.6 2.3 %shard_map.106 = (f32[4,256,256]{2,1,0:T(8,128)S(1)}, bf16[4,256,256]{2,1,0:T(8,128)(2,1)S(1)}, f32[8,128]{1,0:T(8,128)S(1)}) custom-call(s32[1]{0:T(128)} %bitcast.core, s32[3,4]{1,0:T(4,128)S(1)} %copy-done.5, s32[3]{0:T(128)S(1)} %copy-done.7, bf16[4,256,256]{2,1,0:T(8,128)(2,1)S(1)} %get-tuple-element.20.scaled, ...), custom_call_target="tpu_custom_call" | custom-call | flops 940000000 | bytes 6000000 | tf_op jit(solution)/shard_map/pallas_call | solution.py:20
  24.9 0.0 copy-start.4
  25.0 12.1 %all_to_all.21.chunks = bf16[8,128,256]{2,1,0:T(8,128)(2,1)S(1)} all-to-all(bf16[8,128,256]{2,1,0:T(8,128)(2,1)S(1)} %bitcast.23), channel_id=1, replica_groups={{9,8,5,4,13,12,1,0},{11,10,7,6,15,14,3,2},{25,24,21,20,29,28,17,16},{27..., dimensions={0} | all-to-all | bytes 1048576 | tf_op jit(solution)/shard_map/all_to_all | solution.py:263
  37.0 0.1 shard_map.107
  37.1 7.9 %collective-permute-start.2 = (bf16[128,256]{1,0:T(8,128)(2,1)S(1)}, bf16[128,256]{1,0:T(8,128)(2,1)S(1)}, u32[]{:S(2)}, u32[]{:S(2)}) collective-permute-start(bf16[128,256]{1,0:T(8,128)(2,1)S(1)} %shard_map.107), channel_id=1, source_target_pairs={{0,2},{1,3},{2,0},{3,1},{4,6},{5,7},{6,4},{7,5},{8,10},{9,11},{10,... | collective-permute-start | bytes 196616 | tf_op jit(solution)/shard_map/ppermute | solution.py:267
  45.0 0.0 copy-done.4
  45.1 0.1 shard_map.108.sketch
  45.2 2.1 %collective-permute-done.2 = bf16[128,256]{1,0:T(8,128)(2,1)S(1)} collective-permute-done((bf16[128,256]{1,0:T(8,128)(2,1)S(1)}, bf16[128,256]{1,0:T(8,128)(2,1)S(1)}, u32[]{:S(2)}, u32[]{:S(2)}) %collective-permute-start.2) | collective-permute-done | bytes 65568 | tf_op jit(solution)/shard_map/ppermute | solution.py:267
  47.3 12.0 %all_to_all.22 = bf16[8,128,256]{2,1,0:T(8,128)(2,1)S(1)} all-to-all(bf16[8,128,256]{2,1,0:T(8,128)(2,1)S(1)} %broadcast_in_dim.12), channel_id=1, replica_groups={{9,8,5,4,13,12,1,0},{11,10,7,6,15,14,3,2},{25,24,21,20,29,28,17,16},{27..., dimensions={0} | all-to-all | bytes 1048576 | tf_op jit(solution)/shard_map/all_to_all | solution.py:272
  59.3 0.0 copy-start.8
  59.3 1.7 %shard_map.109 = (f32[16,128]{1,0:T(8,128)S(1)}, f32[8,128]{1,0:T(8,128)S(1)}) custom-call(s32[3,4]{1,0:T(4,128)S(1)} %copy-done.5, s32[3]{0:T(128)S(1)} %copy-done.7, bf16[4,256,256]{2,1,0:T(8,128)(2,1)S(1)} %bitcast.19, f32[8,128]{1,0:T(8,128)S(1)} %get-tuple-element.28.first_ray, bf16[3,4,256,256]{3,2,1,0:T(8,128)(2,1)S(1)} %get-tuple-element.24.lenv, ...), custom_call_target="tpu_custom_call" | custom-call | flops 800000000 | bytes 4000000 | tf_op jit(solution)/shard_map/pallas_call | solution.py:20
  61.0 12.5 %all_to_all.23 = f32[16,1,128]{2,1,0:T(1,128)S(1)} all-to-all(f32[16,1,128]{2,1,0:T(1,128)S(1)} %bitcast.27), channel_id=1, replica_groups={{11,10,7,6,15,14,3,2,9,8,5,4,13,12,1,0},{27,26,23,22,31,30,19,18,25,24,..., dimensions={0} | all-to-all | bytes 16384 | tf_op jit(solution)/shard_map/all_to_all | solution.py:323
  73.4 0.0 copy-done.8
  73.4 6.5 %shard_map.110 = (f32[4,128,256]{2,1,0:T(8,128)S(1)}, bf16[4,128,256]{2,1,0:T(8,128)(2,1)S(1)}, f32[4,128,256]{2,1,0:T(8,128)S(1)}) custom-call(s32[1,4]{1,0:T(1,128)S(1)} %copy-done.8, f32[16,128]{1,0:T(8,128)S(1)} %bitcast.26, f32[8,128]{1,0:T(8,128)S(1)} %get-tuple-element.30.coupling, f32[4,256,256]{2,1,0:T(8,128)S(1)} %get-tuple-element.31.first, ...), custom_call_target="tpu_custom_call" | custom-call | flops 1200000000 | bytes 4000000 | tf_op jit(solution)/shard_map/pallas_call | solution.py:20
  79.9 1.9 %collective-permute-start.3 = (bf16[4,128,256]{2,1,0:T(8,128)(2,1)S(1)}, bf16[4,128,256]{2,1,0:T(8,128)(2,1)S(1)}, u32[]{:S(2)}, u32[]{:S(2)}) collective-permute-start(bf16[4,128,256]{2,1,0:T(8,128)(2,1)S(1)} %get-tuple-element.35), channel_id=1, source_target_pairs={{0,16},{16,32},{32,48},{48,64},{64,80},{80,96},{96,112},{112,128},... | collective-permute-start | bytes 786440 | tf_op jit(solution)/shard_map/ppermute | solution.py:258
  81.9 1.8 %fusion.1 = bf16[1,4,256,256]{3,2,1,0:T(8,128)(2,1)} fusion(f32[4,128,256]{2,1,0:T(8,128)S(1)} %get-tuple-element.33, f32[4,128,256]{2,1,0:T(8,128)S(1)} %get-tuple-element.34), kind=kOutput, calls=%fused_computation.2 | convolution fusion | flops 403177472 | bytes 1572864 | tf_op jit(solution)/shard_map/bki,bkj->bij/dot_general | solution.py:333
  83.7 10.3 %collective-permute-done.3 = bf16[4,128,256]{2,1,0:T(8,128)(2,1)S(1)} collective-permute-done((bf16[4,128,256]{2,1,0:T(8,128)(2,1)S(1)}, bf16[4,128,256]{2,1,0:T(8,128)(2,1)S(1)}, u32[]{:S(2)}, u32[]{:S(2)}) %collective-permute-start.3) | collective-permute-done | bytes 262176 | tf_op jit(solution)/shard_map/ppermute | solution.py:258
  94.0 0.7 copy.16
  (3 shorter events, 0.1 us)
Async XLA Ops:
  0.6 1.0 %copy-start = (bf16[1,4,256,256]{3,2,1,0:T(8,128)(2,1)S(1)}, bf16[1,4,256,256]{3,2,1,0:T(8,128)(2,1)}, u32[]{:S(2)}) copy-start(bf16[1,4,256,256]{3,2,1,0:T(8,128)(2,1)} %param.10) | copy-start | bytes 1572868
  1.7 16.3 %collective-permute-start = (bf16[2,256,256]{2,1,0:T(8,128)(2,1)S(1)}, bf16[2,256,256]{2,1,0:T(8,128)(2,1)S(1)}, u32[]{:S(2)}, u32[]{:S(2)}) collective-permute-start(bf16[2,256,256]{2,1,0:T(8,128)(2,1)S(1)} %dynamic-slice_bitcast_fusion), channel_id=1, source_target_pairs={{0,496},{16,0},{32,16},{48,32},{64,48},{80,64},{96,80},{112,96},{1... | collective-permute-start | bytes 786440 | tf_op jit(solution)/shard_map/ppermute | solution.py:258
  13.1 1.4 %copy-start.1 = (bf16[1,3,4,256,256]{4,3,2,1,0:T(8,128)(2,1)S(1)}, bf16[1,3,4,256,256]{4,3,2,1,0:T(8,128)(2,1)}, u32[]{:S(2)}) copy-start(bf16[1,3,4,256,256]{4,3,2,1,0:T(8,128)(2,1)} %param.12) | copy-start | bytes 4718596
  14.5 1.4 %copy-start.2 = (bf16[1,3,4,256,256]{4,3,2,1,0:T(8,128)(2,1)S(1)}, bf16[1,3,4,256,256]{4,3,2,1,0:T(8,128)(2,1)}, u32[]{:S(2)}) copy-start(bf16[1,3,4,256,256]{4,3,2,1,0:T(8,128)(2,1)} %param.13) | copy-start | bytes 4718596
  15.9 1.0 %copy-start.3 = (bf16[1,4,256,256]{3,2,1,0:T(8,128)(2,1)S(1)}, bf16[1,4,256,256]{3,2,1,0:T(8,128)(2,1)}, u32[]{:S(2)}) copy-start(bf16[1,4,256,256]{3,2,1,0:T(8,128)(2,1)} %param.9) | copy-start | bytes 1572868
  16.9 0.7 copy-start.6
  18.0 4.6 %collective-permute-start.1 = (bf16[2,256,256]{2,1,0:T(8,128)(2,1)S(1)}, bf16[2,256,256]{2,1,0:T(8,128)(2,1)S(1)}, u32[]{:S(2)}, u32[]{:S(2)}) collective-permute-start(bf16[2,256,256]{2,1,0:T(8,128)(2,1)S(1)} %collective-permute-done.neighbour), channel_id=1, source_target_pairs={{0,1},{1,0},{2,3},{3,2},{4,5},{5,4},{6,7},{7,6},{8,9},{9,8},{10,11... | collective-permute-start | bytes 786440 | tf_op jit(solution)/shard_map/ppermute | solution.py:297
  21.5 1.1 %copy-start.5 = (s32[3,4]{1,0:T(4,128)S(1)}, s32[3,4]{1,0:T(4,128)}, u32[]{:S(2)}) copy-start(s32[3,4]{1,0:T(4,128)} %source.3) | copy-start | bytes 148
  21.5 1.1 %copy-start.7 = (s32[3]{0:T(128)S(1)}, s32[3]{0:T(128)}, u32[]{:S(2)}) copy-start(s32[3]{0:T(128)} %active.3) | copy-start | bytes 40
  24.9 20.1 %copy-start.4 = (f32[1,256,128]{2,1,0:T(8,128)S(1)}, f32[1,256,128]{2,1,0:T(8,128)}, u32[]{:S(2)}) copy-start(f32[1,256,128]{2,1,0:T(8,128)} %param.16) | copy-start | bytes 393220
  37.1 10.1 %collective-permute-start.2 = (bf16[128,256]{1,0:T(8,128)(2,1)S(1)}, bf16[128,256]{1,0:T(8,128)(2,1)S(1)}, u32[]{:S(2)}, u32[]{:S(2)}) collective-permute-start(bf16[128,256]{1,0:T(8,128)(2,1)S(1)} %shard_map.107), channel_id=1, source_target_pairs={{0,2},{1,3},{2,0},{3,1},{4,6},{5,7},{6,4},{7,5},{8,10},{9,11},{10,... | collective-permute-start | bytes 196616 | tf_op jit(solution)/shard_map/ppermute | solution.py:267
  59.3 14.2 %copy-start.8 = (s32[1,4]{1,0:T(1,128)S(1)}, s32[1,4]{1,0:T(1,128)}, u32[]{:S(2)}) copy-start(s32[1,4]{1,0:T(1,128)} %kept.1) | copy-start | bytes 52
  79.9 14.0 %collective-permute-start.3 = (bf16[4,128,256]{2,1,0:T(8,128)(2,1)S(1)}, bf16[4,128,256]{2,1,0:T(8,128)(2,1)S(1)}, u32[]{:S(2)}, u32[]{:S(2)}) collective-permute-start(bf16[4,128,256]{2,1,0:T(8,128)(2,1)S(1)} %get-tuple-element.35), channel_id=1, source_target_pairs={{0,16},{16,32},{32,48},{48,64},{64,80},{80,96},{96,112},{112,128},... | collective-permute-start | bytes 786440 | tf_op jit(solution)/shard_map/ppermute | solution.py:258
